TPU v7x, 256 devices: a whole 4x4x8 slice. The times are simulated.
256 devices in a mesh: row: 8 (over x, y_lo), col: 32 (over y_hi, z, core).
Axes of the slice: x: 4, y: 4 (y_hi: 2, y_lo: 2; y = y_hi * 2 + y_lo), z: 8, core: 2. Of those that a mesh axis runs over, the one named last changes fastest.
Arguments:
- amplitudes: bfloat16 [4096, 65536], P('row', 'col'), may hold values from -6 to 6, as said below
- integrals: bfloat16 [65536, 6144], P('col', 'row'), may hold values from -0.0234375 to 0.0234375
- cd_irreps: int32 [512], P('col'), may hold values from 0 to 7
- ab_irreps: int32 [48], P('row'), may hold values from 0 to 7
- slab_amplitudes: bfloat16 [4096, 6144], P('col', 'row'), may hold values from -6 to 6, as said below
- occ_fock: float32 [64, 64], replicated, may hold values from -0.75 to 0.75
Outputs:
- update: float32 [4096, 6144], P('col', 'row')
Inputs may be any that keep to these rules, and one draw needn't show every extreme that they name: Antisymmetric in the occupied pair: amplitudes[i * 64 + j, c] = -amplitudes[j * 64 + i, c] exactly. Antisymmetric in the occupied pair: slab_amplitudes[i * 64 + j, b] = -slab_amplitudes[j * 64 + i, b] exactly.
All inputs are finite; a program needn't handle non-finite values.
Results may differ from a plain program's by a relative error of at most 0.0003.
Values may be sent and summed in bfloat16 or wider, within the bound.
No kernel may reach another device: no remote copies, remote signals or barrier semaphores. Data moves between devices by JAX's collectives and lax.ppermute only.
A program may use at most 192 MiB of HBM per device.

v0:
```python
import jax
import jax.numpy as jnp
from jax import lax
from jax.sharding import PartitionSpec as P


def masked_tiles(integrals, cd_irreps, ab_irreps):
    row_tiles = cd_irreps.shape[0]
    col_tiles = ab_irreps.shape[0]
    tile_size = integrals.shape[0] // row_tiles
    matching = (cd_irreps[:, None] == ab_irreps[None, :]).astype(jnp.bfloat16)
    tiled_view = (
        integrals.reshape(row_tiles, tile_size, col_tiles, tile_size) * matching[:, None, :, None]
    )
    return tiled_view.reshape(integrals.shape)


def per_device(amplitudes, integrals, cd_irreps, ab_irreps, slab_amplitudes, occ_fock):
    orbitals = occ_fock.shape[0]
    columns = lax.axis_size("col")
    block_len = orbitals // columns
    panel_tiles = masked_tiles(integrals, cd_irreps, ab_irreps)
    slab_cols = panel_tiles.shape[1]
    gathered = lax.all_gather(amplitudes, "row", axis=0, tiled=True)
    slab_wide = slab_amplitudes.astype(jnp.float32).reshape(block_len, orbitals, slab_cols)
    fock_term = jnp.einsum("ilb,lj->ijb", slab_wide, occ_fock, precision=lax.Precision.HIGHEST)
    ladder = lax.psum_scatter(
        jnp.dot(gathered, panel_tiles, preferred_element_type=jnp.float32),
        "col",
        scatter_dimension=0,
        tiled=True,
    )
    combined = ladder.reshape(block_len, orbitals, slab_cols) + fock_term
    received = lax.all_to_all(combined, "col", split_axis=1, concat_axis=0, tiled=True)
    update = combined - jnp.swapaxes(received, 0, 1)
    return update.reshape(block_len * orbitals, slab_cols)


def solution(mesh):
    return jax.shard_map(
        per_device,
        mesh=mesh,
        in_specs=(P("row", "col"), P("col", "row"), P("col"), P("row"), P("col", "row"), P()),
        out_specs=P("col", "row"),
        check_vma=False,
    )
```

profile of v0, /device:TPU:6, one launch (start us, length us, event | category | flops | bytes accessed | tf_op | source)
XLA Modules:
  0.0 570.6 jit_solution(13701560204973155724)
XLA Ops:
  6.5 0.0 copy-start
  6.5 0.0 all-gather.2.cloned.1.call-start
  6.5 0.7 all-gather.2.cloned.1.call-update
  7.3 0.0 copy-start.2
  7.3 0.0 copy-start.3
  7.3 0.0 reduce-scatter.2.cloned.1.call-start
  7.3 3.2 copy.14
  10.5 0.0 copy-done.2
  10.5 0.0 copy-done.3
  10.5 0.1 compare_convert_fusion
  10.6 329.7 %all-gather.2.cloned.1.call-done = bf16[4096,2048]{1,0:T(8,128)(2,1)} async-done(((bf16[512,2048]{1,0:T(8,128)(2,1)}), bf16[4096,2048]{1,0:T(8,128)(2,1)}) %all-gather.2.cloned.1.call-update) | async-done | bytes 16777232 | tf_op jit(solution)/shard_map/all_gather | solution.py:24
  340.3 2.1 mul.11
  342.4 20.4 %convolution_bitcast_fusion = f32[4096,768]{0,1:T(8,128)} fusion(bf16[4096,2048]{1,0:T(8,128)(2,1)} %all-gather.2.cloned.1.call-done, bf16[2048,768]{0,1:T(8,128)(2,1)S(1)} %copy.14, bf16[96,8,16,128]{3,2,1,0:T(8,128)(2,1)} %bitcast.30), kind=kOutput, calls=%fused_computation | convolution fusion | flops 12886474752 | bytes 35651584 | tf_op jit(solution)/shard_map/dot_general | solution.py:28
  362.8 0.0 copy-start.1
  362.8 0.0 reduce-scatter.2.cloned.1.call-update
  362.8 174.4 %reduce-scatter.2.cloned.1.call-done = f32[128,768]{0,1:T(8,128)} async-done(((f32[4096,768]{0,1:T(8,128)}), f32[128,768]{0,1:T(8,128)}) %reduce-scatter.2.cloned.1.call-update) | async-done | bytes 393232 | tf_op jit(solution)/shard_map/reduce_scatter | solution.py:27
  537.2 1.2 copy.15
  538.4 0.0 copy-done
  538.4 0.0 copy-done.1
  538.4 0.4 fusion.1
  538.8 0.3 copy.17
  539.1 23.6 %all_to_all.18 = f32[2,64,768]{2,0,1:T(2,128)S(1)} all-to-all(f32[2,64,768]{2,0,1:T(2,128)S(1)} %copy.17), channel_id=1, replica_groups=mesh['row'=8,'col'=32] {'col'}, dimensions={1} | all-to-all | bytes 786432 | tf_op jit(solution)/shard_map/all_to_all | solution.py:34
  562.7 0.3 all_to_all.16
  563.0 0.8 bitcast_subtract_fusion
  (1 shorter events, 0.0 us)
Async XLA Ops:
  6.5 531.9 %copy-start = (bf16[128,768]{1,0:T(8,128)(2,1)S(1)}, bf16[128,768]{1,0:T(8,128)(2,1)}, u32[]{:S(2)}) copy-start(bf16[128,768]{1,0:T(8,128)(2,1)} %param.10) | copy-start | bytes 589828
  6.5 333.8 %all-gather.2.cloned.1.call-start = ((), (), s32[]{:S(2)}) async-start(), calls=%async_computation.2 | async-start | bytes 18874368 | tf_op jit(solution)/shard_map/all_gather | solution.py:24
  7.3 3.3 copy-start.2
  7.3 3.3 copy-start.3
  7.3 529.9 %reduce-scatter.2.cloned.1.call-start = ((), (), s32[]{:S(2)}) async-start(), calls=%async_computation.3 | async-start | bytes 12976128 | tf_op jit(solution)/shard_map/reduce_scatter | solution.py:27
  362.8 175.6 %copy-start.1 = (f32[64,64]{1,0:T(8,128)S(1)}, f32[64,64]{1,0:T(8,128)}, u32[]{:S(2)}) copy-start(f32[64,64]{1,0:T(8,128)} %param.11) | copy-start | bytes 49156
Sparse Core Ops, SparseCore 0:
  9.1 331.1 all-gather.1
  362.9 174.2 reduce-scatter.1
where the time goes:
time: 571 us
  waiting for transfers between devices  505 us (88%)
  blocking collectives  23.6 us (4%)
  matrix products  20.7 us (4%)
  between operations  13.5 us (2%)
  local copies, waits for them, and re-layouts  7.1 us (1%)
    all_gather x1, waiting for transfers between devices, per_device(): gathered = lax.all_gather(amplitudes, 'row', axis=0, tiled=True)  330 us
    reduce_scatter x1, waiting for transfers between devices, per_device(): lax.psum_scatter(jnp.dot(gathered, panel_tiles, preferred_element_type=jn...  174 us
    all_to_all x1, blocking collectives, per_device(): lax.all_to_all(combined, 'col', split_axis=1, concat_axis=0, tiled=True)  23.6 us
    dot_general x1, matrix products, per_device(): jnp.dot(gathered, panel_tiles, preferred_element_type=jnp.float32)  20.4 us
  transfers between devices with their start and end apart: 2, of which 2 were waited for; matrix products, arithmetic and copies ran while one was open for 1% of the time, Pallas kernels for 0%

commit v1 on v0

v1 whole, which is shorter than its diff:
```python
import jax
import jax.numpy as jnp
from jax import lax
from jax.sharding import PartitionSpec as P

X, LO, HI, Z, CORES = 4, 2, 2, 8, 2
COLS = HI * Z * CORES
SCALE = 64.0


def x_shift(step):
    return [(2 * x + l, 2 * ((x + step) % X) + l) for x in range(X) for l in range(LO)]


Y_SWAP = [(r, r ^ 1) for r in range(X * LO)]
CORE_SWAP = [(c, c ^ 1) for c in range(COLS)]
H_SWAP = [(c, c ^ 16) for c in range(COLS)]
Z_GROUPS = [[16 * h + 2 * z + k for z in range(Z)] for h in range(HI) for k in range(CORES)]
HZ_GROUPS = [[2 * hz + k for hz in range(HI * Z)] for k in range(CORES)]


def partner_of(i, t):
    group, half, i16, i8 = i // 16, (i // 8) % 2, i % 16, i % 8
    following = 16 * ((group + 1) % 4) + (i16 + t) % 16
    opposite = 16 * ((group + 2) % 4) + 8 * (half ^ (group // 2)) + (i8 + t) % 8
    same = 16 * group + (i16 + t - 23) % 16
    return jnp.where(t < 16, following, jnp.where(t < 24, opposite, same))


def grid(rows, columns):
    return (
        lax.broadcasted_iota(jnp.int32, (rows, columns), 0),
        lax.broadcasted_iota(jnp.int32, (rows, columns), 1),
    )


def masked_tiles(integrals, cd_irreps, ab_irreps):
    row_tiles = cd_irreps.shape[0]
    col_tiles = ab_irreps.shape[0]
    tile_size = integrals.shape[0] // row_tiles
    matching = (cd_irreps[:, None] == ab_irreps[None, :]).astype(jnp.bfloat16)
    tiled_view = (
        integrals.reshape(row_tiles, tile_size, col_tiles, tile_size) * matching[:, None, :, None]
    )
    return tiled_view.reshape(integrals.shape)


def own_pairs(amplitudes, r):
    to, held = grid(256, 512)
    wanted = (to % 8) * 64 + partner_of(8 * r + to % 8, to // 8)
    pick = (wanted == held).astype(jnp.bfloat16)
    return jnp.dot(pick, amplitudes, preferred_element_type=jnp.float32).astype(jnp.bfloat16)


def core_sum(partial, k):
    n = partial.shape[1]
    blocks = partial.reshape(-1, HI * Z, CORES, 8, n)
    mine = lax.dynamic_index_in_dim(blocks, k, 2, keepdims=False)
    theirs = lax.dynamic_index_in_dim(blocks, 1 - k, 2, keepdims=False)
    return jnp.swapaxes(mine + lax.ppermute(theirs, "col", CORE_SWAP), 0, 1)


def per_device(amplitudes, integrals, cd_irreps, ab_irreps, slab_amplitudes, occ_fock):
    r, c = lax.axis_index("row"), lax.axis_index("col")
    x, l = r // 2, r % 2
    h, k = c // 16, c % 2
    n = integrals.shape[1]

    own = own_pairs(amplitudes, r)
    partner = lax.ppermute(own, "row", Y_SWAP)
    left = lax.ppermute(own, "row", x_shift(1))
    right = lax.ppermute(own, "row", x_shift(-1))

    slab, own = lax.optimization_barrier((slab_amplitudes, own))
    slab = slab.astype(jnp.float32).reshape(2, 64, n)
    fock = jnp.einsum("elb,lj->ejb", slab, occ_fock, precision=lax.Precision.HIGHEST)
    mirrored = lax.all_to_all(fock, "col", split_axis=1, concat_axis=0, tiled=True)
    fock_update = (fock - jnp.swapaxes(mirrored, 0, 1)).reshape(128, n)
    panel = masked_tiles(integrals, cd_irreps, ab_irreps)
    partner, left, right, fock_update = lax.optimization_barrier((partner, left, right, fock_update))

    from_left = lax.ppermute(jnp.concatenate([left[:128], partner[128:]]), "row", x_shift(1))
    from_right = lax.ppermute(jnp.concatenate([right[128:], partner[:128]]), "row", x_shift(-1))
    across = lax.ppermute(jnp.concatenate([left[:128], right[128:]]), "row", Y_SWAP)

    first = jnp.dot(
        jnp.concatenate([own, partner, left, right]), panel, preferred_element_type=jnp.float32
    )
    first = core_sum(first, k).reshape(HI, Z, -1, n).swapaxes(0, 1).reshape(-1, n)
    _, from_left, from_right, across = lax.optimization_barrier(
        (first, from_left, from_right, across)
    )
    left_partner = jnp.concatenate([across[:128], from_left[128:]])
    right_partner = jnp.concatenate([from_right[128:], across[128:]])
    far = jnp.concatenate([from_left[:128], from_right[:128]])
    first = lax.psum_scatter(
        first, "col", scatter_dimension=0, axis_index_groups=Z_GROUPS, tiled=True
    ).reshape(HI, -1, n)

    far_partner = jnp.concatenate(
        [
            lax.ppermute(left_partner[:96], "row", x_shift(1)),
            lax.ppermute(right_partner[96:192], "row", x_shift(-1)),
            lax.ppermute(far[192:], "row", Y_SWAP),
        ]
    )
    second = jnp.dot(
        jnp.concatenate([far, left_partner, right_partner, far_partner]),
        panel,
        preferred_element_type=jnp.float32,
    )
    second = (core_sum(second, k) * SCALE).astype(jnp.float16).reshape(HI * Z, -1, n)
    second = lax.all_to_all(
        second, "col", split_axis=0, concat_axis=0, axis_index_groups=HZ_GROUPS, tiled=True
    )
    second = second.astype(jnp.float32).sum(0) * (1 / SCALE)
    first, second = lax.optimization_barrier((first, second))

    kept = lax.dynamic_index_in_dim(first, h, 0, keepdims=False)
    other = lax.dynamic_index_in_dim(first, 1 - h, 0, keepdims=False)
    first = kept + lax.ppermute(other, "col", H_SWAP)
    summed = jnp.concatenate([first, second])

    to, at = grid(128, 64)
    source = at // 8
    dx = jnp.array([0, 0, 3, 1, 2, 3, 1, 2])
    dl = jnp.array([0, 1, 0, 0, 0, 1, 1, 1])
    i = 16 * ((x + dx[source]) % 4) + 8 * (l ^ dl[source]) + at % 8
    wanted = 2 * (to // 4) + to % 2
    held = jnp.where(to % 4 < 2, i, partner_of(i, c))
    spread = (wanted == held).astype(jnp.float32)
    sent = jnp.dot(spread, summed, precision=lax.Precision.HIGHEST)
    got = lax.all_to_all(sent, "col", split_axis=0, concat_axis=0, tiled=True)

    ej, at = grid(128, 128)
    i, j = 2 * c + ej // 64, ej % 64
    t, mine = at // 4, at % 2 == ej // 64
    weight = jnp.where(t == 31, 1.0, 2.0)
    forward = jnp.where(mine & (at % 4 < 2) & (partner_of(i, t) == j), weight, 0.0)
    backward = jnp.where(mine & (at % 4 >= 2) & (partner_of(j, t) == i), weight, 0.0)
    return fock_update + jnp.dot(forward - backward, got, precision=lax.Precision.HIGHEST)


def solution(mesh):
    return jax.shard_map(
        per_device,
        mesh=mesh,
        in_specs=(P("row", "col"), P("col", "row"), P("col"), P("row"), P("col", "row"), P()),
        out_specs=P("col", "row"),
        check_vma=False,
    )
```

time: 571 us -> 211 us (0.37)
  waiting for transfers between devices: 505 us -> 106 us
  starting transfers between devices: 0.04 us -> 35.1 us
  blocking collectives: 23.6 us -> 0 us
  local copies, waits for them, and re-layouts: 7.1 us -> 29.9 us
  other arithmetic: 0.86 us -> 12.7 us
  matrix products: 20.7 us -> 11.5 us
    all_gather x1 -> x0, waiting for transfers between devices: 330 us -> none  [per_device(): gathered = lax.all_gather(amplitudes, 'row', axis=0, tiled=True)]
    reduce_scatter x1, waiting for transfers between devices: 174 us -> 6.64 us  [per_device(): lax.psum_scatter(first, 'col', scatter_dimension=0, axis_index_groups=Z_G...]
    all_to_all x0 -> x3, waiting for transfers between devices: none -> 60.9 us  [the longest x1 31 us: per_device(): lax.all_to_all(second, 'col', split_axis=0, concat_axis=0, axis_index_gro...]
    ppermute x0 -> x12, waiting for transfers between devices: none -> 38.7 us  [the longest x1 20 us: per_device(): lax.ppermute(jnp.concatenate([left[:128], partner[128:]]), 'row', x_shift...]
    all_to_all x0 -> x3, starting transfers between devices: none -> 23.9 us  [the longest x1 11.3 us: per_device(): lax.all_to_all(fock, 'col', split_axis=1, concat_axis=0, tiled=True)]
    all_to_all x1 -> x0, blocking collectives: 23.6 us -> none  [per_device(): lax.all_to_all(combined, 'col', split_axis=1, concat_axis=0, tiled=True)]
    ppermute x0 -> x12, starting transfers between devices: none -> 11.2 us  [the longest x1 3.04 us: per_device(): first = kept + lax.ppermute(other, 'col', H_SWAP)]
    unnamed x9 -> x31, local copies, waits for them, and re-layouts: 3.21 us -> 13.7 us
  transfers between devices with their start and end apart: 2 -> 16, of which waited for: 2 -> 10; matrix products, arithmetic and copies ran while one was open for 1% -> 10% of each run, Pallas kernels for 0% -> 0%
where the time goes in v1:
time: 211 us; the launch traced here: 209 us
  waiting for transfers between devices  106 us (50%)
  starting transfers between devices  35.1 us (17%)
  local copies, waits for them, and re-layouts  29.9 us (14%)
  between operations  13.9 us (7%)
  other arithmetic  12.7 us (6%)
  matrix products  11.5 us (5%)
    all_to_all x1, waiting for transfers between devices, per_device(): lax.all_to_all(second, 'col', split_axis=0, concat_axis=0, axis_index_gro...  31 us
    ppermute x1, waiting for transfers between devices, per_device(): lax.ppermute(jnp.concatenate([left[:128], partner[128:]]), 'row', x_shift...  20 us
    all_to_all x1, waiting for transfers between devices, per_device(): got = lax.all_to_all(sent, 'col', split_axis=0, concat_axis=0, tiled=True)  17.3 us
    unnamed x31, local copies, waits for them, and re-layouts  13.7 us
    all_to_all x1, waiting for transfers between devices, per_device(): lax.all_to_all(fock, 'col', split_axis=1, concat_axis=0, tiled=True)  12.5 us
    all_to_all x1, starting transfers between devices, per_device(): lax.all_to_all(fock, 'col', split_axis=1, concat_axis=0, tiled=True)  11.3 us
    all_to_all x1, starting transfers between devices, per_device(): got = lax.all_to_all(sent, 'col', split_axis=0, concat_axis=0, tiled=True)  6.99 us
    ppermute x1, waiting for transfers between devices, per_device(): lax.ppermute(left_partner[:96], 'row', x_shift(1))  6.93 us
  transfers between devices with their start and end apart: 16, of which 10 were waited for; matrix products, arithmetic and copies ran while one was open for 10% of the time, Pallas kernels for 0%

profile of v1, /device:TPU:6, one launch (start us, length us, event | category | flops | bytes accessed | tf_op | source)
XLA Modules:
  0.0 209.4 jit_solution(17521766182592540002)
XLA Ops:
  6.6 1.6 copy-done
  8.1 2.5 %convolution_convert_fusion = bf16[256,2048]{1,0:T(8,128)(2,1)} fusion(bf16[512,2048]{1,0:T(8,128)(2,1)S(1)} %copy-done, s32[]{:T(128)S(6)} %mul.96, s32[256]{0:T(256)S(1)} %get-tuple-element.44, s32[256]{0:T(256)S(1)} %get-tuple-element.47, s32[256]{0:T(256)S(1)} %get-tuple-element.45, s32[256]{0:T(256)S(1)} %get-tuple-element.46, ...), kind=kOutput, calls=%fused_computation.3 | convolution fusion | flops 555483136 | bytes 3150340 | tf_op jit(solution)/shard_map/dot_general | solution.py:52
  10.7 1.6 collective-permute-start
  12.2 0.6 collective-permute-start.1
  12.9 1.4 collective-permute-start.2
  14.3 0.4 convolution_bitcast_fusion
  14.7 1.1 copy.26
  15.7 11.3 %all-to-all-start = ((f32[2,64,768]{2,0,1:T(2,128)}), f32[2,64,768]{2,0,1:T(2,128)}, u32[]{:S(2)}, u32[]{:S(2)}) async-start(f32[2,64,768]{2,0,1:T(2,128)} %copy.26), calls=%async_computation | async-start | bytes 786432 | tf_op jit(solution)/shard_map/all_to_all | solution.py:77
  27.0 0.0 reduce-scatter.2.cloned.1.call-start
  27.1 4.7 %copy.28 = bf16[2048,768]{0,1:T(8,128)(2,1)} copy(bf16[2048,768]{1,0:T(8,128)(2,1)} %param.9) | data formatting | bytes 6291456 | tf_op args[1]
  31.8 0.1 compare_convert_fusion
  31.9 12.5 %all-to-all-done = f32[2,64,768]{2,0,1:T(2,128)} async-done(((f32[2,64,768]{2,0,1:T(2,128)}), f32[2,64,768]{2,0,1:T(2,128)}, u32[]{:S(2)}, u32[]{:S(2)}) %all-to-all-start) | async-done | bytes 393248 | tf_op jit(solution)/shard_map/all_to_all | solution.py:77
  44.4 1.8 copy.46
  46.2 2.0 all_to_all.27
  48.2 1.8 bitcast_subtract_fusion
  50.0 2.1 %pad_maximum_fusion = bf16[1024,2048]{1,0:T(8,128)(2,1)S(1)} fusion(bf16[256,2048]{1,0:T(8,128)(2,1)} %collective-permute-done.2, bf16[256,2048]{1,0:T(8,128)(2,1)} %collective-permute-done.1, bf16[256,2048]{1,0:T(8,128)(2,1)S(1)} %collective-permute-done, bf16[256,2048]{1,0:T(8,128)(2,1)} %convolution_convert_fusion), kind=kLoop, calls=%fused_computation | loop fusion | flops 16777216 | bytes 8388608 | tf_op jit(solution)/shard_map/concatenate | solution.py:87
  52.1 0.5 mul.117
  52.6 2.5 %copy-done.1 = bf16[2048,768]{0,1:T(8,128)(2,1)S(1)} copy-done((bf16[2048,768]{0,1:T(8,128)(2,1)S(1)}, bf16[2048,768]{0,1:T(8,128)(2,1)}, u32[]{:S(2)}) %copy-start.1) | copy-done | bytes 3145752
  55.1 3.5 %fusion.67 = f32[4,16,2,8,768]{4,3,2,1,0:T(8,128)S(1)} fusion(bf16[4,16,2,8,2048]{4,3,2,1,0:T(8,128)(2,1)S(1)} %bitcast.97, bf16[2048,768]{0,1:T(8,128)(2,1)S(1)} %copy-done.1, bf16[96,8,16,128]{3,2,1,0:T(8,128)(2,1)S(1)} %bitcast.98), kind=kOutput, calls=%fused_computation.114 | convolution fusion | flops 3222798336 | bytes 13631488 | tf_op jit(solution)/shard_map/dot_general | solution.py:86
  58.6 1.4 dynamic-slice_bitcast_fusion.1
  60.0 1.2 slice.43
  61.3 1.1 slice.45
  62.3 0.1 fusion.412
  62.5 1.7 pad_maximum_fusion.1
  64.2 1.7 collective-permute-start.4
  65.9 0.3 collective-permute-start.5
  66.2 0.1 collective-permute-start.6
  66.4 2.1 fusion.3
  68.4 0.1 copy.30
  68.6 1.3 copy.31
  69.9 20.0 %collective-permute-done.4 = bf16[256,2048]{1,0:T(8,128)(2,1)} collective-permute-done((bf16[256,2048]{1,0:T(8,128)(2,1)}, bf16[256,2048]{1,0:T(8,128)(2,1)}, u32[]{:S(2)}, u32[]{:S(2)}) %collective-permute-start.4) | collective-permute-done | bytes 1048608 | tf_op jit(solution)/shard_map/ppermute | solution.py:82
  89.9 2.6 %collective-permute-done.5 = bf16[256,2048]{1,0:T(8,128)(2,1)} collective-permute-done((bf16[256,2048]{1,0:T(8,128)(2,1)}, bf16[256,2048]{1,0:T(8,128)(2,1)}, u32[]{:S(2)}, u32[]{:S(2)}) %collective-permute-start.5) | collective-permute-done | bytes 1048608 | tf_op jit(solution)/shard_map/ppermute | solution.py:83
  92.6 1.1 slice_dynamic-update-slice_fusion.3
  93.7 1.1 slice_dynamic-update-slice_fusion.2
  94.8 1.1 slice_dynamic-update-slice_fusion
  95.9 1.3 fusion.410
  97.2 0.1 fusion.411
  97.3 1.7 collective-permute-start.7
  99.0 0.5 collective-permute-start.8
  99.5 1.0 slice.55
  100.5 0.2 collective-permute-start.9
  100.7 6.9 %collective-permute-done.7 = bf16[96,2048]{1,0:T(8,128)(2,1)S(1)} collective-permute-done((bf16[96,2048]{1,0:T(8,128)(2,1)S(1)}, bf16[96,2048]{1,0:T(8,128)(2,1)S(1)}, u32[]{:S(2)}, u32[]{:S(2)}) %collective-permute-start.7) | collective-permute-done | bytes 393248 | tf_op jit(solution)/shard_map/ppermute | solution.py:102
  107.6 2.3 %collective-permute-done.8 = bf16[96,2048]{1,0:T(8,128)(2,1)S(1)} collective-permute-done((bf16[96,2048]{1,0:T(8,128)(2,1)S(1)}, bf16[96,2048]{1,0:T(8,128)(2,1)S(1)}, u32[]{:S(2)}, u32[]{:S(2)}) %collective-permute-start.8) | collective-permute-done | bytes 393248 | tf_op jit(solution)/shard_map/ppermute | solution.py:103
  110.1 3.5 %fusion.65 = f32[4,16,2,8,768]{4,3,2,1,0:T(8,128)S(1)} fusion(bf16[4,16,2,8,2048]{4,3,2,1,0:T(8,128)(2,1)S(1)} %bitcast.105, bf16[2048,768]{0,1:T(8,128)(2,1)S(1)} %copy-done.2, bf16[96,8,16,128]{3,2,1,0:T(8,128)(2,1)S(1)} %bitcast.99), kind=kOutput, calls=%fused_computation.113 | convolution fusion | flops 3222798336 | bytes 13631488 | tf_op jit(solution)/shard_map/dot_general | solution.py:107
  113.5 1.6 copy-done.6
  115.2 1.3 dynamic-slice_bitcast_fusion
  116.5 0.0 reduce-scatter.2.cloned.1.call-update
  116.5 3.7 %collective-permute-done.10 = f32[4,16,8,768]{3,2,1,0:T(8,128)} collective-permute-done((f32[4,16,8,768]{3,2,1,0:T(8,128)}, f32[4,16,8,768]{3,2,1,0:T(8,128)}, u32[]{:S(2)}, u32[]{:S(2)}) %collective-permute-start.10) | collective-permute-done | bytes 1572896 | tf_op jit(solution)/shard_map/ppermute | solution.py:60
  120.2 3.0 %copy_bitcast_fusion = f16[16,32,768]{2,1,0:T(8,128)(2,1)} fusion(f32[4,16,8,768]{3,2,1,0:T(8,128)} %collective-permute-done.10, f32[4,16,2,8,768]{4,3,2,1,0:T(8,128)} %copy-done.6, s32[]{:T(128)S(6)} %select_n.437), kind=kLoop, calls=%fused_computation.21 | loop fusion | flops 1179648 | bytes 3932164 | tf_op jit(solution)/shard_map/reshape | solution.py:112
  123.3 5.6 %all-to-all-start.1 = ((f16[16,32,768]{2,1,0:T(8,128)(2,1)}), f16[16,32,768]{2,1,0:T(8,128)(2,1)S(1)}, u32[]{:S(2)}, u32[]{:S(2)}) async-start(f16[16,32,768]{2,1,0:T(8,128)(2,1)} %copy_bitcast_fusion), calls=%async_computation.2 | async-start | bytes 1572864 | tf_op jit(solution)/shard_map/all_to_all | solution.py:113
  129.0 31.0 %all-to-all-done.1 = f16[16,32,768]{2,1,0:T(8,128)(2,1)S(1)} async-done(((f16[16,32,768]{2,1,0:T(8,128)(2,1)}), f16[16,32,768]{2,1,0:T(8,128)(2,1)S(1)}, u32[]{:S(2)}, u32[]{:S(2)}) %all-to-all-start.1) | async-done | bytes 786464 | tf_op jit(solution)/shard_map/all_to_all | solution.py:113
  160.0 0.1 convert_reduce_fusion
  160.1 6.6 %reduce-scatter.2.cloned.1.call-done = f32[64,768]{1,0:T(8,128)} async-done(((f32[512,768]{1,0:T(8,128)}), f32[64,768]{1,0:T(8,128)}) %reduce-scatter.2.cloned.1.call-update) | async-done | bytes 196624 | tf_op jit(solution)/shard_map/reduce_scatter | solution.py:96
  166.8 0.9 dynamic-slice_bitcast_fusion.2
  167.7 3.0 %collective-permute-start.11 = (f32[32,768]{1,0:T(8,128)S(1)}, f32[32,768]{1,0:T(8,128)S(1)}, u32[]{:S(2)}, u32[]{:S(2)}) collective-permute-start(f32[32,768]{1,0:T(8,128)S(1)} %dynamic-slice_bitcast_fusion.2), channel_id=1, source_target_pairs={{0,16},{1,17},{2,18},{3,19},{4,20},{5,21},{6,22},{7,23},{8,24},{9,... | collective-permute-start | bytes 294920 | tf_op jit(solution)/shard_map/ppermute | solution.py:121
  170.7 3.1 %collective-permute-done.11 = f32[32,768]{1,0:T(8,128)S(1)} collective-permute-done((f32[32,768]{1,0:T(8,128)S(1)}, f32[32,768]{1,0:T(8,128)S(1)}, u32[]{:S(2)}, u32[]{:S(2)}) %collective-permute-start.11) | collective-permute-done | bytes 98336 | tf_op jit(solution)/shard_map/ppermute | solution.py:121
  173.8 0.9 bitcast_add_fusion.2
  174.7 0.5 fusion.89
  175.2 0.9 all_to_all.29
  176.1 7.0 %all-to-all-start.2 = ((f32[32,4,768]{2,1,0:T(4,128)}), f32[32,4,768]{2,1,0:T(4,128)S(1)}, u32[]{:S(2)}, u32[]{:S(2)}) async-start(f32[32,4,768]{2,1,0:T(4,128)} %all_to_all.29), calls=%async_computation.3 | async-start | bytes 786432 | tf_op jit(solution)/shard_map/all_to_all | solution.py:133
  183.1 17.3 %all-to-all-done.2 = f32[32,4,768]{2,1,0:T(4,128)S(1)} async-done(((f32[32,4,768]{2,1,0:T(4,128)}), f32[32,4,768]{2,1,0:T(4,128)S(1)}, u32[]{:S(2)}, u32[]{:S(2)}) %all-to-all-start.2) | async-done | bytes 393248 | tf_op jit(solution)/shard_map/all_to_all | solution.py:133
  200.5 0.1 all_to_all.31
  200.6 1.2 fusion.105
  201.8 0.8 add.497
  (50 shorter events, 0.3 us)
Async XLA Ops:
  6.5 1.6 copy-start
  8.1 6.1 %copy-start.8 = (bf16[128,768]{1,0:T(8,128)(2,1)S(1)}, bf16[128,768]{1,0:T(8,128)(2,1)}, u32[]{:S(2)}) copy-start(bf16[128,768]{1,0:T(8,128)(2,1)} %param.12) | copy-start | bytes 589828
  8.1 6.1 %copy-start.9 = (f32[64,64]{1,0:T(8,128)S(1)}, f32[64,64]{1,0:T(8,128)}, u32[]{:S(2)}) copy-start(f32[64,64]{1,0:T(8,128)} %param.13) | copy-start | bytes 49156
  10.7 39.3 %collective-permute-start = (bf16[256,2048]{1,0:T(8,128)(2,1)}, bf16[256,2048]{1,0:T(8,128)(2,1)S(1)}, u32[]{:S(2)}, u32[]{:S(2)}) collective-permute-start(bf16[256,2048]{1,0:T(8,128)(2,1)} %convolution_convert_fusion), channel_id=1, source_target_pairs={{0,32},{32,0},{64,96},{96,64},{128,160},{160,128},{192,224},{224,1... | collective-permute-start | bytes 3145736 | tf_op jit(solution)/shard_map/ppermute | solution.py:70
  12.2 37.8 %collective-permute-start.1 = (bf16[256,2048]{1,0:T(8,128)(2,1)}, bf16[256,2048]{1,0:T(8,128)(2,1)}, u32[]{:S(2)}, u32[]{:S(2)}) collective-permute-start(bf16[256,2048]{1,0:T(8,128)(2,1)} %convolution_convert_fusion), channel_id=1, source_target_pairs={{0,64},{32,96},{64,128},{96,160},{128,192},{160,224},{192,0},{224,... | collective-permute-start | bytes 3145736 | tf_op jit(solution)/shard_map/ppermute | solution.py:71
  12.9 37.1 %collective-permute-start.2 = (bf16[256,2048]{1,0:T(8,128)(2,1)}, bf16[256,2048]{1,0:T(8,128)(2,1)}, u32[]{:S(2)}, u32[]{:S(2)}) collective-permute-start(bf16[256,2048]{1,0:T(8,128)(2,1)} %convolution_convert_fusion), channel_id=1, source_target_pairs={{0,192},{32,224},{64,0},{96,32},{128,64},{160,96},{192,128},{224,1... | collective-permute-start | bytes 3145736 | tf_op jit(solution)/shard_map/ppermute | solution.py:72
  15.7 28.7 %all-to-all-start = ((f32[2,64,768]{2,0,1:T(2,128)}), f32[2,64,768]{2,0,1:T(2,128)}, u32[]{:S(2)}, u32[]{:S(2)}) async-start(f32[2,64,768]{2,0,1:T(2,128)} %copy.26), calls=%async_computation | async-start | bytes 786432 | tf_op jit(solution)/shard_map/all_to_all | solution.py:77
  27.0 139.7 %reduce-scatter.2.cloned.1.call-start = ((), (), s32[]{:S(2)}) async-start(), calls=%async_computation.4 | async-start | bytes 1769472 | tf_op jit(solution)/shard_map/reduce_scatter | solution.py:96
  27.1 4.7 %copy-start.10 = (s32[16]{0:T(128)S(1)}, s32[16]{0:T(128)}, u32[]{:S(2)}) copy-start(s32[16]{0:T(128)} %param.10) | copy-start | bytes 196
  27.1 4.7 %copy-start.11 = (s32[6]{0:T(128)S(1)}, s32[6]{0:T(128)}, u32[]{:S(2)}) copy-start(s32[6]{0:T(128)} %param.11) | copy-start | bytes 76
  52.1 3.0 %copy-start.1 = (bf16[2048,768]{0,1:T(8,128)(2,1)S(1)}, bf16[2048,768]{0,1:T(8,128)(2,1)}, u32[]{:S(2)}) copy-start(bf16[2048,768]{0,1:T(8,128)(2,1)} %copy.28) | copy-start | bytes 9437188
  52.6 6.0 %copy-start.4 = (bf16[16,128,6,128]{1,0,3,2:T(8,128)(2,1)}, bf16[16,128,6,128]{1,0,3,2:T(8,128)(2,1)S(1)}, u32[]{:S(2)}) copy-start(bf16[16,128,6,128]{1,0,3,2:T(8,128)(2,1)S(1)} %mul.117) | copy-start | bytes 9437188
  58.6 3.9 %copy-start.3 = (f32[4,16,2,8,768]{4,3,2,1,0:T(8,128)}, f32[4,16,2,8,768]{4,3,2,1,0:T(8,128)S(1)}, u32[]{:S(2)}) copy-start(f32[4,16,2,8,768]{4,3,2,1,0:T(8,128)S(1)} %fusion.67) | copy-start | bytes 9437188
  60.0 6.3 %collective-permute-start.3 = (f32[4,16,8,768]{3,2,1,0:T(8,128)}, f32[4,16,8,768]{3,2,1,0:T(8,128)}, u32[]{:S(2)}, u32[]{:S(2)}) collective-permute-start(f32[4,16,8,768]{3,2,1,0:T(8,128)} %dynamic-slice_bitcast_fusion.1), channel_id=1, source_target_pairs={{0,1},{1,0},{2,3},{3,2},{4,5},{5,4},{6,7},{7,6},{8,9},{9,8},{10,11... | collective-permute-start | bytes 4718600 | tf_op jit(solution)/shard_map/ppermute | solution.py:60
  64.2 25.8 %collective-permute-start.4 = (bf16[256,2048]{1,0:T(8,128)(2,1)}, bf16[256,2048]{1,0:T(8,128)(2,1)}, u32[]{:S(2)}, u32[]{:S(2)}) collective-permute-start(bf16[256,2048]{1,0:T(8,128)(2,1)} %get-tuple-element.35), channel_id=1, source_target_pairs={{0,64},{32,96},{64,128},{96,160},{128,192},{160,224},{192,0},{224,... | collective-permute-start | bytes 3145736 | tf_op jit(solution)/shard_map/ppermute | solution.py:82
  65.9 26.7 %collective-permute-start.5 = (bf16[256,2048]{1,0:T(8,128)(2,1)}, bf16[256,2048]{1,0:T(8,128)(2,1)}, u32[]{:S(2)}, u32[]{:S(2)}) collective-permute-start(bf16[256,2048]{1,0:T(8,128)(2,1)} %get-tuple-element.34), channel_id=1, source_target_pairs={{0,192},{32,224},{64,0},{96,32},{128,64},{160,96},{192,128},{224,1... | collective-permute-start | bytes 3145736 | tf_op jit(solution)/shard_map/ppermute | solution.py:83
  66.2 26.3 %collective-permute-start.6 = (bf16[256,2048]{1,0:T(8,128)(2,1)}, bf16[256,2048]{1,0:T(8,128)(2,1)S(1)}, u32[]{:S(2)}, u32[]{:S(2)}) collective-permute-start(bf16[256,2048]{1,0:T(8,128)(2,1)} %get-tuple-element.33), channel_id=1, source_target_pairs={{0,32},{32,0},{64,96},{96,64},{128,160},{160,128},{192,224},{224,1... | collective-permute-start | bytes 3145736 | tf_op jit(solution)/shard_map/ppermute | solution.py:84
  95.9 14.2 %copy-start.5 = (bf16[16,128,6,128]{1,0,3,2:T(8,128)(2,1)S(1)}, bf16[16,128,6,128]{1,0,3,2:T(8,128)(2,1)}, u32[]{:S(2)}) copy-start(bf16[16,128,6,128]{1,0,3,2:T(8,128)(2,1)} %copy-done.4) | copy-start | bytes 9437188
  97.2 12.9 %copy-start.2 = (bf16[2048,768]{0,1:T(8,128)(2,1)S(1)}, bf16[2048,768]{0,1:T(8,128)(2,1)}, u32[]{:S(2)}) copy-start(bf16[2048,768]{0,1:T(8,128)(2,1)} %copy.28) | copy-start | bytes 9437188
  97.3 10.3 %collective-permute-start.7 = (bf16[96,2048]{1,0:T(8,128)(2,1)S(1)}, bf16[96,2048]{1,0:T(8,128)(2,1)S(1)}, u32[]{:S(2)}, u32[]{:S(2)}) collective-permute-start(bf16[96,2048]{1,0:T(8,128)(2,1)S(1)} %slice.53), channel_id=1, source_target_pairs={{0,64},{32,96},{64,128},{96,160},{128,192},{160,224},{192,0},{224,... | collective-permute-start | bytes 1179656 | tf_op jit(solution)/shard_map/ppermute | solution.py:102
  99.0 10.9 %collective-permute-start.8 = (bf16[96,2048]{1,0:T(8,128)(2,1)S(1)}, bf16[96,2048]{1,0:T(8,128)(2,1)S(1)}, u32[]{:S(2)}, u32[]{:S(2)}) collective-permute-start(bf16[96,2048]{1,0:T(8,128)(2,1)S(1)} %pad_maximum_fusion.4), channel_id=1, source_target_pairs={{0,192},{32,224},{64,0},{96,32},{128,64},{160,96},{192,128},{224,1... | collective-permute-start | bytes 1179656 | tf_op jit(solution)/shard_map/ppermute | solution.py:103
  100.5 9.5 %collective-permute-start.9 = (bf16[64,2048]{1,0:T(8,128)(2,1)S(1)}, bf16[64,2048]{1,0:T(8,128)(2,1)S(1)}, u32[]{:S(2)}, u32[]{:S(2)}) collective-permute-start(bf16[64,2048]{1,0:T(8,128)(2,1)S(1)} %slice.55), channel_id=1, source_target_pairs={{0,32},{32,0},{64,96},{96,64},{128,160},{160,128},{192,224},{224,1... | collective-permute-start | bytes 786440 | tf_op jit(solution)/shard_map/ppermute | solution.py:104
  113.5 1.6 copy-start.6
  116.5 3.8 %collective-permute-start.10 = (f32[4,16,8,768]{3,2,1,0:T(8,128)}, f32[4,16,8,768]{3,2,1,0:T(8,128)}, u32[]{:S(2)}, u32[]{:S(2)}) collective-permute-start(f32[4,16,8,768]{3,2,1,0:T(8,128)} %dynamic-slice_bitcast_fusion), channel_id=1, source_target_pairs={{0,1},{1,0},{2,3},{3,2},{4,5},{5,4},{6,7},{7,6},{8,9},{9,8},{10,11... | collective-permute-start | bytes 4718600 | tf_op jit(solution)/shard_map/ppermute | solution.py:60
  123.3 36.7 %all-to-all-start.1 = ((f16[16,32,768]{2,1,0:T(8,128)(2,1)}), f16[16,32,768]{2,1,0:T(8,128)(2,1)S(1)}, u32[]{:S(2)}, u32[]{:S(2)}) async-start(f16[16,32,768]{2,1,0:T(8,128)(2,1)} %copy_bitcast_fusion), calls=%async_computation.2 | async-start | bytes 1572864 | tf_op jit(solution)/shard_map/all_to_all | solution.py:113
  167.7 6.1 %collective-permute-start.11 = (f32[32,768]{1,0:T(8,128)S(1)}, f32[32,768]{1,0:T(8,128)S(1)}, u32[]{:S(2)}, u32[]{:S(2)}) collective-permute-start(f32[32,768]{1,0:T(8,128)S(1)} %dynamic-slice_bitcast_fusion.2), channel_id=1, source_target_pairs={{0,16},{1,17},{2,18},{3,19},{4,20},{5,21},{6,22},{7,23},{8,24},{9,... | collective-permute-start | bytes 294920 | tf_op jit(solution)/shard_map/ppermute | solution.py:121
  176.1 24.4 %all-to-all-start.2 = ((f32[32,4,768]{2,1,0:T(4,128)}), f32[32,4,768]{2,1,0:T(4,128)S(1)}, u32[]{:S(2)}, u32[]{:S(2)}) async-start(f32[32,4,768]{2,1,0:T(4,128)} %all_to_all.29), calls=%async_computation.3 | async-start | bytes 786432 | tf_op jit(solution)/shard_map/all_to_all | solution.py:133
  183.1 18.7 %copy-start.7 = (f32[2,64,768]{2,1,0:T(8,128)S(1)}, f32[2,64,768]{2,1,0:T(8,128)}, u32[]{:S(2)}) copy-start(f32[2,64,768]{2,1,0:T(8,128)} %bitcast_subtract_fusion) | copy-start | bytes 1179652
Sparse Core Ops, SparseCore 0:
  116.6 50.0 reduce-scatter.1

commit v2 on v1

v2 whole, which is shorter than its diff:
```python
import jax
import jax.numpy as jnp
from jax import lax
from jax.experimental import pallas as pl
from jax.experimental.pallas import tpu as pltpu
from jax.sharding import PartitionSpec as P

X, LO, HI, Z, CORES = 4, 2, 2, 8, 2
COLS = HI * Z * CORES
SCALE = 64.0


def x_shift(step):
    return [(2 * x + l, 2 * ((x + step) % X) + l) for x in range(X) for l in range(LO)]


Y_SWAP = [(r, r ^ 1) for r in range(X * LO)]
CORE_SWAP = [(c, c ^ 1) for c in range(COLS)]
HZ_GROUPS = [[2 * hz + k for hz in range(HI * Z)] for k in range(CORES)]


def partner_of(i, t):
    group, half, i16, i8 = i // 16, (i // 8) % 2, i % 16, i % 8
    following = 16 * ((group + 1) % 4) + (i16 + t) % 16
    opposite = 16 * ((group + 2) % 4) + 8 * (half ^ (group // 2)) + (i8 + t) % 8
    same = 16 * group + (i16 + t - 23) % 16
    return jnp.where(t < 16, following, jnp.where(t < 24, opposite, same))


def grid(rows, columns):
    return (
        lax.broadcasted_iota(jnp.int32, (rows, columns), 0),
        lax.broadcasted_iota(jnp.int32, (rows, columns), 1),
    )


def masked_tiles(integrals, cd_irreps, ab_irreps):
    row_tiles = cd_irreps.shape[0]
    col_tiles = ab_irreps.shape[0]
    tile_size = integrals.shape[0] // row_tiles
    matching = (cd_irreps[:, None] == ab_irreps[None, :]).astype(jnp.bfloat16)
    tiled_view = (
        integrals.reshape(row_tiles, tile_size, col_tiles, tile_size) * matching[:, None, :, None]
    )
    return tiled_view.reshape(integrals.shape)


def own_pairs(amplitudes, r):
    to, held = grid(256, 512)
    wanted = (to % 8) * 64 + partner_of(8 * r + to % 8, to // 8)
    pick = (wanted == held).astype(jnp.bfloat16)
    return jnp.dot(pick, amplitudes, preferred_element_type=jnp.float32).astype(jnp.bfloat16)


def slot_sums_kernel(k_ref, panel_ref, *refs):
    *sources, mine_ref, theirs_ref = refs
    columns = panel_ref.shape[1]
    for s, source in enumerate(sources):
        sums = jnp.dot(source[...], panel_ref[...], preferred_element_type=jnp.float32)
        sums = sums.reshape(HI * Z, CORES, 8, columns)
        first = k_ref[0] == 0
        mine_ref[:, 8 * s : 8 * s + 8, :] = jnp.where(first, sums[:, 0], sums[:, 1])
        theirs_ref[:, 8 * s : 8 * s + 8, :] = jnp.where(first, sums[:, 1], sums[:, 0])


def slot_sums(k, panel, sources):
    depth, n = panel.shape
    tile = min(n, 256)
    rows = 8 * len(sources)
    out = jax.ShapeDtypeStruct((HI * Z, rows, n), jnp.float32)
    return pl.pallas_call(
        slot_sums_kernel,
        grid=(n // tile,),
        in_specs=[
            pl.BlockSpec(memory_space=pltpu.SMEM),
            pl.BlockSpec((depth, tile), lambda j: (0, j)),
        ]
        + [pl.BlockSpec((256, depth), lambda j: (0, 0))] * len(sources),
        out_specs=[pl.BlockSpec((HI * Z, rows, tile), lambda j: (0, 0, j))] * 2,
        out_shape=[out, out],
        compiler_params=pltpu.CompilerParams(vmem_limit_bytes=40 * 2**20),
        cost_estimate=pl.CostEstimate(
            flops=2 * 32 * rows * depth * n,
            bytes_accessed=2 * depth * (n + 32 * rows) + 4 * 32 * rows * n,
            transcendentals=0,
        ),
    )(k.reshape(1), panel, *sources)


def core_sum(mine, theirs):
    return ((mine + lax.ppermute(theirs, "col", CORE_SWAP)) * SCALE).astype(jnp.float16)


def col_sum(parts):
    got = lax.all_to_all(
        parts, "col", split_axis=0, concat_axis=0, axis_index_groups=HZ_GROUPS, tiled=True
    )
    return got.astype(jnp.float32).sum(0) * (1 / SCALE)


def exact_dot(a, b):
    return jnp.dot(a, b, precision=lax.Precision.HIGHEST)


def fock_terms(c, slab, occ_fock):
    ej, el = grid(128, 128)
    own = jnp.where(ej // 64 == el // 64, jnp.tile(occ_fock.T, (2, 2)), 0.0)
    mixed = 64 * ((ej // 2) % 2) + 2 * (ej // 4) + ej % 2
    order = (mixed == el).astype(jnp.float32)
    got = lax.all_to_all(
        exact_dot(exact_dot(order, own), slab), "col", split_axis=0, concat_axis=0, tiled=True
    )
    mirror = (2 * (el // 4) + (el // 2) % 2 == ej % 64) & (el % 2 == ej // 64)
    return exact_dot(own, slab) - exact_dot(mirror.astype(jnp.float32), got)


def per_device(amplitudes, integrals, cd_irreps, ab_irreps, slab_amplitudes, occ_fock):
    r, c = lax.axis_index("row"), lax.axis_index("col")
    x, l = r // 2, r % 2
    h, k = c // 16, c % 2

    own = own_pairs(amplitudes, r)
    partner = lax.ppermute(own, "row", Y_SWAP)
    left = lax.ppermute(own, "row", x_shift(1))
    right = lax.ppermute(own, "row", x_shift(-1))
    slab, _ = lax.optimization_barrier((slab_amplitudes, own))
    fock_update = fock_terms(c, slab.astype(jnp.float32), occ_fock)
    panel = masked_tiles(integrals, cd_irreps, ab_irreps)

    to_right = jnp.concatenate([left[:128], partner[128:]])
    to_left = jnp.concatenate([partner[:128], right[128:]])
    to_partner = jnp.concatenate([left[:128], right[128:]])
    to_right, to_left, to_partner, own, partner, left, right = lax.optimization_barrier(
        (to_right, to_left, to_partner, own, partner, left, right)
    )
    from_left = lax.ppermute(to_right, "row", x_shift(1))
    from_right = lax.ppermute(to_left, "row", x_shift(-1))
    across = lax.ppermute(to_partner, "row", Y_SWAP)
    first = core_sum(*slot_sums(k, panel, [own, partner, left, right]))

    to_right, to_left = across[:96], across[160:]
    to_partner = jnp.concatenate([from_left[96:128], from_right[128:160]])
    to_right, to_left, to_partner, first = lax.optimization_barrier(
        (to_right, to_left, to_partner, first)
    )
    first = col_sum(first)
    far_partner = jnp.concatenate(
        [
            lax.ppermute(to_right, "row", x_shift(1)),
            lax.ppermute(to_partner, "row", Y_SWAP),
            lax.ppermute(to_left, "row", x_shift(-1)),
        ]
    )
    second = core_sum(*slot_sums(k, panel, [from_left, from_right, across]))
    third = core_sum(*slot_sums(k, panel, [far_partner]))
    summed = jnp.concatenate([first, col_sum(jnp.concatenate([second, third], axis=1))])

    to, at = grid(128, 64)
    source = at // 8
    dx = jnp.where(h == 0, jnp.array([0, 0, 3, 1, 2, 1, 3, 2]), jnp.array([0, 0, 3, 1, 3, 2, 1, 2]))
    dl = jnp.where(h == 0, jnp.array([0, 1, 0, 0, 0, 1, 1, 1]), jnp.array([0, 1, 0, 0, 1, 0, 1, 1]))
    i = 16 * ((x + dx[source]) % 4) + 8 * (l ^ dl[source]) + at % 8
    wanted = 2 * (to // 4) + to % 2
    held = jnp.where(to % 4 < 2, i, partner_of(i, c))
    spread = (wanted == held).astype(jnp.float32)
    got = lax.all_to_all(exact_dot(spread, summed), "col", split_axis=0, concat_axis=0, tiled=True)

    ej, at = grid(128, 128)
    i, j = 2 * c + ej // 64, ej % 64
    t, mine = at // 4, at % 2 == ej // 64
    weight = jnp.where(t == 31, 1.0, 2.0)
    forward = jnp.where(mine & (at % 4 < 2) & (partner_of(i, t) == j), weight, 0.0)
    backward = jnp.where(mine & (at % 4 >= 2) & (partner_of(j, t) == i), weight, 0.0)
    return fock_update + exact_dot(forward - backward, got)


def solution(mesh):
    return jax.shard_map(
        per_device,
        mesh=mesh,
        in_specs=(P("row", "col"), P("col", "row"), P("col"), P("row"), P("col", "row"), P()),
        out_specs=P("col", "row"),
        check_vma=False,
    )
```

time: 211 us -> 191 us (0.905)
  waiting for transfers between devices: 106 us -> 74.6 us
  between operations: 13.9 us -> 0.48 us
  Pallas kernels: 0 us -> 11.7 us
  other arithmetic: 12.7 us -> 21.9 us
  matrix products: 11.5 us -> 19.6 us
  local copies, waits for them, and re-layouts: 29.9 us -> 22.1 us
  starting transfers between devices: 35.1 us -> 39.7 us
    all_to_all x3 -> x4, waiting for transfers between devices: 60.9 us -> 32.6 us  [the longest x2 14.7 us: col_sum(): lax.all_to_all(parts, 'col', split_axis=0, concat_axis=0, axis_index_grou...]
    ppermute x1, waiting for transfers between devices: 0.01 us -> 21.3 us  [per_device(): left = lax.ppermute(own, 'row', x_shift(1))]
    ppermute x9, waiting for transfers between devices: 38.7 us -> 19.1 us  [the longest x1 11.7 us: per_device(): lax.ppermute(to_partner, 'row', Y_SWAP)]
    pallas_call x0 -> x3, Pallas kernels: none -> 11.7 us  [slot_sums(): pl.pallas_call(slot_sums_kernel, grid=(n // tile,), in_specs=[pl.BlockSpe...]
    dot_general x5 -> x6, matrix products: 9.01 us -> 17.8 us  [exact_dot(): return jnp.dot(a, b, precision=lax.Precision.HIGHEST)]
    reduce_scatter x1 -> x0, waiting for transfers between devices: 6.64 us -> none  [per_device(): lax.psum_scatter(first, 'col', scatter_dimension=0, axis_index_groups=Z_G...]
    all_to_all x3 -> x4, starting transfers between devices: 23.9 us -> 30.1 us  [the longest x2 20.3 us: col_sum(): lax.all_to_all(parts, 'col', split_axis=0, concat_axis=0, axis_index_grou...]
    unnamed x31 -> x49, local copies, waits for them, and re-layouts: 13.7 us -> 8.47 us
  transfers between devices with their start and end apart: 16 -> 16, of which waited for: 10 -> 10; matrix products, arithmetic and copies ran while one was open for 10% -> 26% of each run, Pallas kernels for 0% -> 6%
where the time goes in v2:
time: 191 us; the launch traced here: 190 us
  waiting for transfers between devices  74.6 us (39%)
  starting transfers between devices  39.7 us (21%)
  local copies, waits for them, and re-layouts  22.1 us (12%)
  other arithmetic  21.9 us (11%)
  matrix products  19.6 us (10%)
  Pallas kernels  11.7 us (6%)
    ppermute x1, waiting for transfers between devices, per_device(): left = lax.ppermute(own, 'row', x_shift(1))  21.3 us
    all_to_all x2, starting transfers between devices, col_sum(): lax.all_to_all(parts, 'col', split_axis=0, concat_axis=0, axis_index_grou...  20.3 us
    dot_general x6, matrix products, exact_dot(): return jnp.dot(a, b, precision=lax.Precision.HIGHEST)  17.8 us
    all_to_all x2, waiting for transfers between devices, col_sum(): lax.all_to_all(parts, 'col', split_axis=0, concat_axis=0, axis_index_grou...  14.7 us
    all_to_all x1, waiting for transfers between devices, per_device(): lax.all_to_all(exact_dot(spread, summed), 'col', split_axis=0, concat_axi...  13.5 us
    ppermute x1, waiting for transfers between devices, per_device(): lax.ppermute(to_partner, 'row', Y_SWAP)  11.7 us
    pallas_call x3, Pallas kernels, slot_sums(): pl.pallas_call(slot_sums_kernel, grid=(n // tile,), in_specs=[pl.BlockSpe...  11.7 us
    unnamed x49, local copies, waits for them, and re-layouts  8.47 us
  transfers between devices with their start and end apart: 16, of which 10 were waited for; matrix products, arithmetic and copies ran while one was open for 26% of the time, Pallas kernels for 6%

profile of v2, /device:TPU:6, one launch (start us, length us, event | category | flops | bytes accessed | tf_op | source)
XLA Modules:
  0.0 190.0 jit_solution(8406313100881609673)
XLA Ops:
  0.0 1.6 copy-done
  1.6 1.8 convolution_convert_fusion.refs_0_
  3.4 2.3 %collective-permute-start = (bf16[256,2048]{1,0:T(8,128)(2,1)S(1)}, bf16[256,2048]{1,0:T(8,128)(2,1)S(1)}, u32[]{:S(2)}, u32[]{:S(2)}) collective-permute-start(bf16[256,2048]{1,0:T(8,128)(2,1)S(1)} %convolution_convert_fusion.refs_0_), channel_id=1, source_target_pairs={{0,64},{32,96},{64,128},{96,160},{128,192},{160,224},{192,0},{224,... | collective-permute-start | bytes 3145736 | tf_op jit(solution)/shard_map/ppermute | solution.py:124
  5.7 1.4 collective-permute-start.2
  7.0 21.3 %collective-permute-done.refs_2_ = bf16[256,2048]{1,0:T(8,128)(2,1)S(1)} collective-permute-done((bf16[256,2048]{1,0:T(8,128)(2,1)S(1)}, bf16[256,2048]{1,0:T(8,128)(2,1)S(1)}, u32[]{:S(2)}, u32[]{:S(2)}) %collective-permute-start) | collective-permute-done | bytes 1048608 | tf_op jit(solution)/shard_map/ppermute | solution.py:124
  28.4 1.0 copy-done.3
  29.4 1.6 collective-permute-done.2.refs_3_
  31.1 1.0 copy-done.5
  32.1 1.9 %pad_maximum_fusion = (bf16[256,2048]{1,0:T(8,128)(2,1)}, bf16[256,2048]{1,0:T(8,128)(2,1)}, bf16[256,2048]{1,0:T(8,128)(2,1)}) fusion(bf16[128,2048]{1,0:T(8,128)(2,1)S(1)} %slice.52, bf16[128,2048]{1,0:T(8,128)(2,1)S(1)} %slice.55, bf16[128,2048]{1,0:T(8,128)(2,1)S(1)} %get-tuple-element.43, bf16[128,2048]{1,0:T(8,128)(2,1)S(1)} %get-tuple-element.44), kind=kLoop, calls=%fused_computation.11 | loop fusion | flops 5242880 | bytes 5242880 | tf_op jit(solution)/shard_map/concatenate | solution.py:132
  34.4 1.3 collective-permute-start.4
  35.7 0.7 collective-permute-start.5
  36.5 0.5 mul.141
  37.0 3.0 %copy.16 = bf16[96,8,16,128]{3,1,2,0:T(8,128)(2,1)} copy(bf16[96,8,16,128]{3,2,1,0:T(8,128)(2,1)S(1)} %bitcast.56) | data formatting | bytes 6291456
  39.9 4.7 %copy.13 = bf16[2048,768]{1,0:T(8,128)(2,1)} copy(bf16[2048,768]{0,1:T(8,128)(2,1)} %bitcast.57) | data formatting | bytes 6291456 | tf_op jit(solution)/shard_map/mul | solution.py:43
  44.6 3.8 %mul.143.panel_ref = bf16[2048,768]{1,0:T(8,128)(2,1)S(1)} multiply(bf16[2048,768]{1,0:T(8,128)(2,1)} %param.11, bf16[2048,768]{1,0:T(8,128)(2,1)} %copy.13) | non-fusion elementwise | flops 1572864 | bytes 9437184 | tf_op jit(solution)/shard_map/mul | solution.py:43
  48.4 4.2 %shard_map.100 = (f32[16,32,768]{2,1,0:T(8,128)S(1)}, f32[16,32,768]{2,1,0:T(8,128)S(1)}) custom-call(s32[1]{0:T(128)} %bitcast.20.k_ref, bf16[2048,768]{1,0:T(8,128)(2,1)S(1)} %mul.143.panel_ref, bf16[256,2048]{1,0:T(8,128)(2,1)S(1)} %copy-done.8, bf16[256,2048]{1,0:T(8,128)(2,1)S(1)} %collective-permute-done.1.refs_1_, bf16[256,2048]{1,0:T(8,128)(2,1)S(1)} %copy-done.4, ...), custom_call_target="tpu_custom_call" | custom-call | flops 3221225472 | bytes 10485760 | tf_op jit(solution)/shard_map/pallas_call | solution.py:71
  52.8 0.6 compare_and_fusion.3
  53.3 4.2 %collective-permute-done.3.refs_2_ = bf16[256,2048]{1,0:T(8,128)(2,1)} collective-permute-done((bf16[256,2048]{1,0:T(8,128)(2,1)}, bf16[256,2048]{1,0:T(8,128)(2,1)}, u32[]{:S(2)}, u32[]{:S(2)}) %collective-permute-start.3) | collective-permute-done | bytes 1048608 | tf_op jit(solution)/shard_map/ppermute | solution.py:138
  58.1 2.6 %collective-permute-done.5.refs_1_ = bf16[256,2048]{1,0:T(8,128)(2,1)} collective-permute-done((bf16[256,2048]{1,0:T(8,128)(2,1)}, bf16[256,2048]{1,0:T(8,128)(2,1)}, u32[]{:S(2)}, u32[]{:S(2)}) %collective-permute-start.5) | collective-permute-done | bytes 1048608 | tf_op jit(solution)/shard_map/ppermute | solution.py:137
  60.7 5.8 %shard_map.101 = (f32[16,24,768]{2,1,0:T(8,128)S(1)}, f32[16,24,768]{2,1,0:T(8,128)}) custom-call(s32[1]{0:T(128)} %bitcast.20.k_ref, bf16[2048,768]{1,0:T(8,128)(2,1)S(1)} %mul.143.panel_ref, bf16[256,2048]{1,0:T(8,128)(2,1)} %collective-permute-done.4.refs_0_, bf16[256,2048]{1,0:T(8,128)(2,1)} %collective-permute-done.5.refs_1_, ...), custom_call_target="tpu_custom_call" | custom-call | flops 2415919104 | bytes 8650752 | tf_op jit(solution)/shard_map/pallas_call | solution.py:71
  66.5 0.9 slice.58
  67.4 0.9 slice.59
  68.3 0.7 pad_maximum_fusion.5
  69.0 2.1 %fusion.491 = (bf16[96,2048]{1,0:T(8,128)(2,1)}, bf16[96,2048]{1,0:T(8,128)(2,1)}) fusion(bf16[256,2048]{1,0:T(8,128)(2,1)} %collective-permute-done.3.refs_2_), kind=kLoop, calls=%fused_computation.677 | loop fusion | bytes 1572864 | tf_op jit(solution)/shard_map/slice | solution.py:141
  71.1 1.1 multiply_convert_fusion
  72.3 3.2 %collective-permute-start.8 = (bf16[96,2048]{1,0:T(8,128)(2,1)}, bf16[96,2048]{1,0:T(8,128)(2,1)}, u32[]{:S(2)}, u32[]{:S(2)}) collective-permute-start(bf16[96,2048]{1,0:T(8,128)(2,1)} %get-tuple-element.36), channel_id=1, source_target_pairs={{0,64},{32,96},{64,128},{96,160},{128,192},{160,224},{192,0},{224,... | collective-permute-start | bytes 1179656 | tf_op jit(solution)/shard_map/ppermute | solution.py:149
  75.5 11.0 %all-to-all-start.1 = ((f16[16,32,768]{2,1,0:T(8,128)(2,1)}), f16[16,32,768]{2,1,0:T(8,128)(2,1)}, u32[]{:S(2)}, u32[]{:S(2)}) async-start(f16[16,32,768]{2,1,0:T(8,128)(2,1)} %multiply_convert_fusion), calls=%async_computation.1 | async-start | bytes 1572864 | tf_op jit(solution)/shard_map/all_to_all | solution.py:95
  86.5 0.5 iota_and_fusion
  87.2 0.5 broadcast_add_fusion.5
  88.0 0.6 compare_and_fusion.7
  88.5 11.7 %collective-permute-done.9 = bf16[64,2048]{1,0:T(8,128)(2,1)} collective-permute-done((bf16[64,2048]{1,0:T(8,128)(2,1)}, bf16[64,2048]{1,0:T(8,128)(2,1)}, u32[]{:S(2)}, u32[]{:S(2)}) %collective-permute-start.9) | collective-permute-done | bytes 262176 | tf_op jit(solution)/shard_map/ppermute | solution.py:150
  100.3 1.3 pad_maximum_fusion.3.refs_0_
  101.6 1.9 copy-done.2
  103.5 1.7 shard_map.102
  105.2 0.6 iota_shift-right-logical_fusion.1
  105.8 1.4 multiply_convert_fusion.1
  107.4 1.1 pad_maximum_fusion.4
  108.5 0.8 all-to-all-done.1
  109.4 9.3 %all-to-all-start.2 = ((f16[16,32,768]{2,1,0:T(8,128)(2,1)}), f16[16,32,768]{2,1,0:T(8,128)(2,1)S(1)}, u32[]{:S(2)}, u32[]{:S(2)}) async-start(f16[16,32,768]{2,1,0:T(8,128)(2,1)} %pad_maximum_fusion.4), calls=%async_computation.2 | async-start | bytes 1572864 | tf_op jit(solution)/shard_map/all_to_all | solution.py:95
  118.7 1.0 fusion.183
  119.8 1.1 fusion.495
  120.9 0.9 all_to_all.22
  121.8 0.6 compare_and_fusion.2
  122.4 0.6 iota_and_fusion.1
  123.0 0.5 compare_and_fusion
  123.5 0.6 iota_shift-right-logical_fusion.3
  124.1 0.6 broadcast_add_fusion.1
  124.7 0.7 broadcast_select_fusion
  125.4 0.7 fusion.494
  126.0 0.7 fusion.493
  126.7 1.9 convert_reduce_fusion.1
  128.6 13.9 %all-to-all-done.2 = f16[16,32,768]{2,1,0:T(8,128)(2,1)S(1)} async-done(((f16[16,32,768]{2,1,0:T(8,128)(2,1)}), f16[16,32,768]{2,1,0:T(8,128)(2,1)S(1)}, u32[]{:S(2)}, u32[]{:S(2)}) %all-to-all-start.2) | async-done | bytes 786464 | tf_op jit(solution)/shard_map/all_to_all | solution.py:95
  142.5 4.5 %all-to-all-start = ((f32[32,4,768]{2,1,0:T(4,128)}), f32[32,4,768]{2,1,0:T(4,128)S(1)}, u32[]{:S(2)}, u32[]{:S(2)}) async-start(f32[32,4,768]{2,1,0:T(4,128)} %all_to_all.22), calls=%async_computation | async-start | bytes 786432 | tf_op jit(solution)/shard_map/all_to_all | solution.py:110
  147.0 0.9 broadcast_multiply_fusion.1
  148.0 11.1 %fusion.80 = f32[128,768]{1,0:T(8,128)S(1)} fusion(f32[32,768]{1,0:T(8,128)S(1)} %broadcast_multiply_fusion, f32[32,768]{1,0:T(8,128)S(1)} %broadcast_multiply_fusion.1, s32[]{:T(128)} %bitcast.12, s32[]{:T(128)} %bitcast.3, s32[]{:T(128)} %bitcast.13, s32[]{:T(128)} %bitcast.4, s32[]{:T(128)} %bitcast.14, s32[]{:T(128)} %bitcast.5, s32[]{:T(128)} %bitcast.15, ...), kind=kOutput, calls=%fused_computation.140 | convolution fusion | flops 77029376 | bytes 594510 | tf_op jit(solution)/shard_map/dot_general | solution.py:102
  159.1 0.9 all_to_all.27
  160.0 4.4 %all-to-all-done = f32[32,4,768]{2,1,0:T(4,128)S(1)} async-done(((f32[32,4,768]{2,1,0:T(4,128)}), f32[32,4,768]{2,1,0:T(4,128)S(1)}, u32[]{:S(2)}, u32[]{:S(2)}) %all-to-all-start) | async-done | bytes 393248 | tf_op jit(solution)/shard_map/all_to_all | solution.py:110
  164.4 5.4 %all-to-all-start.3 = ((f32[32,4,768]{2,1,0:T(4,128)}), f32[32,4,768]{2,1,0:T(4,128)S(1)}, u32[]{:S(2)}, u32[]{:S(2)}) async-start(f32[32,4,768]{2,1,0:T(4,128)} %all_to_all.27), calls=%async_computation.3 | async-start | bytes 786432 | tf_op jit(solution)/shard_map/all_to_all | solution.py:166
  169.8 0.6 compare_and_fusion.4
  170.4 0.5 iota_and_fusion.4
  171.3 0.9 all_to_all.24
  172.2 1.5 convolution_subtract_fusion
  173.7 13.5 %all-to-all-done.3 = f32[32,4,768]{2,1,0:T(4,128)S(1)} async-done(((f32[32,4,768]{2,1,0:T(4,128)}), f32[32,4,768]{2,1,0:T(4,128)S(1)}, u32[]{:S(2)}, u32[]{:S(2)}) %all-to-all-start.3) | async-done | bytes 393248 | tf_op jit(solution)/shard_map/all_to_all | solution.py:166
  187.4 2.6 %convolution_add_fusion = f32[128,768]{1,0:T(8,128)} fusion(f32[128,768]{1,0:T(8,128)S(1)} %convolution_subtract_fusion, f32[128,768]{1,0:T(8,128)S(1)} %all_to_all.29, s32[]{:T(128)S(6)} %mul.125, s32[128]{0:T(128)} %get-tuple-element.88, s32[128]{0:T(128)} %get-tuple-element.89, s32[128]{0:T(128)} %get-tuple-element.78, s32[128]{0:T(128)} %get-tuple-element.82, ...), kind=kOutput, calls=%fused_computation.9 | convolution fusion | flops 155713536 | bytes 1185412 | tf_op jit(solution)/shard_map/dot_general | solution.py:102
  (74 shorter events, 2.4 us)
Async XLA Ops:
  0.0 1.6 copy-start
  3.4 28.7 %copy-start.7 = (bf16[256,2048]{1,0:T(8,128)(2,1)}, bf16[256,2048]{1,0:T(8,128)(2,1)S(1)}, u32[]{:S(2)}) copy-start(bf16[256,2048]{1,0:T(8,128)(2,1)S(1)} %convolution_convert_fusion.refs_0_) | copy-start | bytes 3145732
  3.4 25.0 %collective-permute-start = (bf16[256,2048]{1,0:T(8,128)(2,1)S(1)}, bf16[256,2048]{1,0:T(8,128)(2,1)S(1)}, u32[]{:S(2)}, u32[]{:S(2)}) collective-permute-start(bf16[256,2048]{1,0:T(8,128)(2,1)S(1)} %convolution_convert_fusion.refs_0_), channel_id=1, source_target_pairs={{0,64},{32,96},{64,128},{96,160},{128,192},{160,224},{192,0},{224,... | collective-permute-start | bytes 3145736 | tf_op jit(solution)/shard_map/ppermute | solution.py:124
  5.7 23.7 %collective-permute-start.1 = (bf16[256,2048]{1,0:T(8,128)(2,1)S(1)}, bf16[256,2048]{1,0:T(8,128)(2,1)S(1)}, u32[]{:S(2)}, u32[]{:S(2)}) collective-permute-start(bf16[256,2048]{1,0:T(8,128)(2,1)S(1)} %convolution_convert_fusion.refs_0_), channel_id=1, source_target_pairs={{0,32},{32,0},{64,96},{96,64},{128,160},{160,128},{192,224},{224,1... | collective-permute-start | bytes 3145736 | tf_op jit(solution)/shard_map/ppermute | solution.py:123
  5.7 25.4 %collective-permute-start.2 = (bf16[256,2048]{1,0:T(8,128)(2,1)S(1)}, bf16[256,2048]{1,0:T(8,128)(2,1)S(1)}, u32[]{:S(2)}, u32[]{:S(2)}) collective-permute-start(bf16[256,2048]{1,0:T(8,128)(2,1)S(1)} %convolution_convert_fusion.refs_0_), channel_id=1, source_target_pairs={{0,192},{32,224},{64,0},{96,32},{128,64},{160,96},{192,128},{224,1... | collective-permute-start | bytes 3145736 | tf_op jit(solution)/shard_map/ppermute | solution.py:125
  28.4 1.0 copy-start.3
  31.1 1.0 copy-start.5
  32.1 4.3 %copy-start.22 = (s32[16]{0:T(128)S(1)}, s32[16]{0:T(128)}, u32[]{:S(2)}) copy-start(s32[16]{0:T(128)} %param.12) | copy-start | bytes 196
  32.1 4.3 %copy-start.23 = (s32[6]{0:T(128)S(1)}, s32[6]{0:T(128)}, u32[]{:S(2)}) copy-start(s32[6]{0:T(128)} %param.13) | copy-start | bytes 76
  34.0 23.6 %collective-permute-start.3 = (bf16[256,2048]{1,0:T(8,128)(2,1)}, bf16[256,2048]{1,0:T(8,128)(2,1)}, u32[]{:S(2)}, u32[]{:S(2)}) collective-permute-start(bf16[256,2048]{1,0:T(8,128)(2,1)} %get-tuple-element.24), channel_id=1, source_target_pairs={{0,32},{32,0},{64,96},{96,64},{128,160},{160,128},{192,224},{224,1... | collective-permute-start | bytes 3145736 | tf_op jit(solution)/shard_map/ppermute | solution.py:138
  34.4 23.7 %collective-permute-start.4 = (bf16[256,2048]{1,0:T(8,128)(2,1)}, bf16[256,2048]{1,0:T(8,128)(2,1)}, u32[]{:S(2)}, u32[]{:S(2)}) collective-permute-start(bf16[256,2048]{1,0:T(8,128)(2,1)} %get-tuple-element.25), channel_id=1, source_target_pairs={{0,64},{32,96},{64,128},{96,160},{128,192},{160,224},{192,0},{224,... | collective-permute-start | bytes 3145736 | tf_op jit(solution)/shard_map/ppermute | solution.py:136
  35.7 25.0 %collective-permute-start.5 = (bf16[256,2048]{1,0:T(8,128)(2,1)}, bf16[256,2048]{1,0:T(8,128)(2,1)}, u32[]{:S(2)}, u32[]{:S(2)}) collective-permute-start(bf16[256,2048]{1,0:T(8,128)(2,1)} %get-tuple-element.26), channel_id=1, source_target_pairs={{0,192},{32,224},{64,0},{96,32},{128,64},{160,96},{192,128},{224,1... | collective-permute-start | bytes 3145736 | tf_op jit(solution)/shard_map/ppermute | solution.py:137
  44.6 3.8 %copy-start.4 = (bf16[256,2048]{1,0:T(8,128)(2,1)S(1)}, bf16[256,2048]{1,0:T(8,128)(2,1)}, u32[]{:S(2)}) copy-start(bf16[256,2048]{1,0:T(8,128)(2,1)} %copy-done.3) | copy-start | bytes 3145732
  44.6 3.8 %copy-start.6 = (bf16[256,2048]{1,0:T(8,128)(2,1)S(1)}, bf16[256,2048]{1,0:T(8,128)(2,1)}, u32[]{:S(2)}) copy-start(bf16[256,2048]{1,0:T(8,128)(2,1)} %copy-done.5) | copy-start | bytes 3145732
  44.6 3.8 %copy-start.8 = (bf16[256,2048]{1,0:T(8,128)(2,1)S(1)}, bf16[256,2048]{1,0:T(8,128)(2,1)}, u32[]{:S(2)}) copy-start(bf16[256,2048]{1,0:T(8,128)(2,1)} %copy-done.7) | copy-start | bytes 3145732
  48.4 12.3 %copy-start.1 = (bf16[2048,768]{1,0:T(8,128)(2,1)}, bf16[2048,768]{1,0:T(8,128)(2,1)S(1)}, u32[]{:S(2)}) copy-start(bf16[2048,768]{1,0:T(8,128)(2,1)S(1)} %mul.143.panel_ref) | copy-start | bytes 9437188
  52.7 18.5 %collective-permute-start.6 = (f32[16,32,768]{2,1,0:T(8,128)S(1)}, f32[16,32,768]{2,1,0:T(8,128)S(1)}, u32[]{:S(2)}, u32[]{:S(2)}) collective-permute-start(f32[16,32,768]{2,1,0:T(8,128)S(1)} %get-tuple-element.32), channel_id=1, source_target_pairs={{0,1},{1,0},{2,3},{3,2},{4,5},{5,4},{6,7},{7,6},{8,9},{9,8},{10,11... | collective-permute-start | bytes 4718600 | tf_op jit(solution)/shard_map/ppermute | solution.py:91
  66.5 39.3 %collective-permute-start.7 = (f32[16,24,768]{2,1,0:T(8,128)}, f32[16,24,768]{2,1,0:T(8,128)}, u32[]{:S(2)}, u32[]{:S(2)}) collective-permute-start(f32[16,24,768]{2,1,0:T(8,128)} %get-tuple-element.35), channel_id=1, source_target_pairs={{0,1},{1,0},{2,3},{3,2},{4,5},{5,4},{6,7},{7,6},{8,9},{9,8},{10,11... | collective-permute-start | bytes 3538952 | tf_op jit(solution)/shard_map/ppermute | solution.py:91
  71.1 16.6 %copy-start.10 = (f32[64,64]{1,0:T(8,128)S(1)}, f32[64,64]{1,0:T(8,128)}, u32[]{:S(2)}) copy-start(f32[64,64]{1,0:T(8,128)} %param.15) | copy-start | bytes 49156
  72.3 28.0 %collective-permute-start.10 = (bf16[96,2048]{1,0:T(8,128)(2,1)}, bf16[96,2048]{1,0:T(8,128)(2,1)}, u32[]{:S(2)}, u32[]{:S(2)}) collective-permute-start(bf16[96,2048]{1,0:T(8,128)(2,1)} %get-tuple-element.38), channel_id=1, source_target_pairs={{0,192},{32,224},{64,0},{96,32},{128,64},{160,96},{192,128},{224,1... | collective-permute-start | bytes 1179656 | tf_op jit(solution)/shard_map/ppermute | solution.py:151
  72.3 28.0 %collective-permute-start.8 = (bf16[96,2048]{1,0:T(8,128)(2,1)}, bf16[96,2048]{1,0:T(8,128)(2,1)}, u32[]{:S(2)}, u32[]{:S(2)}) collective-permute-start(bf16[96,2048]{1,0:T(8,128)(2,1)} %get-tuple-element.36), channel_id=1, source_target_pairs={{0,64},{32,96},{64,128},{96,160},{128,192},{160,224},{192,0},{224,... | collective-permute-start | bytes 1179656 | tf_op jit(solution)/shard_map/ppermute | solution.py:149
  75.5 33.8 %all-to-all-start.1 = ((f16[16,32,768]{2,1,0:T(8,128)(2,1)}), f16[16,32,768]{2,1,0:T(8,128)(2,1)}, u32[]{:S(2)}, u32[]{:S(2)}) async-start(f16[16,32,768]{2,1,0:T(8,128)(2,1)} %multiply_convert_fusion), calls=%async_computation.1 | async-start | bytes 1572864 | tf_op jit(solution)/shard_map/all_to_all | solution.py:95
  87.0 13.2 %collective-permute-start.9 = (bf16[64,2048]{1,0:T(8,128)(2,1)}, bf16[64,2048]{1,0:T(8,128)(2,1)}, u32[]{:S(2)}, u32[]{:S(2)}) collective-permute-start(bf16[64,2048]{1,0:T(8,128)(2,1)} %pad_maximum_fusion.5), channel_id=1, source_target_pairs={{0,32},{32,0},{64,96},{96,64},{128,160},{160,128},{192,224},{224,1... | collective-permute-start | bytes 786440 | tf_op jit(solution)/shard_map/ppermute | solution.py:150
  101.6 1.9 copy-start.2
  105.1 2.2 %collective-permute-start.11 = (f32[16,8,768]{2,1,0:T(8,128)S(1)}, f32[16,8,768]{2,1,0:T(8,128)S(1)}, u32[]{:S(2)}, u32[]{:S(2)}) collective-permute-start(f32[16,8,768]{2,1,0:T(8,128)S(1)} %get-tuple-element.40), channel_id=1, source_target_pairs={{0,1},{1,0},{2,3},{3,2},{4,5},{5,4},{6,7},{7,6},{8,9},{9,8},{10,11... | collective-permute-start | bytes 1179656 | tf_op jit(solution)/shard_map/ppermute | solution.py:91
  107.2 11.4 %copy-start.11 = (pred[128]{0:T(512)(128)(4,1)S(1)}, pred[128]{0:T(512)(128)(4,1)}, u32[]{:S(2)}) copy-start(pred[128]{0:T(512)(128)(4,1)} %get-tuple-element.75) | copy-start | bytes 388
  107.3 11.4 %copy-start.12 = (s32[128]{0:T(128)S(1)}, s32[128]{0:T(128)}, u32[]{:S(2)}) copy-start(s32[128]{0:T(128)} %get-tuple-element.78) | copy-start | bytes 1540
  107.3 11.4 %copy-start.13 = (s32[128]{0:T(128)S(1)}, s32[128]{0:T(128)}, u32[]{:S(2)}) copy-start(s32[128]{0:T(128)} %get-tuple-element.79) | copy-start | bytes 1540
  107.3 11.4 %copy-start.14 = (s32[128]{0:T(128)S(1)}, s32[128]{0:T(128)}, u32[]{:S(2)}) copy-start(s32[128]{0:T(128)} %get-tuple-element.82) | copy-start | bytes 1540
  107.3 11.4 %copy-start.15 = (s32[128]{0:T(128)S(1)}, s32[128]{0:T(128)}, u32[]{:S(2)}) copy-start(s32[128]{0:T(128)} %get-tuple-element.83) | copy-start | bytes 1540
  107.3 11.4 %copy-start.16 = (pred[128]{0:T(512)(128)(4,1)S(1)}, pred[128]{0:T(512)(128)(4,1)}, u32[]{:S(2)}) copy-start(pred[128]{0:T(512)(128)(4,1)} %get-tuple-element.80) | copy-start | bytes 388
  107.3 11.4 %copy-start.17 = (s32[128]{0:T(128)S(1)}, s32[128]{0:T(128)}, u32[]{:S(2)}) copy-start(s32[128]{0:T(128)} %get-tuple-element.76) | copy-start | bytes 1540
  107.3 11.4 %copy-start.18 = (s32[128]{0:T(128)S(1)}, s32[128]{0:T(128)}, u32[]{:S(2)}) copy-start(s32[128]{0:T(128)} %get-tuple-element.77) | copy-start | bytes 1540
  107.4 12.4 %copy-start.9 = (bf16[128,768]{1,0:T(8,128)(2,1)S(1)}, bf16[128,768]{1,0:T(8,128)(2,1)}, u32[]{:S(2)}) copy-start(bf16[128,768]{1,0:T(8,128)(2,1)} %param.14) | copy-start | bytes 589828
  109.4 33.2 %all-to-all-start.2 = ((f16[16,32,768]{2,1,0:T(8,128)(2,1)}), f16[16,32,768]{2,1,0:T(8,128)(2,1)S(1)}, u32[]{:S(2)}, u32[]{:S(2)}) async-start(f16[16,32,768]{2,1,0:T(8,128)(2,1)} %pad_maximum_fusion.4), calls=%async_computation.2 | async-start | bytes 1572864 | tf_op jit(solution)/shard_map/all_to_all | solution.py:95
  142.5 21.9 %all-to-all-start = ((f32[32,4,768]{2,1,0:T(4,128)}), f32[32,4,768]{2,1,0:T(4,128)S(1)}, u32[]{:S(2)}, u32[]{:S(2)}) async-start(f32[32,4,768]{2,1,0:T(4,128)} %all_to_all.22), calls=%async_computation | async-start | bytes 786432 | tf_op jit(solution)/shard_map/all_to_all | solution.py:110
  164.4 22.8 %all-to-all-start.3 = ((f32[32,4,768]{2,1,0:T(4,128)}), f32[32,4,768]{2,1,0:T(4,128)S(1)}, u32[]{:S(2)}, u32[]{:S(2)}) async-start(f32[32,4,768]{2,1,0:T(4,128)} %all_to_all.27), calls=%async_computation.3 | async-start | bytes 786432 | tf_op jit(solution)/shard_map/all_to_all | solution.py:166
  171.3 16.0 %copy-start.19 = (pred[128]{0:T(512)(128)(4,1)S(1)}, pred[128]{0:T(512)(128)(4,1)}, u32[]{:S(2)}) copy-start(pred[128]{0:T(512)(128)(4,1)} %compare_and_fusion.4) | copy-start | bytes 388
  171.3 16.0 %copy-start.20 = (s32[128]{0:T(128)S(1)}, s32[128]{0:T(128)}, u32[]{:S(2)}) copy-start(s32[128]{0:T(128)} %get-tuple-element.84) | copy-start | bytes 1540
  171.3 16.0 %copy-start.21 = (s32[128]{0:T(128)S(1)}, s32[128]{0:T(128)}, u32[]{:S(2)}) copy-start(s32[128]{0:T(128)} %get-tuple-element.85) | copy-start | bytes 1540

commit v3 on v0

v3 whole, which is shorter than its diff:
```python
import functools

import jax
import jax.numpy as jnp
from jax import lax
from jax.experimental import pallas as pl
from jax.experimental.pallas import tpu as pltpu
from jax.sharding import PartitionSpec as P

X, LO, HI, Z, CORES = 4, 2, 2, 8, 2
COLS = HI * Z * CORES
SCALE = 64.0
LADDER_SCALE, FOCK_SCALE = 4.0, 128.0
COST = 40 * 10**9
SCALARS = pl.BlockSpec(memory_space=pltpu.SMEM)


def x_shift(step):
    return [(2 * x + l, 2 * ((x + step) % X) + l) for x in range(X) for l in range(LO)]


Y_SWAP = [(r, r ^ 1) for r in range(X * LO)]
CORE_SWAP = [(c, c ^ 1) for c in range(COLS)]
HZ_GROUPS = [[2 * hz + k for hz in range(HI * Z)] for k in range(CORES)]


def partner_of(i, t):
    group, half = i >> 4, (i >> 3) & 1
    following = (((group + 1) & 3) << 4) + ((i + t) & 15)
    opposite = (((group + 2) & 3) << 4) + ((half ^ (group >> 1)) << 3) + ((i + t) & 7)
    same = (group << 4) + ((i + t - 23) & 15)
    return jnp.where(t < 16, following, jnp.where(t < 24, opposite, same))


def grid(rows, columns):
    return (
        lax.broadcasted_iota(jnp.int32, (rows, columns), 0),
        lax.broadcasted_iota(jnp.int32, (rows, columns), 1),
    )


def masked_tiles_kernel(cd_ref, ab_ref, integrals_ref, out_ref):
    j = pl.program_id(0)
    row_tiles = cd_ref.shape[0]
    size = integrals_ref.shape[0] // row_tiles
    for b in range(integrals_ref.shape[1] // size):
        irrep = ab_ref[j * (integrals_ref.shape[1] // size) + b]
        for a in range(row_tiles):
            at = (slice(a * size, a * size + size), slice(b * size, b * size + size))
            matching = (cd_ref[a] == irrep).astype(jnp.float32).astype(jnp.bfloat16)
            out_ref[at] = integrals_ref[at] * matching


def masked_tiles(integrals, cd_irreps, ab_irreps):
    depth, n = integrals.shape
    tile = min(n, 256)
    block = pl.BlockSpec((depth, tile), lambda j: (0, j))
    return pl.pallas_call(
        masked_tiles_kernel,
        grid=(n // tile,),
        in_specs=[SCALARS, SCALARS, block],
        out_specs=block,
        out_shape=jax.ShapeDtypeStruct((depth, n), jnp.bfloat16),
        compiler_params=pltpu.CompilerParams(vmem_limit_bytes=16 * 2**20),
        cost_estimate=pl.CostEstimate(flops=0, bytes_accessed=4 * depth * n, transcendentals=0),
    )(cd_irreps, ab_irreps, integrals)


def own_pairs_kernel(r_ref, amplitudes_ref, own_ref, right_ref, mirrored_ref):
    r = r_ref[0]
    x, l = r >> 1, r & 1
    to, held = grid(448, 512)
    rho, j = to & 7, (r << 3) + (to & 7)
    t = to >> 3
    direct = (rho << 6) + partner_of(j, t)
    before = (((x + 3) & 3) << 4) + ((j - t) & 15)
    opposite = (x + 2) & 3
    across = (opposite << 4) + ((l ^ (opposite >> 1)) << 3) + ((j - t) & 7)
    wanted = jnp.where(to < 256, direct, (rho << 6) + jnp.where(to < 384, before, across))
    sign = jnp.where(to < 256, 1.0, -1.0)
    pick = jnp.where(wanted == held, sign, 0.0).astype(jnp.bfloat16)
    rows = jnp.dot(pick, amplitudes_ref[...], preferred_element_type=jnp.float32)
    rows = rows.astype(jnp.bfloat16)
    own_ref[...] = rows[:256]
    right_ref[...] = rows[128:384]
    mirrored_ref[...] = rows[256:]


def by_depth(kernel, scalars, arrays, out_rows, flops=0):
    depth = arrays[0].shape[1]
    tile = min(depth, 512)
    outs = [jax.ShapeDtypeStruct((rows, depth), jnp.bfloat16) for rows in out_rows]
    return pl.pallas_call(
        kernel,
        grid=(depth // tile,),
        in_specs=[SCALARS] * len(scalars)
        + [pl.BlockSpec((a.shape[0], tile), lambda j: (0, j)) for a in arrays],
        out_specs=[pl.BlockSpec((rows, tile), lambda j: (0, j)) for rows in out_rows],
        out_shape=outs,
        compiler_params=pltpu.CompilerParams(vmem_limit_bytes=32 * 2**20),
        cost_estimate=pl.CostEstimate(flops=flops, bytes_accessed=0, transcendentals=0),
    )(*scalars, *arrays)


def second_phase_kernel(partner_ref, left_ref, mirrored_ref, right_out, across_out, far_out):
    right_out[:128] = partner_ref[128:]
    right_out[128:] = left_ref[64:128]
    across_out[:192] = mirrored_ref[...]
    across_out[192:] = left_ref[128:]
    far_out[...] = partner_ref[192:]


OWN, MIRROR = 0, 1
SOURCES = (
    ((OWN, 0, 0),) * 3,
    ((OWN, 0, 1),) * 3,
    ((OWN, 1, 0),) * 3,
    ((MIRROR, 3, 0), (OWN, 3, 0), (OWN, 3, 0)),
    ((OWN, 1, 1),) * 3,
    ((MIRROR, 0, 0), (MIRROR, 0, 0), (OWN, 2, 0)),
    ((MIRROR, 0, 1), (MIRROR, 0, 1), (OWN, 2, 1)),
    ((MIRROR, 3, 1), (OWN, 3, 1), (OWN, 3, 1)),
)
FIRST = (((0, 0, 256),), ((1, 0, 256),), ((2, 0, 256),), ((3, 128, 256), (3, 0, 128)))
SECOND = (
    ((0, 0, 256),),
    ((1, 0, 192), (2, 128, 192)),
    ((3, 0, 192), (4, 0, 64)),
    ((3, 192, 320), (2, 0, 128)),
)


def slot_sums_kernel(layout, k_ref, panel_ref, *refs):
    *arrays, mine_ref, theirs_ref = refs
    columns = panel_ref.shape[1]
    for s, pieces in enumerate(layout):
        rows = [arrays[at][start:end, :] for at, start, end in pieces]
        rows = rows[0] if len(rows) == 1 else jnp.concatenate(rows)
        sums = jnp.dot(rows, panel_ref[...], preferred_element_type=jnp.float32)
        sums = sums.reshape(HI * Z, CORES, 8, columns)
        first = k_ref[0] == 0
        mine_ref[:, 8 * s : 8 * s + 8, :] = jnp.where(first, sums[:, 0], sums[:, 1])
        theirs_ref[:, 8 * s : 8 * s + 8, :] = jnp.where(first, sums[:, 1], sums[:, 0])


def slot_sums(k, panel, layout, arrays, flops):
    depth, n = panel.shape
    tile = min(n, 256)
    rows = 8 * len(layout)
    out = jax.ShapeDtypeStruct((HI * Z, rows, n), jnp.float32)
    return pl.pallas_call(
        functools.partial(slot_sums_kernel, layout),
        grid=(n // tile,),
        in_specs=[SCALARS, pl.BlockSpec((depth, tile), lambda j: (0, j))]
        + [pl.BlockSpec(a.shape, lambda j: (0, 0)) for a in arrays],
        out_specs=[pl.BlockSpec((HI * Z, rows, tile), lambda j: (0, 0, j))] * 2,
        out_shape=[out, out],
        compiler_params=pltpu.CompilerParams(vmem_limit_bytes=40 * 2**20),
        cost_estimate=pl.CostEstimate(flops=flops, bytes_accessed=0, transcendentals=0),
    )(k.reshape(1), panel, *arrays)


def core_sum(mine, theirs):
    return ((mine + lax.ppermute(theirs, "col", CORE_SWAP)) * SCALE).astype(jnp.float16)


def send_to_slots(parts):
    got = lax.all_to_all(
        parts, "col", split_axis=0, concat_axis=0, axis_index_groups=HZ_GROUPS, tiled=True
    )
    return got.astype(jnp.float32).sum(0)


def exact_dot(a, b):
    return jnp.dot(
        a, b, precision=lax.Precision.HIGHEST, preferred_element_type=jnp.float32
    )


def whole(kernel, scalars, arrays, rows, n):
    tile = n

    def block(shape):
        if shape[-1] != n:
            return pl.BlockSpec(shape, lambda j: (0,) * len(shape))
        return pl.BlockSpec(shape[:-1] + (tile,), lambda j: (0,) * (len(shape) - 1) + (j,))

    return pl.pallas_call(
        kernel,
        grid=(n // tile,),
        in_specs=[SCALARS] + [block(a.shape) for a in arrays],
        out_specs=block((rows, n)),
        out_shape=jax.ShapeDtypeStruct((rows, n), jnp.float32),
        compiler_params=pltpu.CompilerParams(vmem_limit_bytes=32 * 2**20),
        cost_estimate=pl.CostEstimate(
            flops=0, bytes_accessed=sum(a.size * a.dtype.itemsize for a in arrays), transcendentals=0
        ),
    )(scalars, *arrays)


def fock_matrix(fock_ref):
    ej, el = grid(128, 128)
    return jnp.where((ej >> 6) == (el >> 6), fock_ref[...], 0.0)


def fock_kernel(_, fock_ref, slab_ref, out_ref):
    out_ref[...] = exact_dot(fock_matrix(fock_ref), slab_ref[...].astype(jnp.float32))


def spread_kernel(at_ref, first_ref, second_ref, fock_ref, out_ref):
    x, l, c = at_ref[0], at_ref[1], at_ref[2]
    to, at = grid(256, 64)
    source, rho = at >> 3, at & 7
    i = jnp.zeros_like(at)
    for s, ranges in enumerate(SOURCES):
        options = []
        for (kind, dx, dl), narrow in zip(ranges, (False, True, True)):
            group, half = (x + dx) & 3, l ^ dl
            if kind == OWN:
                options.append((group << 4) + (half << 3) + rho)
            elif narrow:
                opposite = (group + 2) & 3
                options.append((opposite << 4) + ((half ^ (opposite >> 1)) << 3) + ((rho - c) & 7))
            else:
                options.append((((group + 3) & 3) << 4) + (((half << 3) + rho - c) & 15))
        chosen = jnp.where(c < 16, options[0], jnp.where(c < 24, options[1], options[2]))
        i = jnp.where(source == s, chosen, i)
    wanted = ((to >> 3) << 1) + (to & 1)
    held = jnp.where((to & 2) == 0, i, partner_of(i, c))
    spread = jnp.where((wanted == held) & ((to & 4) == 0), LADDER_SCALE / SCALE, 0.0)
    to, ej = grid(256, 128)
    order = ((((to >> 1) & 1) << 6) + ((to >> 3) << 1) + (to & 1) == ej) & ((to & 4) != 0)
    out_ref[...] = exact_dot(
        jnp.concatenate([spread, jnp.where(order, FOCK_SCALE, 0.0)], axis=1),
        jnp.concatenate([first_ref[...], second_ref[...], fock_ref[...]]),
    )


def update_kernel(at_ref, fock_ref, got_ref, out_ref):
    ej, at = grid(128, 256)
    e, j = ej >> 6, ej & 63
    i, t, mine = 2 * at_ref[2] + e, at >> 3, (at & 1) == e
    weight = jnp.where(t == 31, 1 / LADDER_SCALE, 2 / LADDER_SCALE)
    forward = jnp.where(mine & ((at & 6) == 0) & (partner_of(i, t) == j), weight, 0.0)
    backward = jnp.where(mine & ((at & 6) == 2) & (partner_of(j, t) == i), weight, 0.0)
    mirror = jnp.where(mine & ((at & 4) != 0) & ((t << 1) + ((at >> 1) & 1) == j), 1 / FOCK_SCALE, 0.0)
    out_ref[...] = fock_ref[...] + exact_dot(forward - backward - mirror, got_ref[...])


def exchange(rows):
    return lax.all_to_all(rows, "col", split_axis=0, concat_axis=0, tiled=True)


def per_device(amplitudes, integrals, cd_irreps, ab_irreps, slab, occ_fock):
    r, c = lax.axis_index("row"), lax.axis_index("col")
    k = c % 2
    place = jnp.stack([r // 2, r % 2, c])
    n = integrals.shape[1]
    fock_twice = jnp.tile(occ_fock.T, (2, 2))

    own, to_right, mirrored = by_depth(
        own_pairs_kernel, [r.reshape(1)], [amplitudes], (256, 256, 192)
    )
    partner = lax.ppermute(own, "row", Y_SWAP)
    right = lax.ppermute(own, "row", x_shift(-1))
    left = lax.ppermute(to_right, "row", x_shift(1))
    fock = whole(fock_kernel, place, [fock_twice, slab], 128, n)
    panel = masked_tiles(integrals, cd_irreps, ab_irreps)

    partner, left, right = lax.optimization_barrier((partner, left, right))
    to_right, to_partner, to_far = by_depth(
        second_phase_kernel, [], [partner, left, mirrored], (192, 320, 64)
    )
    to_right, to_partner, to_far, partner, left, right, panel = lax.optimization_barrier(
        (to_right, to_partner, to_far, partner, left, right, panel)
    )
    right_partner = lax.ppermute(partner, "row", x_shift(-1))
    from_left = lax.ppermute(to_right, "row", x_shift(1))
    across = lax.ppermute(to_partner, "row", Y_SWAP)
    far = lax.ppermute(to_far, "row", x_shift(2))

    first = core_sum(*slot_sums(k, panel, FIRST, [own, partner, right, left], COST))
    mine, theirs = slot_sums(
        k, panel, SECOND, [right_partner, mirrored, from_left, across, far], COST
    )
    second = core_sum(mine, theirs)
    summed = send_to_slots(jnp.concatenate([first, second], axis=1))
    first, second = summed[:32], summed[32:]

    sent = whole(spread_kernel, place, [first, second, fock], 256, n).astype(jnp.float16)
    got = exchange(sent).astype(jnp.float32)
    return whole(update_kernel, place, [fock, got], 128, n)


def solution(mesh):
    return jax.shard_map(
        per_device,
        mesh=mesh,
        in_specs=(P("row", "col"), P("col", "row"), P("col"), P("row"), P("col", "row"), P()),
        out_specs=P("col", "row"),
        check_vma=False,
    )
```

time: 571 us -> 152 us (0.27)
  waiting for transfers between devices: 505 us -> 81.9 us
  starting transfers between devices: 0.04 us -> 21.2 us
  matrix products: 20.7 us -> 0 us
  Pallas kernels: 0 us -> 19.7 us
  between operations: 13.5 us -> 0.16 us
    all_gather x1 -> x0, waiting for transfers between devices: 330 us -> none  [per_device(): gathered = lax.all_gather(amplitudes, 'row', axis=0, tiled=True)]
    reduce_scatter x1 -> x0, waiting for transfers between devices: 174 us -> none  [per_device(): lax.psum_scatter(jnp.dot(gathered, panel_tiles, preferred_element_type=jn...]
    ppermute x0 -> x9, waiting for transfers between devices: none -> 43.4 us  [the longest x1 20.9 us: per_device(): far = lax.ppermute(to_far, 'row', x_shift(2))]
    all_to_all x0 -> x1, waiting for transfers between devices: none -> 38.4 us  [send_to_slots(): lax.all_to_all(parts, 'col', split_axis=0, concat_axis=0, axis_index_grou...]
    dot_general x2 -> x0, matrix products: 20.7 us -> none  [the longest x1 20.4 us: per_device(): jnp.dot(gathered, panel_tiles, preferred_element_type=jnp.float32)]
    pallas_call x0 -> x8, Pallas kernels: none -> 19.7 us  [the longest x2 9.9 us: slot_sums(): pl.pallas_call(functools.partial(slot_sums_kernel, layout), grid=(n // ti...]
    all_to_all x0 -> x1, starting transfers between devices: none -> 11.3 us  [send_to_slots(): lax.all_to_all(parts, 'col', split_axis=0, concat_axis=0, axis_index_grou...]
    ppermute x0 -> x9, starting transfers between devices: none -> 9.85 us  [the longest x1 3.23 us: per_device(): from_left = lax.ppermute(to_right, 'row', x_shift(1))]
  transfers between devices with their start and end apart: 2 -> 10, of which waited for: 2 -> 5; matrix products, arithmetic and copies ran while one was open for 1% -> 0% of each run, Pallas kernels for 0% -> 8%
where the time goes in v3:
time: 152 us
  waiting for transfers between devices  81.9 us (54%)
  blocking collectives  22.6 us (15%)
  starting transfers between devices  21.2 us (14%)
  Pallas kernels  19.7 us (13%)
  local copies, waits for them, and re-layouts  3.78 us (2%)
  other arithmetic  2.44 us (2%)
    all_to_all x1, waiting for transfers between devices, send_to_slots(): lax.all_to_all(parts, 'col', split_axis=0, concat_axis=0, axis_index_grou...  38.4 us
    all_to_all x1, blocking collectives, exchange(): return lax.all_to_all(rows, 'col', split_axis=0, concat_axis=0, tiled=True)  22.6 us
    ppermute x1, waiting for transfers between devices, per_device(): far = lax.ppermute(to_far, 'row', x_shift(2))  20.9 us
    ppermute x1, waiting for transfers between devices, per_device(): partner = lax.ppermute(own, 'row', Y_SWAP)  16.8 us
    all_to_all x1, starting transfers between devices, send_to_slots(): lax.all_to_all(parts, 'col', split_axis=0, concat_axis=0, axis_index_grou...  11.3 us
    pallas_call x2, Pallas kernels, slot_sums(): pl.pallas_call(functools.partial(slot_sums_kernel, layout), grid=(n // ti...  9.9 us
    pallas_call x3, Pallas kernels, whole(): pl.pallas_call(kernel, grid=(n // tile,), in_specs=[SCALARS] + [block(a.s...  4.42 us
    pallas_call x2, Pallas kernels, by_depth(): pl.pallas_call(kernel, grid=(depth // tile,), in_specs=[SCALARS] * len(sc...  3.78 us
  transfers between devices with their start and end apart: 10, of which 5 were waited for; matrix products, arithmetic and copies ran while one was open for 0% of the time, Pallas kernels for 8%

profile of v3, /device:TPU:6, one launch (start us, length us, event | category | flops | bytes accessed | tf_op | source)
XLA Modules:
  0.0 151.7 jit_solution(13340925048563180932)
XLA Ops:
  0.0 0.0 copy-start.3
  0.0 0.0 copy-start.4
  0.0 0.0 copy-start.1
  0.0 1.6 %copy-done.1 = bf16[512,2048]{1,0:T(8,128)(2,1)S(1)} copy-done((bf16[512,2048]{1,0:T(8,128)(2,1)S(1)}, bf16[512,2048]{1,0:T(8,128)(2,1)}, u32[]{:S(2)}) %copy-start.1) | copy-done | bytes 2097176
  1.6 3.2 %shard_map.65 = (bf16[256,2048]{1,0:T(8,128)(2,1)}, bf16[256,2048]{1,0:T(8,128)(2,1)}, bf16[192,2048]{1,0:T(8,128)(2,1)S(1)}) custom-call(s32[1]{0:T(128)} %bitcast.5.r_ref, bf16[512,2048]{1,0:T(8,128)(2,1)S(1)} %copy-done.1), custom_call_target="tpu_custom_call" | custom-call | tf_op jit(solution)/shard_map/pallas_call | solution.py:93
  4.8 1.6 %collective-permute-start = (bf16[256,2048]{1,0:T(8,128)(2,1)}, bf16[256,2048]{1,0:T(8,128)(2,1)S(1)}, u32[]{:S(2)}, u32[]{:S(2)}) collective-permute-start(bf16[256,2048]{1,0:T(8,128)(2,1)} %get-tuple-element.25.refs_0_), channel_id=1, source_target_pairs={{0,32},{32,0},{64,96},{96,64},{128,160},{160,128},{192,224},{224,1... | collective-permute-start | bytes 3145736 | tf_op jit(solution)/shard_map/ppermute | solution.py:264
  6.4 0.8 collective-permute-start.2
  7.2 2.4 %collective-permute-start.1 = (bf16[256,2048]{1,0:T(8,128)(2,1)}, bf16[256,2048]{1,0:T(8,128)(2,1)S(1)}, u32[]{:S(2)}, u32[]{:S(2)}) collective-permute-start(bf16[256,2048]{1,0:T(8,128)(2,1)} %get-tuple-element.26), channel_id=1, source_target_pairs={{0,64},{32,96},{64,128},{96,160},{128,192},{160,224},{192,0},{224,... | collective-permute-start | bytes 3145736 | tf_op jit(solution)/shard_map/ppermute | solution.py:266
  9.6 0.0 copy-done.3
  9.6 0.0 copy-done.4
  9.6 0.0 copy-start
  9.6 1.9 %copy-done = bf16[2048,768]{1,0:T(8,128)(2,1)S(1)} copy-done((bf16[2048,768]{1,0:T(8,128)(2,1)S(1)}, bf16[2048,768]{1,0:T(8,128)(2,1)}, u32[]{:S(2)}) %copy-start) | copy-done | bytes 3145752
  11.5 1.6 %shard_map.67.panel_ref = bf16[2048,768]{1,0:T(8,128)(2,1)S(1)} custom-call(s32[16]{0:T(128)S(1)} %copy-done.3, s32[6]{0:T(128)S(1)} %copy-done.4, bf16[2048,768]{1,0:T(8,128)(2,1)S(1)} %copy-done), custom_call_target="tpu_custom_call" | custom-call | bytes 6291456 | tf_op jit(solution)/shard_map/pallas_call | solution.py:58
  13.2 16.8 %collective-permute-done.partner_ref.refs_1_ = bf16[256,2048]{1,0:T(8,128)(2,1)S(1)} collective-permute-done((bf16[256,2048]{1,0:T(8,128)(2,1)}, bf16[256,2048]{1,0:T(8,128)(2,1)S(1)}, u32[]{:S(2)}, u32[]{:S(2)}) %collective-permute-start) | collective-permute-done | bytes 1048608 | tf_op jit(solution)/shard_map/ppermute | solution.py:264
  29.9 2.6 %collective-permute-done.2.refs_2_ = bf16[256,2048]{1,0:T(8,128)(2,1)} collective-permute-done((bf16[256,2048]{1,0:T(8,128)(2,1)}, bf16[256,2048]{1,0:T(8,128)(2,1)}, u32[]{:S(2)}, u32[]{:S(2)}) %collective-permute-start.2) | collective-permute-done | bytes 1048608 | tf_op jit(solution)/shard_map/ppermute | solution.py:265
  32.5 0.0 collective-permute-done.1.left_ref.refs_3_
  32.5 0.6 shard_map.66
  33.1 0.5 collective-permute-start.6
  33.7 0.0 collective-permute-start.4
  33.7 3.2 %collective-permute-start.5 = (bf16[192,2048]{1,0:T(8,128)(2,1)S(1)}, bf16[192,2048]{1,0:T(8,128)(2,1)S(1)}, u32[]{:S(2)}, u32[]{:S(2)}) collective-permute-start(bf16[192,2048]{1,0:T(8,128)(2,1)S(1)} %get-tuple-element.40), channel_id=1, source_target_pairs={{0,64},{32,96},{64,128},{96,160},{128,192},{160,224},{192,0},{224,... | collective-permute-start | bytes 2359304 | tf_op jit(solution)/shard_map/ppermute | solution.py:278
  36.9 1.1 collective-permute-start.7
  38.0 5.7 %shard_map.68 = (f32[16,32,768]{2,1,0:T(8,128)S(1)}, f32[16,32,768]{2,1,0:T(8,128)S(1)}) custom-call(s32[1]{0:T(128)} %bitcast.4.k_ref, bf16[2048,768]{1,0:T(8,128)(2,1)S(1)} %shard_map.67.panel_ref, bf16[256,2048]{1,0:T(8,128)(2,1)} %get-tuple-element.25.refs_0_, bf16[256,2048]{1,0:T(8,128)(2,1)S(1)} %collective-permute-done.partner_ref.refs_1_, ...), custom_call_target="tpu_custom_call" | custom-call | flops 40000000000 | tf_op jit(solution)/shard_map/pallas_call | solution.py:151
  43.7 0.1 collective-permute-start.3
  43.8 20.9 %collective-permute-done.7.refs_4_ = bf16[64,2048]{1,0:T(8,128)(2,1)S(1)} collective-permute-done((bf16[64,2048]{1,0:T(8,128)(2,1)S(1)}, bf16[64,2048]{1,0:T(8,128)(2,1)S(1)}, u32[]{:S(2)}, u32[]{:S(2)}) %collective-permute-start.7) | collective-permute-done | bytes 262176 | tf_op jit(solution)/shard_map/ppermute | solution.py:280
  64.7 0.0 collective-permute-done.5.refs_2_
  64.7 0.0 collective-permute-done.4.refs_0_
  64.7 0.0 collective-permute-done.6.refs_3_
  64.7 4.2 %shard_map.69 = (f32[16,32,768]{2,1,0:T(8,128)S(1)}, f32[16,32,768]{2,1,0:T(8,128)S(1)}) custom-call(s32[1]{0:T(128)} %bitcast.4.k_ref, bf16[2048,768]{1,0:T(8,128)(2,1)S(1)} %shard_map.67.panel_ref, bf16[256,2048]{1,0:T(8,128)(2,1)S(1)} %collective-permute-done.4.refs_0_, bf16[192,2048]{1,0:T(8,128)(2,1)S(1)} %get-tuple-element.29.mirrored_ref.refs_1_, ...), custom_call_target="tpu_custom_call" | custom-call | flops 40000000000 | tf_op jit(solution)/shard_map/pallas_call | solution.py:151
  68.9 0.1 collective-permute-start.8
  69.0 0.0 collective-permute-done.3
  69.1 0.3 multiply_convert_fusion.1
  69.3 3.1 %collective-permute-done.8 = f32[16,32,768]{2,1,0:T(8,128)S(1)} collective-permute-done((f32[16,32,768]{2,1,0:T(8,128)S(1)}, f32[16,32,768]{2,1,0:T(8,128)S(1)}, u32[]{:S(2)}, u32[]{:S(2)}) %collective-permute-start.8) | collective-permute-done | bytes 1572896 | tf_op jit(solution)/shard_map/ppermute | solution.py:164
  72.4 0.3 multiply_convert_fusion
  72.7 1.5 %pad_maximum_fusion = f16[16,64,768]{2,1,0:T(8,128)(2,1)} fusion(f16[16,32,768]{2,1,0:T(8,128)(2,1)S(1)} %multiply_convert_fusion, f16[16,32,768]{2,1,0:T(8,128)(2,1)S(1)} %multiply_convert_fusion.1), kind=kLoop, calls=%fused_computation.1 | loop fusion | flops 786432 | bytes 3145728 | tf_op jit(solution)/shard_map/concatenate | solution.py:287
  74.2 0.0 copy-start.5
  74.3 0.0 copy-start.2
  74.3 11.3 %all-to-all-start = ((f16[16,64,768]{2,1,0:T(8,128)(2,1)}), f16[16,64,768]{2,1,0:T(8,128)(2,1)S(1)}, u32[]{:S(2)}, u32[]{:S(2)}) async-start(f16[16,64,768]{2,1,0:T(8,128)(2,1)} %pad_maximum_fusion), calls=%async_computation | async-start | bytes 3145728 | tf_op jit(solution)/shard_map/all_to_all | solution.py:168
  85.6 0.0 copy-done.5
  85.6 0.1 copy.7
  85.7 0.1 tile.10.fock_ref
  85.9 0.1 pad_add_fusion._.at_ref
  85.9 0.0 copy-done.2
  86.0 1.0 shard_map.64.fock_ref
  87.0 38.4 %all-to-all-done = f16[16,64,768]{2,1,0:T(8,128)(2,1)S(1)} async-done(((f16[16,64,768]{2,1,0:T(8,128)(2,1)}), f16[16,64,768]{2,1,0:T(8,128)(2,1)S(1)}, u32[]{:S(2)}, u32[]{:S(2)}) %all-to-all-start) | async-done | bytes 1572896 | tf_op jit(solution)/shard_map/all_to_all | solution.py:168
  125.4 0.2 convert_reduce_fusion
  125.6 1.4 shard_map.70
  127.1 22.6 %all_to_all.14 = f16[32,8,768]{2,1,0:T(8,128)(2,1)S(1)} all-to-all(f16[32,8,768]{2,1,0:T(8,128)(2,1)S(1)} %convert_bitcast_fusion), channel_id=1, replica_groups=mesh['row'=8,'col'=32] {'col'}, dimensions={0} | all-to-all | bytes 786432 | tf_op jit(solution)/shard_map/all_to_all | solution.py:251
  149.7 0.1 bitcast_convert_fusion.got_ref
  149.7 2.0 %shard_map.71 = f32[128,768]{1,0:T(8,128)} custom-call(s32[3]{0:T(128)S(1)} %pad_add_fusion._.at_ref, f32[128,768]{1,0:T(8,128)S(1)} %shard_map.64.fock_ref, f32[256,768]{1,0:T(8,128)S(1)} %bitcast_convert_fusion.got_ref), custom_call_target="tpu_custom_call" | custom-call | bytes 1179648 | tf_op jit(solution)/shard_map/pallas_call | solution.py:188
  (3 shorter events, 0.1 us)
Async XLA Ops:
  0.0 9.6 %copy-start.3 = (s32[16]{0:T(128)S(1)}, s32[16]{0:T(128)}, u32[]{:S(2)}) copy-start(s32[16]{0:T(128)} %cd_ref.1) | copy-start | bytes 196
  0.0 9.6 %copy-start.4 = (s32[6]{0:T(128)S(1)}, s32[6]{0:T(128)}, u32[]{:S(2)}) copy-start(s32[6]{0:T(128)} %ab_ref.1) | copy-start | bytes 76
  0.0 1.6 %copy-start.1 = (bf16[512,2048]{1,0:T(8,128)(2,1)S(1)}, bf16[512,2048]{1,0:T(8,128)(2,1)}, u32[]{:S(2)}) copy-start(bf16[512,2048]{1,0:T(8,128)(2,1)} %amplitudes_ref.1) | copy-start | bytes 6291460
  4.8 25.1 %collective-permute-start = (bf16[256,2048]{1,0:T(8,128)(2,1)}, bf16[256,2048]{1,0:T(8,128)(2,1)S(1)}, u32[]{:S(2)}, u32[]{:S(2)}) collective-permute-start(bf16[256,2048]{1,0:T(8,128)(2,1)} %get-tuple-element.25.refs_0_), channel_id=1, source_target_pairs={{0,32},{32,0},{64,96},{96,64},{128,160},{160,128},{192,224},{224,1... | collective-permute-start | bytes 3145736 | tf_op jit(solution)/shard_map/ppermute | solution.py:264
  6.4 26.1 %collective-permute-start.2 = (bf16[256,2048]{1,0:T(8,128)(2,1)}, bf16[256,2048]{1,0:T(8,128)(2,1)}, u32[]{:S(2)}, u32[]{:S(2)}) collective-permute-start(bf16[256,2048]{1,0:T(8,128)(2,1)} %get-tuple-element.25.refs_0_), channel_id=1, source_target_pairs={{0,192},{32,224},{64,0},{96,32},{128,64},{160,96},{192,128},{224,1... | collective-permute-start | bytes 3145736 | tf_op jit(solution)/shard_map/ppermute | solution.py:265
  7.2 25.3 %collective-permute-start.1 = (bf16[256,2048]{1,0:T(8,128)(2,1)}, bf16[256,2048]{1,0:T(8,128)(2,1)S(1)}, u32[]{:S(2)}, u32[]{:S(2)}) collective-permute-start(bf16[256,2048]{1,0:T(8,128)(2,1)} %get-tuple-element.26), channel_id=1, source_target_pairs={{0,64},{32,96},{64,128},{96,160},{128,192},{160,224},{192,0},{224,... | collective-permute-start | bytes 3145736 | tf_op jit(solution)/shard_map/ppermute | solution.py:266
  9.6 1.9 %copy-start = (bf16[2048,768]{1,0:T(8,128)(2,1)S(1)}, bf16[2048,768]{1,0:T(8,128)(2,1)}, u32[]{:S(2)}) copy-start(bf16[2048,768]{1,0:T(8,128)(2,1)} %integrals_ref.1) | copy-start | bytes 9437188
  33.1 31.6 %collective-permute-start.6 = (bf16[320,2048]{1,0:T(8,128)(2,1)S(1)}, bf16[320,2048]{1,0:T(8,128)(2,1)S(1)}, u32[]{:S(2)}, u32[]{:S(2)}) collective-permute-start(bf16[320,2048]{1,0:T(8,128)(2,1)S(1)} %get-tuple-element.41), channel_id=1, source_target_pairs={{0,32},{32,0},{64,96},{96,64},{128,160},{160,128},{192,224},{224,1... | collective-permute-start | bytes 3932168 | tf_op jit(solution)/shard_map/ppermute | solution.py:279
  33.7 31.0 %collective-permute-start.4 = (bf16[256,2048]{1,0:T(8,128)(2,1)S(1)}, bf16[256,2048]{1,0:T(8,128)(2,1)S(1)}, u32[]{:S(2)}, u32[]{:S(2)}) collective-permute-start(bf16[256,2048]{1,0:T(8,128)(2,1)S(1)} %collective-permute-done.partner_ref.refs_1_), channel_id=1, source_target_pairs={{0,192},{32,224},{64,0},{96,32},{128,64},{160,96},{192,128},{224,1... | collective-permute-start | bytes 3145736 | tf_op jit(solution)/shard_map/ppermute | solution.py:277
  33.7 31.0 %collective-permute-start.5 = (bf16[192,2048]{1,0:T(8,128)(2,1)S(1)}, bf16[192,2048]{1,0:T(8,128)(2,1)S(1)}, u32[]{:S(2)}, u32[]{:S(2)}) collective-permute-start(bf16[192,2048]{1,0:T(8,128)(2,1)S(1)} %get-tuple-element.40), channel_id=1, source_target_pairs={{0,64},{32,96},{64,128},{96,160},{128,192},{160,224},{192,0},{224,... | collective-permute-start | bytes 2359304 | tf_op jit(solution)/shard_map/ppermute | solution.py:278
  36.9 27.8 %collective-permute-start.7 = (bf16[64,2048]{1,0:T(8,128)(2,1)S(1)}, bf16[64,2048]{1,0:T(8,128)(2,1)S(1)}, u32[]{:S(2)}, u32[]{:S(2)}) collective-permute-start(bf16[64,2048]{1,0:T(8,128)(2,1)S(1)} %get-tuple-element.42), channel_id=1, source_target_pairs={{0,128},{32,160},{64,192},{96,224},{128,0},{160,32},{192,64},{224,... | collective-permute-start | bytes 786440 | tf_op jit(solution)/shard_map/ppermute | solution.py:280
  43.7 25.4 %collective-permute-start.3 = (f32[16,32,768]{2,1,0:T(8,128)S(1)}, f32[16,32,768]{2,1,0:T(8,128)S(1)}, u32[]{:S(2)}, u32[]{:S(2)}) collective-permute-start(f32[16,32,768]{2,1,0:T(8,128)S(1)} %get-tuple-element.39), channel_id=1, source_target_pairs={{0,1},{1,0},{2,3},{3,2},{4,5},{5,4},{6,7},{7,6},{8,9},{9,8},{10,11... | collective-permute-start | bytes 4718600 | tf_op jit(solution)/shard_map/ppermute | solution.py:164
  68.9 3.5 %collective-permute-start.8 = (f32[16,32,768]{2,1,0:T(8,128)S(1)}, f32[16,32,768]{2,1,0:T(8,128)S(1)}, u32[]{:S(2)}, u32[]{:S(2)}) collective-permute-start(f32[16,32,768]{2,1,0:T(8,128)S(1)} %get-tuple-element.44), channel_id=1, source_target_pairs={{0,1},{1,0},{2,3},{3,2},{4,5},{5,4},{6,7},{7,6},{8,9},{9,8},{10,11... | collective-permute-start | bytes 4718600 | tf_op jit(solution)/shard_map/ppermute | solution.py:164
  74.2 11.4 %copy-start.5 = (f32[64,64]{1,0:T(8,128)S(1)}, f32[64,64]{1,0:T(8,128)}, u32[]{:S(2)}) copy-start(f32[64,64]{1,0:T(8,128)} %param.11) | copy-start | bytes 49156
  74.3 11.7 %copy-start.2 = (bf16[128,768]{1,0:T(8,128)(2,1)S(1)}, bf16[128,768]{1,0:T(8,128)(2,1)}, u32[]{:S(2)}) copy-start(bf16[128,768]{1,0:T(8,128)(2,1)} %slab_ref.1) | copy-start | bytes 589828
  74.3 51.1 %all-to-all-start = ((f16[16,64,768]{2,1,0:T(8,128)(2,1)}), f16[16,64,768]{2,1,0:T(8,128)(2,1)S(1)}, u32[]{:S(2)}, u32[]{:S(2)}) async-start(f16[16,64,768]{2,1,0:T(8,128)(2,1)} %pad_maximum_fusion), calls=%async_computation | async-start | bytes 3145728 | tf_op jit(solution)/shard_map/all_to_all | solution.py:168

commit v4 on v3

--- a/solution.py
+++ b/solution.py
@@ -21,6 +21,8 @@
 
 Y_SWAP = [(r, r ^ 1) for r in range(X * LO)]
 CORE_SWAP = [(c, c ^ 1) for c in range(COLS)]
+H_SWAP = [(c, c ^ 16) for c in range(COLS)]
+Z_GROUPS = [[16 * h + 2 * z + k for z in range(Z)] for h in range(HI) for k in range(CORES)]
 HZ_GROUPS = [[2 * hz + k for hz in range(HI * Z)] for k in range(CORES)]
 
 
@@ -30,6 +32,10 @@
     opposite = (((group + 2) & 3) << 4) + ((half ^ (group >> 1)) << 3) + ((i + t) & 7)
     same = (group << 4) + ((i + t - 23) & 15)
     return jnp.where(t < 16, following, jnp.where(t < 24, opposite, same))
+
+
+def slot_of(c):
+    return ((c & 1) << 4) + (c >> 1)
 
 
 def grid(rows, columns):
@@ -66,27 +72,30 @@
     )(cd_irreps, ab_irreps, integrals)
 
 
-def own_pairs_kernel(r_ref, amplitudes_ref, own_ref, right_ref, mirrored_ref):
-    r = r_ref[0]
-    x, l = r >> 1, r & 1
-    to, held = grid(448, 512)
-    rho, j = to & 7, (r << 3) + (to & 7)
-    t = to >> 3
-    direct = (rho << 6) + partner_of(j, t)
-    before = (((x + 3) & 3) << 4) + ((j - t) & 15)
-    opposite = (x + 2) & 3
-    across = (opposite << 4) + ((l ^ (opposite >> 1)) << 3) + ((j - t) & 7)
-    wanted = jnp.where(to < 256, direct, (rho << 6) + jnp.where(to < 384, before, across))
-    sign = jnp.where(to < 256, 1.0, -1.0)
-    pick = jnp.where(wanted == held, sign, 0.0).astype(jnp.bfloat16)
-    rows = jnp.dot(pick, amplitudes_ref[...], preferred_element_type=jnp.float32)
+def own_pairs_kernel(r_ref, amplitudes_ref, own_ref, right_ref, mirrored_ref, pick_ref):
+    @pl.when(pl.program_id(0) == 0)
+    def _():
+        r = r_ref[0]
+        x, l = r >> 1, r & 1
+        to, held = grid(448, 512)
+        rho, j = to & 7, (r << 3) + (to & 7)
+        t = to >> 3
+        direct = (rho << 6) + partner_of(j, t)
+        before = (((x + 3) & 3) << 4) + ((j - t) & 15)
+        opposite = (x + 2) & 3
+        across = (opposite << 4) + ((l ^ (opposite >> 1)) << 3) + ((j - t) & 7)
+        wanted = jnp.where(to < 256, direct, (rho << 6) + jnp.where(to < 384, before, across))
+        sign = jnp.where(to < 256, 1.0, -1.0)
+        pick_ref[...] = jnp.where(wanted == held, sign, 0.0).astype(jnp.bfloat16)
+
+    rows = jnp.dot(pick_ref[...], amplitudes_ref[...], preferred_element_type=jnp.float32)
     rows = rows.astype(jnp.bfloat16)
     own_ref[...] = rows[:256]
     right_ref[...] = rows[128:384]
     mirrored_ref[...] = rows[256:]
 
 
-def by_depth(kernel, scalars, arrays, out_rows, flops=0):
+def by_depth(kernel, scalars, arrays, out_rows, flops=0, scratch=()):
     depth = arrays[0].shape[1]
     tile = min(depth, 512)
     outs = [jax.ShapeDtypeStruct((rows, depth), jnp.bfloat16) for rows in out_rows]
@@ -97,17 +106,56 @@
         + [pl.BlockSpec((a.shape[0], tile), lambda j: (0, j)) for a in arrays],
         out_specs=[pl.BlockSpec((rows, tile), lambda j: (0, j)) for rows in out_rows],
         out_shape=outs,
+        scratch_shapes=scratch,
         compiler_params=pltpu.CompilerParams(vmem_limit_bytes=32 * 2**20),
         cost_estimate=pl.CostEstimate(flops=flops, bytes_accessed=0, transcendentals=0),
     )(*scalars, *arrays)
 
 
-def second_phase_kernel(partner_ref, left_ref, mirrored_ref, right_out, across_out, far_out):
+def second_phase_kernel(
+    k_ref, own_ref, partner_ref, right_ref, left_ref, mirrored_ref, right_out, across_out, far_out, core_out
+):
     right_out[:128] = partner_ref[128:]
     right_out[128:] = left_ref[64:128]
     across_out[:192] = mirrored_ref[...]
     across_out[192:] = left_ref[128:]
     far_out[...] = partner_ref[192:]
+    core_out[...] = core_rows(1 - k_ref[0], own_ref, partner_ref, right_ref, left_ref)
+
+
+def core_rows(k, own_ref, partner_ref, right_ref, left_ref):
+    at, at_left = pl.multiple_of(128 * k, 128), pl.multiple_of(128 * (1 - k), 128)
+    return jnp.concatenate(
+        [ref[pl.ds(at, 128), :] for ref in (own_ref, partner_ref, right_ref)]
+        + [left_ref[pl.ds(at_left, 128), :]]
+    )
+
+
+def first_sums_kernel(
+    k_ref, panel_ref, other_panel_ref, own_ref, partner_ref, right_ref, left_ref, got_ref, out_ref
+):
+    rows = core_rows(k_ref[0], own_ref, partner_ref, right_ref, left_ref)
+    sums = jnp.dot(rows, panel_ref[...], preferred_element_type=jnp.float32)
+    sums += jnp.dot(got_ref[...], other_panel_ref[...], preferred_element_type=jnp.float32)
+    for s in range(4):
+        source = sums[128 * s : 128 * s + 128].reshape(HI, Z, 8, sums.shape[1])
+        for h in range(HI):
+            out_ref[:, 32 * h + 8 * s : 32 * h + 8 * s + 8, :] = source[h]
+
+
+def first_sums(k, panel, other_panel, arrays):
+    depth, n = panel.shape
+    tile = min(n, 256)
+    column = pl.BlockSpec((depth, tile), lambda j: (0, j))
+    return pl.pallas_call(
+        first_sums_kernel,
+        grid=(n // tile,),
+        in_specs=[SCALARS, column, column] + [pl.BlockSpec(a.shape, lambda j: (0, 0)) for a in arrays],
+        out_specs=pl.BlockSpec((Z, HI * 32, tile), lambda j: (0, 0, j)),
+        out_shape=jax.ShapeDtypeStruct((Z, HI * 32, n), jnp.float32),
+        compiler_params=pltpu.CompilerParams(vmem_limit_bytes=48 * 2**20),
+        cost_estimate=pl.CostEstimate(flops=COST, bytes_accessed=0, transcendentals=0),
+    )(k.reshape(1), panel, other_panel, *arrays)
 
 
 OWN, MIRROR = 0, 1
@@ -121,7 +169,6 @@
     ((MIRROR, 0, 1), (MIRROR, 0, 1), (OWN, 2, 1)),
     ((MIRROR, 3, 1), (OWN, 3, 1), (OWN, 3, 1)),
 )
-FIRST = (((0, 0, 256),), ((1, 0, 256),), ((2, 0, 256),), ((3, 128, 256), (3, 0, 128)))
 SECOND = (
     ((0, 0, 256),),
     ((1, 0, 192), (2, 128, 192)),
@@ -137,10 +184,10 @@
         rows = [arrays[at][start:end, :] for at, start, end in pieces]
         rows = rows[0] if len(rows) == 1 else jnp.concatenate(rows)
         sums = jnp.dot(rows, panel_ref[...], preferred_element_type=jnp.float32)
-        sums = sums.reshape(HI * Z, CORES, 8, columns)
+        sums = sums.reshape(CORES, HI * Z, 8, columns)
         first = k_ref[0] == 0
-        mine_ref[:, 8 * s : 8 * s + 8, :] = jnp.where(first, sums[:, 0], sums[:, 1])
-        theirs_ref[:, 8 * s : 8 * s + 8, :] = jnp.where(first, sums[:, 1], sums[:, 0])
+        mine_ref[:, 8 * s : 8 * s + 8, :] = jnp.where(first, sums[0], sums[1])
+        theirs_ref[:, 8 * s : 8 * s + 8, :] = jnp.where(first, sums[1], sums[0])
 
 
 def slot_sums(k, panel, layout, arrays, flops):
@@ -169,6 +216,13 @@
         parts, "col", split_axis=0, concat_axis=0, axis_index_groups=HZ_GROUPS, tiled=True
     )
     return got.astype(jnp.float32).sum(0)
+
+
+def send_to_z(parts):
+    got = lax.all_to_all(
+        parts, "col", split_axis=0, concat_axis=0, axis_index_groups=Z_GROUPS, tiled=True
+    )
+    return got.astype(jnp.float32).sum(0).reshape(HI, -1, parts.shape[2])
 
 
 def exact_dot(a, b):
@@ -208,7 +262,7 @@
 
 
 def spread_kernel(at_ref, first_ref, second_ref, fock_ref, out_ref):
-    x, l, c = at_ref[0], at_ref[1], at_ref[2]
+    x, l, c = at_ref[0], at_ref[1], slot_of(at_ref[2])
     to, at = grid(256, 64)
     source, rho = at >> 3, at & 7
     i = jnp.zeros_like(at)
@@ -239,11 +293,12 @@
 def update_kernel(at_ref, fock_ref, got_ref, out_ref):
     ej, at = grid(128, 256)
     e, j = ej >> 6, ej & 63
-    i, t, mine = 2 * at_ref[2] + e, at >> 3, (at & 1) == e
+    i, peer, mine = 2 * at_ref[2] + e, at >> 3, (at & 1) == e
+    t = slot_of(peer)
     weight = jnp.where(t == 31, 1 / LADDER_SCALE, 2 / LADDER_SCALE)
     forward = jnp.where(mine & ((at & 6) == 0) & (partner_of(i, t) == j), weight, 0.0)
     backward = jnp.where(mine & ((at & 6) == 2) & (partner_of(j, t) == i), weight, 0.0)
-    mirror = jnp.where(mine & ((at & 4) != 0) & ((t << 1) + ((at >> 1) & 1) == j), 1 / FOCK_SCALE, 0.0)
+    mirror = jnp.where(mine & ((at & 4) != 0) & ((peer << 1) + ((at >> 1) & 1) == j), 1 / FOCK_SCALE, 0.0)
     out_ref[...] = fock_ref[...] + exact_dot(forward - backward - mirror, got_ref[...])
 
 
@@ -259,33 +314,47 @@
     fock_twice = jnp.tile(occ_fock.T, (2, 2))
 
     own, to_right, mirrored = by_depth(
-        own_pairs_kernel, [r.reshape(1)], [amplitudes], (256, 256, 192)
+        own_pairs_kernel,
+        [r.reshape(1)],
+        [amplitudes],
+        (256, 256, 192),
+        scratch=[pltpu.VMEM((448, 512), jnp.bfloat16)],
     )
     partner = lax.ppermute(own, "row", Y_SWAP)
     right = lax.ppermute(own, "row", x_shift(-1))
     left = lax.ppermute(to_right, "row", x_shift(1))
     fock = whole(fock_kernel, place, [fock_twice, slab], 128, n)
+    integrals, _ = lax.optimization_barrier((integrals, own))
     panel = masked_tiles(integrals, cd_irreps, ab_irreps)
-
-    partner, left, right = lax.optimization_barrier((partner, left, right))
-    to_right, to_partner, to_far = by_depth(
-        second_phase_kernel, [], [partner, left, mirrored], (192, 320, 64)
-    )
-    to_right, to_partner, to_far, partner, left, right, panel = lax.optimization_barrier(
-        (to_right, to_partner, to_far, partner, left, right, panel)
-    )
+    other_panel = lax.ppermute(panel, "col", CORE_SWAP)
+
+    partner, left, right, panel = lax.optimization_barrier((partner, left, right, panel))
+    to_right, to_partner, to_far, to_core = by_depth(
+        second_phase_kernel,
+        [k.reshape(1)],
+        [own, partner, right, left, mirrored],
+        (192, 320, 64, 512),
+    )
+    to_right, to_partner, to_far, to_core, partner, left, right, panel = lax.optimization_barrier(
+        (to_right, to_partner, to_far, to_core, partner, left, right, panel)
+    )
+    from_core = lax.ppermute(to_core, "col", CORE_SWAP)
     right_partner = lax.ppermute(partner, "row", x_shift(-1))
     from_left = lax.ppermute(to_right, "row", x_shift(1))
     across = lax.ppermute(to_partner, "row", Y_SWAP)
     far = lax.ppermute(to_far, "row", x_shift(2))
 
-    first = core_sum(*slot_sums(k, panel, FIRST, [own, partner, right, left], COST))
+    first = first_sums(k, panel, other_panel, [own, partner, right, left, from_core])
+    first = send_to_z((first * SCALE).astype(jnp.float16))
     mine, theirs = slot_sums(
         k, panel, SECOND, [right_partner, mirrored, from_left, across, far], COST
     )
-    second = core_sum(mine, theirs)
-    summed = send_to_slots(jnp.concatenate([first, second], axis=1))
-    first, second = summed[:32], summed[32:]
+    theirs, first = lax.optimization_barrier((theirs, first))
+    h = c // 16
+    kept = lax.dynamic_index_in_dim(first, h, 0, keepdims=False)
+    other = lax.dynamic_index_in_dim(first, 1 - h, 0, keepdims=False)
+    first = kept + lax.ppermute(other, "col", H_SWAP)
+    second = send_to_slots(core_sum(mine, theirs))
 
     sent = whole(spread_kernel, place, [first, second, fock], 256, n).astype(jnp.float16)
     got = exchange(sent).astype(jnp.float32)

time: 152 us -> 150 us (0.987)
  waiting for transfers between devices: 81.9 us -> 55.2 us
  starting transfers between devices: 21.2 us -> 31.2 us
  Pallas kernels: 19.7 us -> 27.4 us
  local copies, waits for them, and re-layouts: 3.78 us -> 8.37 us
  other arithmetic: 2.44 us -> 5.15 us
    all_to_all x1, waiting for transfers between devices: 38.4 us -> 15 us  [send_to_slots(): lax.all_to_all(parts, 'col', split_axis=0, concat_axis=0, axis_index_grou...]
    ppermute x1, waiting for transfers between devices: 20.9 us -> 11.1 us  [per_device(): far = lax.ppermute(to_far, 'row', x_shift(2))]
    all_to_all x0 -> x1, starting transfers between devices: none -> 8.6 us  [send_to_z(): lax.all_to_all(parts, 'col', split_axis=0, concat_axis=0, axis_index_grou...]
    pallas_call x0 -> x1, Pallas kernels: none -> 7.69 us  [first_sums(): pl.pallas_call(first_sums_kernel, grid=(n // tile,), in_specs=[SCALARS, c...]
    unnamed x12 -> x28, local copies, waits for them, and re-layouts: 3.52 us -> 8.11 us
    ppermute x0 -> x3, starting transfers between devices: none -> 3.81 us  [the longest x1 3.66 us: per_device(): first = kept + lax.ppermute(other, 'col', H_SWAP)]
    pallas_call x2 -> x1, Pallas kernels: 9.9 us -> 6.11 us  [slot_sums(): pl.pallas_call(functools.partial(slot_sums_kernel, layout), grid=(n // ti...]
    pallas_call x2, Pallas kernels: 3.78 us -> 7.48 us  [by_depth(): pl.pallas_call(kernel, grid=(depth // tile,), in_specs=[SCALARS] * len(sc...]
  transfers between devices with their start and end apart: 10 -> 13, of which waited for: 5 -> 8; matrix products, arithmetic and copies ran while one was open for 0% -> 1% of each run, Pallas kernels for 8% -> 14%
where the time goes in v4:
time: 150 us; the launch traced here: 149 us
  waiting for transfers between devices  55.2 us (37%)
  starting transfers between devices  31.2 us (21%)
  Pallas kernels  27.4 us (18%)
  blocking collectives  21.9 us (15%)
  local copies, waits for them, and re-layouts  8.37 us (6%)
  other arithmetic  5.15 us (3%)
    all_to_all x1, blocking collectives, exchange(): return lax.all_to_all(rows, 'col', split_axis=0, concat_axis=0, tiled=True)  21.9 us
    ppermute x1, waiting for transfers between devices, per_device(): partner = lax.ppermute(own, 'row', Y_SWAP)  16.7 us
    all_to_all x1, waiting for transfers between devices, send_to_slots(): lax.all_to_all(parts, 'col', split_axis=0, concat_axis=0, axis_index_grou...  15 us
    ppermute x1, waiting for transfers between devices, per_device(): far = lax.ppermute(to_far, 'row', x_shift(2))  11.1 us
    all_to_all x1, starting transfers between devices, send_to_slots(): lax.all_to_all(parts, 'col', split_axis=0, concat_axis=0, axis_index_grou...  8.6 us
    all_to_all x1, starting transfers between devices, send_to_z(): lax.all_to_all(parts, 'col', split_axis=0, concat_axis=0, axis_index_grou...  8.6 us
    unnamed x28, local copies, waits for them, and re-layouts  8.11 us
    pallas_call x1, Pallas kernels, first_sums(): pl.pallas_call(first_sums_kernel, grid=(n // tile,), in_specs=[SCALARS, c...  7.69 us
  transfers between devices with their start and end apart: 13, of which 8 were waited for; matrix products, arithmetic and copies ran while one was open for 1% of the time, Pallas kernels for 14%

profile of v4, /device:TPU:6, one launch (start us, length us, event | category | flops | bytes accessed | tf_op | source)
XLA Modules:
  0.0 149.4 jit_solution(2910876500928069129)
XLA Ops:
  0.0 0.0 copy-start.9
  0.0 0.0 copy-start.10
  0.0 0.0 copy-start.3
  0.0 1.6 %copy-done.3 = bf16[512,2048]{1,0:T(8,128)(2,1)S(1)} copy-done((bf16[512,2048]{1,0:T(8,128)(2,1)S(1)}, bf16[512,2048]{1,0:T(8,128)(2,1)}, u32[]{:S(2)}) %copy-start.3) | copy-done | bytes 2097176
  1.6 3.2 %shard_map.65 = (bf16[256,2048]{1,0:T(8,128)(2,1)}, bf16[256,2048]{1,0:T(8,128)(2,1)}, bf16[192,2048]{1,0:T(8,128)(2,1)S(1)}) custom-call(s32[1]{0:T(128)} %bitcast.5.r_ref, bf16[512,2048]{1,0:T(8,128)(2,1)S(1)} %copy-done.3), custom_call_target="tpu_custom_call" | custom-call | tf_op jit(solution)/shard_map/pallas_call | solution.py:102
  4.8 1.6 %collective-permute-start = (bf16[256,2048]{1,0:T(8,128)(2,1)}, bf16[256,2048]{1,0:T(8,128)(2,1)}, u32[]{:S(2)}, u32[]{:S(2)}) collective-permute-start(bf16[256,2048]{1,0:T(8,128)(2,1)} %get-tuple-element.29.own_ref), channel_id=1, source_target_pairs={{0,32},{32,0},{64,96},{96,64},{128,160},{160,128},{192,224},{224,1... | collective-permute-start | bytes 3145736 | tf_op jit(solution)/shard_map/ppermute | solution.py:323
  6.4 0.8 collective-permute-start.2
  7.2 2.4 %collective-permute-start.1 = (bf16[256,2048]{1,0:T(8,128)(2,1)}, bf16[256,2048]{1,0:T(8,128)(2,1)}, u32[]{:S(2)}, u32[]{:S(2)}) collective-permute-start(bf16[256,2048]{1,0:T(8,128)(2,1)} %get-tuple-element.30), channel_id=1, source_target_pairs={{0,64},{32,96},{64,128},{96,160},{128,192},{160,224},{192,0},{224,... | collective-permute-start | bytes 3145736 | tf_op jit(solution)/shard_map/ppermute | solution.py:325
  9.6 0.0 copy-done.9
  9.6 0.0 copy-done.10
  9.6 1.9 %copy-done = bf16[2048,768]{1,0:T(8,128)(2,1)S(1)} copy-done((bf16[2048,768]{1,0:T(8,128)(2,1)S(1)}, bf16[2048,768]{1,0:T(8,128)(2,1)}, u32[]{:S(2)}) %copy-start) | copy-done | bytes 3145752
  11.5 1.6 %shard_map.66.panel_ref = bf16[2048,768]{1,0:T(8,128)(2,1)S(1)} custom-call(s32[16]{0:T(128)S(1)} %copy-done.9, s32[6]{0:T(128)S(1)} %copy-done.10, bf16[2048,768]{1,0:T(8,128)(2,1)S(1)} %copy-done), custom_call_target="tpu_custom_call" | custom-call | bytes 6291456 | tf_op jit(solution)/shard_map/pallas_call | solution.py:64
  13.2 0.0 copy-done.5
  13.2 0.0 copy-start.1
  13.2 0.1 collective-permute-start.7
  13.3 16.7 %collective-permute-done.partner_ref = bf16[256,2048]{1,0:T(8,128)(2,1)} collective-permute-done((bf16[256,2048]{1,0:T(8,128)(2,1)}, bf16[256,2048]{1,0:T(8,128)(2,1)}, u32[]{:S(2)}, u32[]{:S(2)}) %collective-permute-start) | collective-permute-done | bytes 1048608 | tf_op jit(solution)/shard_map/ppermute | solution.py:323
  30.0 2.5 %collective-permute-done.2.right_ref = bf16[256,2048]{1,0:T(8,128)(2,1)} collective-permute-done((bf16[256,2048]{1,0:T(8,128)(2,1)}, bf16[256,2048]{1,0:T(8,128)(2,1)}, u32[]{:S(2)}, u32[]{:S(2)}) %collective-permute-start.2) | collective-permute-done | bytes 1048608 | tf_op jit(solution)/shard_map/ppermute | solution.py:324
  32.5 0.0 collective-permute-done.1.left_ref
  32.5 1.1 copy-done.6
  33.7 4.3 %shard_map.67 = (bf16[192,2048]{1,0:T(8,128)(2,1)}, bf16[320,2048]{1,0:T(8,128)(2,1)}, bf16[64,2048]{1,0:T(8,128)(2,1)S(1)}, bf16[512,2048]{1,0:T(8,128)(2,1)S(1)}) custom-call(s32[1]{0:T(128)} %bitcast.4.k_ref, bf16[256,2048]{1,0:T(8,128)(2,1)} %get-tuple-element.29.own_ref, bf16[256,2048]{1,0:T(8,128)(2,1)} %collective-permute-done.partner_ref, ...), custom_call_target="tpu_custom_call" | custom-call | tf_op jit(solution)/shard_map/pallas_call | solution.py:102
  38.0 0.0 copy-done.1
  38.0 0.1 collective-permute-start.8
  38.0 0.5 collective-permute-start.5
  38.6 0.0 collective-permute-start.3
  38.6 3.2 %collective-permute-start.4 = (bf16[192,2048]{1,0:T(8,128)(2,1)}, bf16[192,2048]{1,0:T(8,128)(2,1)}, u32[]{:S(2)}, u32[]{:S(2)}) collective-permute-start(bf16[192,2048]{1,0:T(8,128)(2,1)} %get-tuple-element.43), channel_id=1, source_target_pairs={{0,64},{32,96},{64,128},{96,160},{128,192},{160,224},{192,0},{224,... | collective-permute-start | bytes 2359304 | tf_op jit(solution)/shard_map/ppermute | solution.py:343
  41.8 0.4 collective-permute-done.8.got_ref
  42.2 1.5 collective-permute-start.6
  43.6 0.0 collective-permute-done.7.other_panel_ref
  43.7 0.0 copy-done.13
  43.7 7.7 %shard_map.69 = f32[8,64,768]{2,1,0:T(8,128)S(1)} custom-call(s32[1]{0:T(128)} %bitcast.4.k_ref, bf16[2048,768]{1,0:T(8,128)(2,1)} %copy-done.1, bf16[2048,768]{1,0:T(8,128)(2,1)} %collective-permute-done.7.other_panel_ref, bf16[256,2048]{1,0:T(8,128)(2,1)} %get-tuple-element.29.own_ref, bf16[256,2048]{1,0:T(8,128)(2,1)} %collective-permute-done.partner_ref, ...), custom_call_target="tpu_custom_call" | custom-call | flops 40000000000 | tf_op jit(solution)/shard_map/pallas_call | solution.py:150
  51.4 0.0 copy-start.2
  51.4 1.0 multiply_convert_fusion.1
  52.4 8.6 %all-to-all-start = ((f16[8,64,768]{2,1,0:T(8,128)(2,1)}), f16[8,64,768]{2,1,0:T(8,128)(2,1)}, u32[]{:S(2)}, u32[]{:S(2)}) async-start(f16[8,64,768]{2,1,0:T(8,128)(2,1)} %multiply_convert_fusion.1), calls=%async_computation | async-start | bytes 1572864 | tf_op jit(solution)/shard_map/all_to_all | solution.py:222
  61.0 11.1 %collective-permute-done.6.refs_4_ = bf16[64,2048]{1,0:T(8,128)(2,1)} collective-permute-done((bf16[64,2048]{1,0:T(8,128)(2,1)S(1)}, bf16[64,2048]{1,0:T(8,128)(2,1)}, u32[]{:S(2)}, u32[]{:S(2)}) %collective-permute-start.6) | collective-permute-done | bytes 262176 | tf_op jit(solution)/shard_map/ppermute | solution.py:345
  72.1 0.0 collective-permute-done.4.refs_2_
  72.1 0.0 collective-permute-done.3.refs_0_
  72.1 0.0 collective-permute-done.5.refs_3_
  72.1 0.0 copy-done.2
  72.1 0.0 copy-start.7
  72.1 1.1 copy-done.7
  73.3 6.1 %shard_map.68 = (f32[16,32,768]{2,1,0:T(8,128)S(1)}, f32[16,32,768]{2,1,0:T(8,128)S(1)}) custom-call(s32[1]{0:T(128)} %bitcast.4.k_ref, bf16[2048,768]{1,0:T(8,128)(2,1)S(1)} %copy-done.2, bf16[256,2048]{1,0:T(8,128)(2,1)} %collective-permute-done.3.refs_0_, bf16[192,2048]{1,0:T(8,128)(2,1)S(1)} %copy-done.7, ...), custom_call_target="tpu_custom_call" | custom-call | flops 40000000000 | tf_op jit(solution)/shard_map/pallas_call | solution.py:198
  79.4 0.0 copy-start.4
  79.4 1.2 copy-done.4
  80.6 1.1 copy-done.11
  81.7 2.7 %all-to-all-done = f16[8,64,768]{2,1,0:T(8,128)(2,1)} async-done(((f16[8,64,768]{2,1,0:T(8,128)(2,1)}), f16[8,64,768]{2,1,0:T(8,128)(2,1)}, u32[]{:S(2)}, u32[]{:S(2)}) %all-to-all-start) | async-done | bytes 786464 | tf_op jit(solution)/shard_map/all_to_all | solution.py:222
  84.4 1.3 convert_reduce_fusion.1
  85.7 0.1 collective-permute-start.10
  85.8 3.6 %collective-permute-done.10 = f32[16,32,768]{2,1,0:T(8,128)S(1)} collective-permute-done((f32[16,32,768]{2,1,0:T(8,128)}, f32[16,32,768]{2,1,0:T(8,128)S(1)}, u32[]{:S(2)}, u32[]{:S(2)}) %collective-permute-start.10) | collective-permute-done | bytes 1572896 | tf_op jit(solution)/shard_map/ppermute | solution.py:211
  89.4 2.6 %multiply_convert_fusion = f16[16,32,768]{2,1,0:T(8,128)(2,1)} fusion(f32[16,32,768]{2,1,0:T(8,128)} %copy-done.4, f32[16,32,768]{2,1,0:T(8,128)S(1)} %collective-permute-done.10), kind=kLoop, calls=%fused_computation.1 | loop fusion | flops 1179648 | bytes 3932160 | tf_op jit(solution)/shard_map/convert_element_type | solution.py:211
  92.0 8.6 %all-to-all-start.1 = ((f16[16,32,768]{2,1,0:T(8,128)(2,1)}), f16[16,32,768]{2,1,0:T(8,128)(2,1)S(1)}, u32[]{:S(2)}, u32[]{:S(2)}) async-start(f16[16,32,768]{2,1,0:T(8,128)(2,1)} %multiply_convert_fusion), calls=%async_computation.1 | async-start | bytes 1572864 | tf_op jit(solution)/shard_map/all_to_all | solution.py:215
  100.6 0.0 copy-done.12
  100.6 0.1 copy.7
  100.7 0.1 tile.10.fock_ref
  100.9 3.7 %collective-permute-start.9 = (f32[32,768]{1,0:T(8,128)S(1)}, f32[32,768]{1,0:T(8,128)S(1)}, u32[]{:S(2)}, u32[]{:S(2)}) collective-permute-start(f32[32,768]{1,0:T(8,128)S(1)} %dynamic-slice_bitcast_fusion), channel_id=1, source_target_pairs={{0,16},{1,17},{2,18},{3,19},{4,20},{5,21},{6,22},{7,23},{8,24},{9,... | collective-permute-start | bytes 294920 | tf_op jit(solution)/shard_map/ppermute | solution.py:356
  104.6 0.1 pad_add_fusion._.at_ref
  104.6 0.0 copy-done.8
  104.6 1.0 shard_map.64.fock_ref
  105.6 3.2 %collective-permute-done.9 = f32[32,768]{1,0:T(8,128)S(1)} collective-permute-done((f32[32,768]{1,0:T(8,128)S(1)}, f32[32,768]{1,0:T(8,128)S(1)}, u32[]{:S(2)}, u32[]{:S(2)}) %collective-permute-start.9) | collective-permute-done | bytes 98336 | tf_op jit(solution)/shard_map/ppermute | solution.py:356
  108.8 15.0 %all-to-all-done.1 = f16[16,32,768]{2,1,0:T(8,128)(2,1)S(1)} async-done(((f16[16,32,768]{2,1,0:T(8,128)(2,1)}), f16[16,32,768]{2,1,0:T(8,128)(2,1)S(1)}, u32[]{:S(2)}, u32[]{:S(2)}) %all-to-all-start.1) | async-done | bytes 786464 | tf_op jit(solution)/shard_map/all_to_all | solution.py:215
  123.8 0.1 convert_reduce_fusion.second_ref
  123.9 1.4 shard_map.70
  125.4 21.9 %all_to_all.19 = f16[32,8,768]{2,1,0:T(8,128)(2,1)S(1)} all-to-all(f16[32,8,768]{2,1,0:T(8,128)(2,1)S(1)} %convert_bitcast_fusion), channel_id=1, replica_groups=mesh['row'=8,'col'=32] {'col'}, dimensions={0} | all-to-all | bytes 786432 | tf_op jit(solution)/shard_map/all_to_all | solution.py:306
  147.3 0.1 bitcast_convert_fusion.got_ref
  147.4 2.0 %shard_map.71 = f32[128,768]{1,0:T(8,128)} custom-call(s32[3]{0:T(128)S(1)} %pad_add_fusion._.at_ref, f32[128,768]{1,0:T(8,128)S(1)} %shard_map.64.fock_ref, f32[256,768]{1,0:T(8,128)S(1)} %bitcast_convert_fusion.got_ref), custom_call_target="tpu_custom_call" | custom-call | bytes 1179648 | tf_op jit(solution)/shard_map/pallas_call | solution.py:242
  (11 shorter events, 0.1 us)
Async XLA Ops:
  0.0 9.6 %copy-start.9 = (s32[16]{0:T(128)S(1)}, s32[16]{0:T(128)}, u32[]{:S(2)}) copy-start(s32[16]{0:T(128)} %cd_ref.1) | copy-start | bytes 196
  0.0 9.6 %copy-start.10 = (s32[6]{0:T(128)S(1)}, s32[6]{0:T(128)}, u32[]{:S(2)}) copy-start(s32[6]{0:T(128)} %ab_ref.1) | copy-start | bytes 76
  0.0 1.6 %copy-start.3 = (bf16[512,2048]{1,0:T(8,128)(2,1)S(1)}, bf16[512,2048]{1,0:T(8,128)(2,1)}, u32[]{:S(2)}) copy-start(bf16[512,2048]{1,0:T(8,128)(2,1)} %amplitudes_ref.1) | copy-start | bytes 6291460
  4.8 8.4 %copy-start.5 = (bf16[192,2048]{1,0:T(8,128)(2,1)}, bf16[192,2048]{1,0:T(8,128)(2,1)S(1)}, u32[]{:S(2)}) copy-start(bf16[192,2048]{1,0:T(8,128)(2,1)S(1)} %get-tuple-element.35.mirrored_ref.refs_1_) | copy-start | bytes 2359300
  4.8 25.2 %collective-permute-start = (bf16[256,2048]{1,0:T(8,128)(2,1)}, bf16[256,2048]{1,0:T(8,128)(2,1)}, u32[]{:S(2)}, u32[]{:S(2)}) collective-permute-start(bf16[256,2048]{1,0:T(8,128)(2,1)} %get-tuple-element.29.own_ref), channel_id=1, source_target_pairs={{0,32},{32,0},{64,96},{96,64},{128,160},{160,128},{192,224},{224,1... | collective-permute-start | bytes 3145736 | tf_op jit(solution)/shard_map/ppermute | solution.py:323
  6.4 26.1 %collective-permute-start.2 = (bf16[256,2048]{1,0:T(8,128)(2,1)}, bf16[256,2048]{1,0:T(8,128)(2,1)}, u32[]{:S(2)}, u32[]{:S(2)}) collective-permute-start(bf16[256,2048]{1,0:T(8,128)(2,1)} %get-tuple-element.29.own_ref), channel_id=1, source_target_pairs={{0,192},{32,224},{64,0},{96,32},{128,64},{160,96},{192,128},{224,1... | collective-permute-start | bytes 3145736 | tf_op jit(solution)/shard_map/ppermute | solution.py:324
  7.2 25.3 %collective-permute-start.1 = (bf16[256,2048]{1,0:T(8,128)(2,1)}, bf16[256,2048]{1,0:T(8,128)(2,1)}, u32[]{:S(2)}, u32[]{:S(2)}) collective-permute-start(bf16[256,2048]{1,0:T(8,128)(2,1)} %get-tuple-element.30), channel_id=1, source_target_pairs={{0,64},{32,96},{64,128},{96,160},{128,192},{160,224},{192,0},{224,... | collective-permute-start | bytes 3145736 | tf_op jit(solution)/shard_map/ppermute | solution.py:325
  9.6 1.9 %copy-start = (bf16[2048,768]{1,0:T(8,128)(2,1)S(1)}, bf16[2048,768]{1,0:T(8,128)(2,1)}, u32[]{:S(2)}) copy-start(bf16[2048,768]{1,0:T(8,128)(2,1)} %integrals_ref) | copy-start | bytes 9437188
  13.2 24.8 %copy-start.1 = (bf16[2048,768]{1,0:T(8,128)(2,1)}, bf16[2048,768]{1,0:T(8,128)(2,1)S(1)}, u32[]{:S(2)}) copy-start(bf16[2048,768]{1,0:T(8,128)(2,1)S(1)} %shard_map.66.panel_ref) | copy-start | bytes 9437188
  13.2 30.5 %collective-permute-start.7 = (bf16[2048,768]{1,0:T(8,128)(2,1)S(1)}, bf16[2048,768]{1,0:T(8,128)(2,1)}, u32[]{:S(2)}, u32[]{:S(2)}) collective-permute-start(bf16[2048,768]{1,0:T(8,128)(2,1)S(1)} %shard_map.66.panel_ref), channel_id=1, source_target_pairs={{0,1},{1,0},{2,3},{3,2},{4,5},{5,4},{6,7},{7,6},{8,9},{9,8},{10,11... | collective-permute-start | bytes 9437192 | tf_op jit(solution)/shard_map/ppermute | solution.py:329
  32.5 1.1 copy-start.6
  38.0 4.2 %collective-permute-start.8 = (bf16[512,2048]{1,0:T(8,128)(2,1)S(1)}, bf16[512,2048]{1,0:T(8,128)(2,1)S(1)}, u32[]{:S(2)}, u32[]{:S(2)}) collective-permute-start(bf16[512,2048]{1,0:T(8,128)(2,1)S(1)} %get-tuple-element.49), channel_id=1, source_target_pairs={{0,1},{1,0},{2,3},{3,2},{4,5},{5,4},{6,7},{7,6},{8,9},{9,8},{10,11... | collective-permute-start | bytes 6291464 | tf_op jit(solution)/shard_map/ppermute | solution.py:341
  38.0 34.1 %collective-permute-start.5 = (bf16[320,2048]{1,0:T(8,128)(2,1)}, bf16[320,2048]{1,0:T(8,128)(2,1)}, u32[]{:S(2)}, u32[]{:S(2)}) collective-permute-start(bf16[320,2048]{1,0:T(8,128)(2,1)} %get-tuple-element.44), channel_id=1, source_target_pairs={{0,32},{32,0},{64,96},{96,64},{128,160},{160,128},{192,224},{224,1... | collective-permute-start | bytes 3932168 | tf_op jit(solution)/shard_map/ppermute | solution.py:344
  38.6 33.5 %collective-permute-start.3 = (bf16[256,2048]{1,0:T(8,128)(2,1)}, bf16[256,2048]{1,0:T(8,128)(2,1)}, u32[]{:S(2)}, u32[]{:S(2)}) collective-permute-start(bf16[256,2048]{1,0:T(8,128)(2,1)} %collective-permute-done.partner_ref), channel_id=1, source_target_pairs={{0,192},{32,224},{64,0},{96,32},{128,64},{160,96},{192,128},{224,1... | collective-permute-start | bytes 3145736 | tf_op jit(solution)/shard_map/ppermute | solution.py:342
  38.6 33.5 %collective-permute-start.4 = (bf16[192,2048]{1,0:T(8,128)(2,1)}, bf16[192,2048]{1,0:T(8,128)(2,1)}, u32[]{:S(2)}, u32[]{:S(2)}) collective-permute-start(bf16[192,2048]{1,0:T(8,128)(2,1)} %get-tuple-element.43), channel_id=1, source_target_pairs={{0,64},{32,96},{64,128},{96,160},{128,192},{160,224},{192,0},{224,... | collective-permute-start | bytes 2359304 | tf_op jit(solution)/shard_map/ppermute | solution.py:343
  42.2 1.5 copy-start.13
  42.2 29.9 %collective-permute-start.6 = (bf16[64,2048]{1,0:T(8,128)(2,1)S(1)}, bf16[64,2048]{1,0:T(8,128)(2,1)}, u32[]{:S(2)}, u32[]{:S(2)}) collective-permute-start(bf16[64,2048]{1,0:T(8,128)(2,1)S(1)} %get-tuple-element.45), channel_id=1, source_target_pairs={{0,128},{32,160},{64,192},{96,224},{128,0},{160,32},{192,64},{224,... | collective-permute-start | bytes 786440 | tf_op jit(solution)/shard_map/ppermute | solution.py:345
  51.4 20.8 %copy-start.2 = (bf16[2048,768]{1,0:T(8,128)(2,1)S(1)}, bf16[2048,768]{1,0:T(8,128)(2,1)}, u32[]{:S(2)}) copy-start(bf16[2048,768]{1,0:T(8,128)(2,1)} %copy-done.1) | copy-start | bytes 9437188
  52.4 32.0 %all-to-all-start = ((f16[8,64,768]{2,1,0:T(8,128)(2,1)}), f16[8,64,768]{2,1,0:T(8,128)(2,1)}, u32[]{:S(2)}, u32[]{:S(2)}) async-start(f16[8,64,768]{2,1,0:T(8,128)(2,1)} %multiply_convert_fusion.1), calls=%async_computation | async-start | bytes 1572864 | tf_op jit(solution)/shard_map/all_to_all | solution.py:222
  72.1 1.1 copy-start.7
  79.4 1.2 copy-start.4
  80.6 1.1 copy-start.11
  85.7 3.7 %collective-permute-start.10 = (f32[16,32,768]{2,1,0:T(8,128)}, f32[16,32,768]{2,1,0:T(8,128)S(1)}, u32[]{:S(2)}, u32[]{:S(2)}) collective-permute-start(f32[16,32,768]{2,1,0:T(8,128)} %copy-done.11), channel_id=1, source_target_pairs={{0,1},{1,0},{2,3},{3,2},{4,5},{5,4},{6,7},{7,6},{8,9},{9,8},{10,11... | collective-permute-start | bytes 4718600 | tf_op jit(solution)/shard_map/ppermute | solution.py:211
  92.0 8.6 %copy-start.12 = (f32[64,64]{1,0:T(8,128)S(1)}, f32[64,64]{1,0:T(8,128)}, u32[]{:S(2)}) copy-start(f32[64,64]{1,0:T(8,128)} %param.11) | copy-start | bytes 49156
  92.0 12.7 %copy-start.8 = (bf16[128,768]{1,0:T(8,128)(2,1)S(1)}, bf16[128,768]{1,0:T(8,128)(2,1)}, u32[]{:S(2)}) copy-start(bf16[128,768]{1,0:T(8,128)(2,1)} %slab_ref.1) | copy-start | bytes 589828
  92.0 31.9 %all-to-all-start.1 = ((f16[16,32,768]{2,1,0:T(8,128)(2,1)}), f16[16,32,768]{2,1,0:T(8,128)(2,1)S(1)}, u32[]{:S(2)}, u32[]{:S(2)}) async-start(f16[16,32,768]{2,1,0:T(8,128)(2,1)} %multiply_convert_fusion), calls=%async_computation.1 | async-start | bytes 1572864 | tf_op jit(solution)/shard_map/all_to_all | solution.py:215
  100.9 7.9 %collective-permute-start.9 = (f32[32,768]{1,0:T(8,128)S(1)}, f32[32,768]{1,0:T(8,128)S(1)}, u32[]{:S(2)}, u32[]{:S(2)}) collective-permute-start(f32[32,768]{1,0:T(8,128)S(1)} %dynamic-slice_bitcast_fusion), channel_id=1, source_target_pairs={{0,16},{1,17},{2,18},{3,19},{4,20},{5,21},{6,22},{7,23},{8,24},{9,... | collective-permute-start | bytes 294920 | tf_op jit(solution)/shard_map/ppermute | solution.py:356

commit v5 on v4

--- a/solution.py
+++ b/solution.py
@@ -219,10 +219,9 @@
 
 
 def send_to_z(parts):
-    got = lax.all_to_all(
+    return lax.all_to_all(
         parts, "col", split_axis=0, concat_axis=0, axis_index_groups=Z_GROUPS, tiled=True
     )
-    return got.astype(jnp.float32).sum(0).reshape(HI, -1, parts.shape[2])
 
 
 def exact_dot(a, b):
@@ -350,6 +349,7 @@
         k, panel, SECOND, [right_partner, mirrored, from_left, across, far], COST
     )
     theirs, first = lax.optimization_barrier((theirs, first))
+    first = first.astype(jnp.float32).sum(0).reshape(HI, -1, n)
     h = c // 16
     kept = lax.dynamic_index_in_dim(first, h, 0, keepdims=False)
     other = lax.dynamic_index_in_dim(first, 1 - h, 0, keepdims=False)

time: 150 us -> 149 us (level)
  transfers between devices with their start and end apart: 13 -> 13, of which waited for: 8 -> 8; matrix products, arithmetic and copies ran while one was open for 1% -> 2% of each run, Pallas kernels for 14% -> 14%
where the time goes in v5:
time: 149 us; the launch traced here: 148 us
  waiting for transfers between devices  54 us (36%)
  starting transfers between devices  31.1 us (21%)
  Pallas kernels  27.3 us (18%)
  blocking collectives  21.9 us (15%)
  local copies, waits for them, and re-layouts  8.37 us (6%)
  other arithmetic  5.15 us (3%)
    all_to_all x1, blocking collectives, exchange(): return lax.all_to_all(rows, 'col', split_axis=0, concat_axis=0, tiled=True)  21.9 us
    ppermute x1, waiting for transfers between devices, per_device(): partner = lax.ppermute(own, 'row', Y_SWAP)  16.7 us
    all_to_all x1, waiting for transfers between devices, send_to_slots(): lax.all_to_all(parts, 'col', split_axis=0, concat_axis=0, axis_index_grou...  14.1 us
    ppermute x1, waiting for transfers between devices, per_device(): far = lax.ppermute(to_far, 'row', x_shift(2))  11.1 us
    all_to_all x1, starting transfers between devices, send_to_z(): lax.all_to_all(parts, 'col', split_axis=0, concat_axis=0, axis_index_grou...  8.6 us
    all_to_all x1, starting transfers between devices, send_to_slots(): lax.all_to_all(parts, 'col', split_axis=0, concat_axis=0, axis_index_grou...  8.6 us
    unnamed x28, local copies, waits for them, and re-layouts  8.11 us
    pallas_call x1, Pallas kernels, first_sums(): pl.pallas_call(first_sums_kernel, grid=(n // tile,), in_specs=[SCALARS, c...  7.69 us
  transfers between devices with their start and end apart: 13, of which 8 were waited for; matrix products, arithmetic and copies ran while one was open for 2% of the time, Pallas kernels for 14%

profile of v5, /device:TPU:6, one launch (start us, length us, event | category | flops | bytes accessed | tf_op | source)
XLA Modules:
  0.0 148.0 jit_solution(8513049232342398390)
XLA Ops:
  0.0 0.0 copy-start.9
  0.0 0.0 copy-start.10
  0.0 0.0 copy-start.3
  0.0 1.6 %copy-done.3 = bf16[512,2048]{1,0:T(8,128)(2,1)S(1)} copy-done((bf16[512,2048]{1,0:T(8,128)(2,1)S(1)}, bf16[512,2048]{1,0:T(8,128)(2,1)}, u32[]{:S(2)}) %copy-start.3) | copy-done | bytes 2097176
  1.6 3.2 %shard_map.65 = (bf16[256,2048]{1,0:T(8,128)(2,1)}, bf16[256,2048]{1,0:T(8,128)(2,1)}, bf16[192,2048]{1,0:T(8,128)(2,1)S(1)}) custom-call(s32[1]{0:T(128)} %bitcast.5.r_ref, bf16[512,2048]{1,0:T(8,128)(2,1)S(1)} %copy-done.3), custom_call_target="tpu_custom_call" | custom-call | tf_op jit(solution)/shard_map/pallas_call | solution.py:102
  4.8 1.6 %collective-permute-start = (bf16[256,2048]{1,0:T(8,128)(2,1)}, bf16[256,2048]{1,0:T(8,128)(2,1)}, u32[]{:S(2)}, u32[]{:S(2)}) collective-permute-start(bf16[256,2048]{1,0:T(8,128)(2,1)} %get-tuple-element.29.own_ref), channel_id=1, source_target_pairs={{0,32},{32,0},{64,96},{96,64},{128,160},{160,128},{192,224},{224,1... | collective-permute-start | bytes 3145736 | tf_op jit(solution)/shard_map/ppermute | solution.py:322
  6.4 0.8 collective-permute-start.2
  7.2 2.4 %collective-permute-start.1 = (bf16[256,2048]{1,0:T(8,128)(2,1)}, bf16[256,2048]{1,0:T(8,128)(2,1)}, u32[]{:S(2)}, u32[]{:S(2)}) collective-permute-start(bf16[256,2048]{1,0:T(8,128)(2,1)} %get-tuple-element.30), channel_id=1, source_target_pairs={{0,64},{32,96},{64,128},{96,160},{128,192},{160,224},{192,0},{224,... | collective-permute-start | bytes 3145736 | tf_op jit(solution)/shard_map/ppermute | solution.py:324
  9.6 0.0 copy-done.9
  9.6 0.0 copy-done.10
  9.6 1.9 %copy-done = bf16[2048,768]{1,0:T(8,128)(2,1)S(1)} copy-done((bf16[2048,768]{1,0:T(8,128)(2,1)S(1)}, bf16[2048,768]{1,0:T(8,128)(2,1)}, u32[]{:S(2)}) %copy-start) | copy-done | bytes 3145752
  11.5 1.6 %shard_map.66.panel_ref = bf16[2048,768]{1,0:T(8,128)(2,1)S(1)} custom-call(s32[16]{0:T(128)S(1)} %copy-done.9, s32[6]{0:T(128)S(1)} %copy-done.10, bf16[2048,768]{1,0:T(8,128)(2,1)S(1)} %copy-done), custom_call_target="tpu_custom_call" | custom-call | bytes 6291456 | tf_op jit(solution)/shard_map/pallas_call | solution.py:64
  13.2 0.0 copy-done.5
  13.2 0.0 copy-start.1
  13.2 0.1 collective-permute-start.7
  13.3 16.7 %collective-permute-done.partner_ref = bf16[256,2048]{1,0:T(8,128)(2,1)} collective-permute-done((bf16[256,2048]{1,0:T(8,128)(2,1)}, bf16[256,2048]{1,0:T(8,128)(2,1)}, u32[]{:S(2)}, u32[]{:S(2)}) %collective-permute-start) | collective-permute-done | bytes 1048608 | tf_op jit(solution)/shard_map/ppermute | solution.py:322
  30.0 2.5 %collective-permute-done.2.right_ref = bf16[256,2048]{1,0:T(8,128)(2,1)} collective-permute-done((bf16[256,2048]{1,0:T(8,128)(2,1)}, bf16[256,2048]{1,0:T(8,128)(2,1)}, u32[]{:S(2)}, u32[]{:S(2)}) %collective-permute-start.2) | collective-permute-done | bytes 1048608 | tf_op jit(solution)/shard_map/ppermute | solution.py:323
  32.5 0.0 collective-permute-done.1.left_ref
  32.5 1.1 copy-done.6
  33.7 4.3 %shard_map.67 = (bf16[192,2048]{1,0:T(8,128)(2,1)}, bf16[320,2048]{1,0:T(8,128)(2,1)}, bf16[64,2048]{1,0:T(8,128)(2,1)S(1)}, bf16[512,2048]{1,0:T(8,128)(2,1)S(1)}) custom-call(s32[1]{0:T(128)} %bitcast.4.k_ref, bf16[256,2048]{1,0:T(8,128)(2,1)} %get-tuple-element.29.own_ref, bf16[256,2048]{1,0:T(8,128)(2,1)} %collective-permute-done.partner_ref, ...), custom_call_target="tpu_custom_call" | custom-call | tf_op jit(solution)/shard_map/pallas_call | solution.py:102
  38.0 0.0 copy-done.1
  38.0 0.1 collective-permute-start.8
  38.0 0.5 collective-permute-start.5
  38.6 0.0 collective-permute-start.3
  38.6 3.2 %collective-permute-start.4 = (bf16[192,2048]{1,0:T(8,128)(2,1)}, bf16[192,2048]{1,0:T(8,128)(2,1)}, u32[]{:S(2)}, u32[]{:S(2)}) collective-permute-start(bf16[192,2048]{1,0:T(8,128)(2,1)} %get-tuple-element.43), channel_id=1, source_target_pairs={{0,64},{32,96},{64,128},{96,160},{128,192},{160,224},{192,0},{224,... | collective-permute-start | bytes 2359304 | tf_op jit(solution)/shard_map/ppermute | solution.py:342
  41.8 0.4 collective-permute-done.8.got_ref
  42.2 1.5 collective-permute-start.6
  43.6 0.0 collective-permute-done.7.other_panel_ref
  43.7 0.0 copy-done.13
  43.7 7.7 %shard_map.69 = f32[8,64,768]{2,1,0:T(8,128)S(1)} custom-call(s32[1]{0:T(128)} %bitcast.4.k_ref, bf16[2048,768]{1,0:T(8,128)(2,1)} %copy-done.1, bf16[2048,768]{1,0:T(8,128)(2,1)} %collective-permute-done.7.other_panel_ref, bf16[256,2048]{1,0:T(8,128)(2,1)} %get-tuple-element.29.own_ref, bf16[256,2048]{1,0:T(8,128)(2,1)} %collective-permute-done.partner_ref, ...), custom_call_target="tpu_custom_call" | custom-call | flops 40000000000 | tf_op jit(solution)/shard_map/pallas_call | solution.py:150
  51.4 0.0 copy-start.2
  51.4 1.0 multiply_convert_fusion.1
  52.4 8.6 %all-to-all-start = ((f16[8,64,768]{2,1,0:T(8,128)(2,1)}), f16[8,64,768]{2,1,0:T(8,128)(2,1)}, u32[]{:S(2)}, u32[]{:S(2)}) async-start(f16[8,64,768]{2,1,0:T(8,128)(2,1)} %multiply_convert_fusion.1), calls=%async_computation | async-start | bytes 1572864 | tf_op jit(solution)/shard_map/all_to_all | solution.py:222
  61.0 11.1 %collective-permute-done.6.refs_4_ = bf16[64,2048]{1,0:T(8,128)(2,1)} collective-permute-done((bf16[64,2048]{1,0:T(8,128)(2,1)S(1)}, bf16[64,2048]{1,0:T(8,128)(2,1)}, u32[]{:S(2)}, u32[]{:S(2)}) %collective-permute-start.6) | collective-permute-done | bytes 262176 | tf_op jit(solution)/shard_map/ppermute | solution.py:344
  72.1 0.0 collective-permute-done.4.refs_2_
  72.1 0.0 collective-permute-done.3.refs_0_
  72.1 0.0 collective-permute-done.5.refs_3_
  72.1 0.0 copy-done.2
  72.1 0.0 copy-start.7
  72.1 1.1 copy-done.7
  73.3 6.1 %shard_map.68 = (f32[16,32,768]{2,1,0:T(8,128)S(1)}, f32[16,32,768]{2,1,0:T(8,128)S(1)}) custom-call(s32[1]{0:T(128)} %bitcast.4.k_ref, bf16[2048,768]{1,0:T(8,128)(2,1)S(1)} %copy-done.2, bf16[256,2048]{1,0:T(8,128)(2,1)} %collective-permute-done.3.refs_0_, bf16[192,2048]{1,0:T(8,128)(2,1)S(1)} %copy-done.7, ...), custom_call_target="tpu_custom_call" | custom-call | flops 40000000000 | tf_op jit(solution)/shard_map/pallas_call | solution.py:198
  79.4 0.0 copy-start.4
  79.4 1.2 copy-done.4
  80.6 1.1 copy-done.11
  81.7 2.7 %all-to-all-done = f16[8,64,768]{2,1,0:T(8,128)(2,1)} async-done(((f16[8,64,768]{2,1,0:T(8,128)(2,1)}), f16[8,64,768]{2,1,0:T(8,128)(2,1)}, u32[]{:S(2)}, u32[]{:S(2)}) %all-to-all-start) | async-done | bytes 786464 | tf_op jit(solution)/shard_map/all_to_all | solution.py:222
  84.4 0.0 collective-permute-start.10
  84.5 3.6 %collective-permute-done.10 = f32[16,32,768]{2,1,0:T(8,128)S(1)} collective-permute-done((f32[16,32,768]{2,1,0:T(8,128)}, f32[16,32,768]{2,1,0:T(8,128)S(1)}, u32[]{:S(2)}, u32[]{:S(2)}) %collective-permute-start.10) | collective-permute-done | bytes 1572896 | tf_op jit(solution)/shard_map/ppermute | solution.py:211
  88.1 2.6 %multiply_convert_fusion = f16[16,32,768]{2,1,0:T(8,128)(2,1)} fusion(f32[16,32,768]{2,1,0:T(8,128)} %copy-done.4, f32[16,32,768]{2,1,0:T(8,128)S(1)} %collective-permute-done.10), kind=kLoop, calls=%fused_computation.1 | loop fusion | flops 1179648 | bytes 3932160 | tf_op jit(solution)/shard_map/convert_element_type | solution.py:211
  90.6 8.6 %all-to-all-start.1 = ((f16[16,32,768]{2,1,0:T(8,128)(2,1)}), f16[16,32,768]{2,1,0:T(8,128)(2,1)S(1)}, u32[]{:S(2)}, u32[]{:S(2)}) async-start(f16[16,32,768]{2,1,0:T(8,128)(2,1)} %multiply_convert_fusion), calls=%async_computation.1 | async-start | bytes 1572864 | tf_op jit(solution)/shard_map/all_to_all | solution.py:215
  99.3 0.0 copy-done.12
  99.3 0.1 copy.7
  99.4 0.1 tile.10.fock_ref
  99.5 1.3 convert_reduce_fusion.1
  100.8 3.7 %collective-permute-start.9 = (f32[32,768]{1,0:T(8,128)S(1)}, f32[32,768]{1,0:T(8,128)S(1)}, u32[]{:S(2)}, u32[]{:S(2)}) collective-permute-start(f32[32,768]{1,0:T(8,128)S(1)} %dynamic-slice_bitcast_fusion), channel_id=1, source_target_pairs={{0,16},{1,17},{2,18},{3,19},{4,20},{5,21},{6,22},{7,23},{8,24},{9,... | collective-permute-start | bytes 294920 | tf_op jit(solution)/shard_map/ppermute | solution.py:356
  104.5 0.1 pad_add_fusion._.at_ref
  104.5 0.0 copy-done.8
  104.6 1.0 shard_map.64.fock_ref
  105.6 2.8 %collective-permute-done.9 = f32[32,768]{1,0:T(8,128)S(1)} collective-permute-done((f32[32,768]{1,0:T(8,128)S(1)}, f32[32,768]{1,0:T(8,128)S(1)}, u32[]{:S(2)}, u32[]{:S(2)}) %collective-permute-start.9) | collective-permute-done | bytes 98336 | tf_op jit(solution)/shard_map/ppermute | solution.py:356
  108.3 14.1 %all-to-all-done.1 = f16[16,32,768]{2,1,0:T(8,128)(2,1)S(1)} async-done(((f16[16,32,768]{2,1,0:T(8,128)(2,1)}), f16[16,32,768]{2,1,0:T(8,128)(2,1)S(1)}, u32[]{:S(2)}, u32[]{:S(2)}) %all-to-all-start.1) | async-done | bytes 786464 | tf_op jit(solution)/shard_map/all_to_all | solution.py:215
  122.5 0.1 convert_reduce_fusion.second_ref
  122.6 1.4 shard_map.70
  124.1 21.9 %all_to_all.19 = f16[32,8,768]{2,1,0:T(8,128)(2,1)S(1)} all-to-all(f16[32,8,768]{2,1,0:T(8,128)(2,1)S(1)} %convert_bitcast_fusion), channel_id=1, replica_groups=mesh['row'=8,'col'=32] {'col'}, dimensions={0} | all-to-all | bytes 786432 | tf_op jit(solution)/shard_map/all_to_all | solution.py:305
  146.0 0.1 bitcast_convert_fusion.got_ref
  146.0 2.0 %shard_map.71 = f32[128,768]{1,0:T(8,128)} custom-call(s32[3]{0:T(128)S(1)} %pad_add_fusion._.at_ref, f32[128,768]{1,0:T(8,128)S(1)} %shard_map.64.fock_ref, f32[256,768]{1,0:T(8,128)S(1)} %bitcast_convert_fusion.got_ref), custom_call_target="tpu_custom_call" | custom-call | bytes 1179648 | tf_op jit(solution)/shard_map/pallas_call | solution.py:241
  (11 shorter events, 0.1 us)
Async XLA Ops:
  0.0 9.6 %copy-start.9 = (s32[16]{0:T(128)S(1)}, s32[16]{0:T(128)}, u32[]{:S(2)}) copy-start(s32[16]{0:T(128)} %cd_ref.1) | copy-start | bytes 196
  0.0 9.6 %copy-start.10 = (s32[6]{0:T(128)S(1)}, s32[6]{0:T(128)}, u32[]{:S(2)}) copy-start(s32[6]{0:T(128)} %ab_ref.1) | copy-start | bytes 76
  0.0 1.6 %copy-start.3 = (bf16[512,2048]{1,0:T(8,128)(2,1)S(1)}, bf16[512,2048]{1,0:T(8,128)(2,1)}, u32[]{:S(2)}) copy-start(bf16[512,2048]{1,0:T(8,128)(2,1)} %amplitudes_ref.1) | copy-start | bytes 6291460
  4.8 8.4 %copy-start.5 = (bf16[192,2048]{1,0:T(8,128)(2,1)}, bf16[192,2048]{1,0:T(8,128)(2,1)S(1)}, u32[]{:S(2)}) copy-start(bf16[192,2048]{1,0:T(8,128)(2,1)S(1)} %get-tuple-element.35.mirrored_ref.refs_1_) | copy-start | bytes 2359300
  4.8 25.2 %collective-permute-start = (bf16[256,2048]{1,0:T(8,128)(2,1)}, bf16[256,2048]{1,0:T(8,128)(2,1)}, u32[]{:S(2)}, u32[]{:S(2)}) collective-permute-start(bf16[256,2048]{1,0:T(8,128)(2,1)} %get-tuple-element.29.own_ref), channel_id=1, source_target_pairs={{0,32},{32,0},{64,96},{96,64},{128,160},{160,128},{192,224},{224,1... | collective-permute-start | bytes 3145736 | tf_op jit(solution)/shard_map/ppermute | solution.py:322
  6.4 26.1 %collective-permute-start.2 = (bf16[256,2048]{1,0:T(8,128)(2,1)}, bf16[256,2048]{1,0:T(8,128)(2,1)}, u32[]{:S(2)}, u32[]{:S(2)}) collective-permute-start(bf16[256,2048]{1,0:T(8,128)(2,1)} %get-tuple-element.29.own_ref), channel_id=1, source_target_pairs={{0,192},{32,224},{64,0},{96,32},{128,64},{160,96},{192,128},{224,1... | collective-permute-start | bytes 3145736 | tf_op jit(solution)/shard_map/ppermute | solution.py:323
  7.2 25.3 %collective-permute-start.1 = (bf16[256,2048]{1,0:T(8,128)(2,1)}, bf16[256,2048]{1,0:T(8,128)(2,1)}, u32[]{:S(2)}, u32[]{:S(2)}) collective-permute-start(bf16[256,2048]{1,0:T(8,128)(2,1)} %get-tuple-element.30), channel_id=1, source_target_pairs={{0,64},{32,96},{64,128},{96,160},{128,192},{160,224},{192,0},{224,... | collective-permute-start | bytes 3145736 | tf_op jit(solution)/shard_map/ppermute | solution.py:324
  9.6 1.9 %copy-start = (bf16[2048,768]{1,0:T(8,128)(2,1)S(1)}, bf16[2048,768]{1,0:T(8,128)(2,1)}, u32[]{:S(2)}) copy-start(bf16[2048,768]{1,0:T(8,128)(2,1)} %integrals_ref) | copy-start | bytes 9437188
  13.2 24.8 %copy-start.1 = (bf16[2048,768]{1,0:T(8,128)(2,1)}, bf16[2048,768]{1,0:T(8,128)(2,1)S(1)}, u32[]{:S(2)}) copy-start(bf16[2048,768]{1,0:T(8,128)(2,1)S(1)} %shard_map.66.panel_ref) | copy-start | bytes 9437188
  13.2 30.5 %collective-permute-start.7 = (bf16[2048,768]{1,0:T(8,128)(2,1)S(1)}, bf16[2048,768]{1,0:T(8,128)(2,1)}, u32[]{:S(2)}, u32[]{:S(2)}) collective-permute-start(bf16[2048,768]{1,0:T(8,128)(2,1)S(1)} %shard_map.66.panel_ref), channel_id=1, source_target_pairs={{0,1},{1,0},{2,3},{3,2},{4,5},{5,4},{6,7},{7,6},{8,9},{9,8},{10,11... | collective-permute-start | bytes 9437192 | tf_op jit(solution)/shard_map/ppermute | solution.py:328
  32.5 1.1 copy-start.6
  38.0 4.2 %collective-permute-start.8 = (bf16[512,2048]{1,0:T(8,128)(2,1)S(1)}, bf16[512,2048]{1,0:T(8,128)(2,1)S(1)}, u32[]{:S(2)}, u32[]{:S(2)}) collective-permute-start(bf16[512,2048]{1,0:T(8,128)(2,1)S(1)} %get-tuple-element.49), channel_id=1, source_target_pairs={{0,1},{1,0},{2,3},{3,2},{4,5},{5,4},{6,7},{7,6},{8,9},{9,8},{10,11... | collective-permute-start | bytes 6291464 | tf_op jit(solution)/shard_map/ppermute | solution.py:340
  38.0 34.1 %collective-permute-start.5 = (bf16[320,2048]{1,0:T(8,128)(2,1)}, bf16[320,2048]{1,0:T(8,128)(2,1)}, u32[]{:S(2)}, u32[]{:S(2)}) collective-permute-start(bf16[320,2048]{1,0:T(8,128)(2,1)} %get-tuple-element.44), channel_id=1, source_target_pairs={{0,32},{32,0},{64,96},{96,64},{128,160},{160,128},{192,224},{224,1... | collective-permute-start | bytes 3932168 | tf_op jit(solution)/shard_map/ppermute | solution.py:343
  38.6 33.5 %collective-permute-start.3 = (bf16[256,2048]{1,0:T(8,128)(2,1)}, bf16[256,2048]{1,0:T(8,128)(2,1)}, u32[]{:S(2)}, u32[]{:S(2)}) collective-permute-start(bf16[256,2048]{1,0:T(8,128)(2,1)} %collective-permute-done.partner_ref), channel_id=1, source_target_pairs={{0,192},{32,224},{64,0},{96,32},{128,64},{160,96},{192,128},{224,1... | collective-permute-start | bytes 3145736 | tf_op jit(solution)/shard_map/ppermute | solution.py:341
  38.6 33.5 %collective-permute-start.4 = (bf16[192,2048]{1,0:T(8,128)(2,1)}, bf16[192,2048]{1,0:T(8,128)(2,1)}, u32[]{:S(2)}, u32[]{:S(2)}) collective-permute-start(bf16[192,2048]{1,0:T(8,128)(2,1)} %get-tuple-element.43), channel_id=1, source_target_pairs={{0,64},{32,96},{64,128},{96,160},{128,192},{160,224},{192,0},{224,... | collective-permute-start | bytes 2359304 | tf_op jit(solution)/shard_map/ppermute | solution.py:342
  42.2 1.5 copy-start.13
  42.2 29.9 %collective-permute-start.6 = (bf16[64,2048]{1,0:T(8,128)(2,1)S(1)}, bf16[64,2048]{1,0:T(8,128)(2,1)}, u32[]{:S(2)}, u32[]{:S(2)}) collective-permute-start(bf16[64,2048]{1,0:T(8,128)(2,1)S(1)} %get-tuple-element.45), channel_id=1, source_target_pairs={{0,128},{32,160},{64,192},{96,224},{128,0},{160,32},{192,64},{224,... | collective-permute-start | bytes 786440 | tf_op jit(solution)/shard_map/ppermute | solution.py:344
  51.4 20.8 %copy-start.2 = (bf16[2048,768]{1,0:T(8,128)(2,1)S(1)}, bf16[2048,768]{1,0:T(8,128)(2,1)}, u32[]{:S(2)}) copy-start(bf16[2048,768]{1,0:T(8,128)(2,1)} %copy-done.1) | copy-start | bytes 9437188
  52.4 32.0 %all-to-all-start = ((f16[8,64,768]{2,1,0:T(8,128)(2,1)}), f16[8,64,768]{2,1,0:T(8,128)(2,1)}, u32[]{:S(2)}, u32[]{:S(2)}) async-start(f16[8,64,768]{2,1,0:T(8,128)(2,1)} %multiply_convert_fusion.1), calls=%async_computation | async-start | bytes 1572864 | tf_op jit(solution)/shard_map/all_to_all | solution.py:222
  72.1 1.1 copy-start.7
  79.4 1.2 copy-start.4
  80.6 1.1 copy-start.11
  84.4 3.6 %collective-permute-start.10 = (f32[16,32,768]{2,1,0:T(8,128)}, f32[16,32,768]{2,1,0:T(8,128)S(1)}, u32[]{:S(2)}, u32[]{:S(2)}) collective-permute-start(f32[16,32,768]{2,1,0:T(8,128)} %copy-done.11), channel_id=1, source_target_pairs={{0,1},{1,0},{2,3},{3,2},{4,5},{5,4},{6,7},{7,6},{8,9},{9,8},{10,11... | collective-permute-start | bytes 4718600 | tf_op jit(solution)/shard_map/ppermute | solution.py:211
  90.6 8.6 %copy-start.12 = (f32[64,64]{1,0:T(8,128)S(1)}, f32[64,64]{1,0:T(8,128)}, u32[]{:S(2)}) copy-start(f32[64,64]{1,0:T(8,128)} %param.11) | copy-start | bytes 49156
  90.6 13.9 %copy-start.8 = (bf16[128,768]{1,0:T(8,128)(2,1)S(1)}, bf16[128,768]{1,0:T(8,128)(2,1)}, u32[]{:S(2)}) copy-start(bf16[128,768]{1,0:T(8,128)(2,1)} %slab_ref.1) | copy-start | bytes 589828
  90.6 31.9 %all-to-all-start.1 = ((f16[16,32,768]{2,1,0:T(8,128)(2,1)}), f16[16,32,768]{2,1,0:T(8,128)(2,1)S(1)}, u32[]{:S(2)}, u32[]{:S(2)}) async-start(f16[16,32,768]{2,1,0:T(8,128)(2,1)} %multiply_convert_fusion), calls=%async_computation.1 | async-start | bytes 1572864 | tf_op jit(solution)/shard_map/all_to_all | solution.py:215
  100.8 7.5 %collective-permute-start.9 = (f32[32,768]{1,0:T(8,128)S(1)}, f32[32,768]{1,0:T(8,128)S(1)}, u32[]{:S(2)}, u32[]{:S(2)}) collective-permute-start(f32[32,768]{1,0:T(8,128)S(1)} %dynamic-slice_bitcast_fusion), channel_id=1, source_target_pairs={{0,16},{1,17},{2,18},{3,19},{4,20},{5,21},{6,22},{7,23},{8,24},{9,... | collective-permute-start | bytes 294920 | tf_op jit(solution)/shard_map/ppermute | solution.py:356

commit v6 on v5

--- a/solution.py
+++ b/solution.py
@@ -289,7 +289,7 @@
     )
 
 
-def update_kernel(at_ref, fock_ref, got_ref, out_ref):
+def weights_kernel(at_ref, out_ref):
     ej, at = grid(128, 256)
     e, j = ej >> 6, ej & 63
     i, peer, mine = 2 * at_ref[2] + e, at >> 3, (at & 1) == e
@@ -297,8 +297,14 @@
     weight = jnp.where(t == 31, 1 / LADDER_SCALE, 2 / LADDER_SCALE)
     forward = jnp.where(mine & ((at & 6) == 0) & (partner_of(i, t) == j), weight, 0.0)
     backward = jnp.where(mine & ((at & 6) == 2) & (partner_of(j, t) == i), weight, 0.0)
-    mirror = jnp.where(mine & ((at & 4) != 0) & ((peer << 1) + ((at >> 1) & 1) == j), 1 / FOCK_SCALE, 0.0)
-    out_ref[...] = fock_ref[...] + exact_dot(forward - backward - mirror, got_ref[...])
+    mirror = jnp.where(
+        mine & ((at & 4) != 0) & ((peer << 1) + ((at >> 1) & 1) == j), 1 / FOCK_SCALE, 0.0
+    )
+    out_ref[...] = forward - backward - mirror
+
+
+def update_kernel(_, fock_ref, weights_ref, got_ref, out_ref):
+    out_ref[...] = fock_ref[...] + exact_dot(weights_ref[...], got_ref[...])
 
 
 def exchange(rows):
@@ -348,7 +354,8 @@
     mine, theirs = slot_sums(
         k, panel, SECOND, [right_partner, mirrored, from_left, across, far], COST
     )
-    theirs, first = lax.optimization_barrier((theirs, first))
+    weights = whole(weights_kernel, place, [], 128, 256)
+    theirs, first, weights = lax.optimization_barrier((theirs, first, weights))
     first = first.astype(jnp.float32).sum(0).reshape(HI, -1, n)
     h = c // 16
     kept = lax.dynamic_index_in_dim(first, h, 0, keepdims=False)
@@ -358,7 +365,7 @@
 
     sent = whole(spread_kernel, place, [first, second, fock], 256, n).astype(jnp.float16)
     got = exchange(sent).astype(jnp.float32)
-    return whole(update_kernel, place, [fock, got], 128, n)
+    return whole(update_kernel, place, [fock, weights, got], 128, n)
 
 
 def solution(mesh):

time: 149 us -> 151 us (1.013)
  local copies, waits for them, and re-layouts: 8.37 us -> 10.3 us
    unnamed x28 -> x30, local copies, waits for them, and re-layouts: 8.11 us -> 10.1 us
    pallas_call x3 -> x4, Pallas kernels: 4.42 us -> 4.99 us  [whole(): pl.pallas_call(kernel, grid=(n // tile,), in_specs=[SCALARS] + [block(a.s...]
  transfers between devices with their start and end apart: 13 -> 13, of which waited for: 8 -> 7; matrix products, arithmetic and copies ran while one was open for 2% -> 2% of each run, Pallas kernels for 14% -> 14%
where the time goes in v6:
time: 151 us
  waiting for transfers between devices  53.5 us (35%)
  starting transfers between devices  31.7 us (21%)
  Pallas kernels  28 us (19%)
  blocking collectives  21.9 us (15%)
  local copies, waits for them, and re-layouts  10.3 us (7%)
  other arithmetic  5.16 us (3%)
    all_to_all x1, blocking collectives, exchange(): return lax.all_to_all(rows, 'col', split_axis=0, concat_axis=0, tiled=True)  21.9 us
    ppermute x1, waiting for transfers between devices, per_device(): partner = lax.ppermute(own, 'row', Y_SWAP)  16.7 us
    all_to_all x1, waiting for transfers between devices, send_to_slots(): lax.all_to_all(parts, 'col', split_axis=0, concat_axis=0, axis_index_grou...  14.4 us
    ppermute x1, waiting for transfers between devices, per_device(): far = lax.ppermute(to_far, 'row', x_shift(2))  11.7 us
    unnamed x30, local copies, waits for them, and re-layouts  10.1 us
    all_to_all x1, starting transfers between devices, send_to_slots(): lax.all_to_all(parts, 'col', split_axis=0, concat_axis=0, axis_index_grou...  9.38 us
    all_to_all x1, starting transfers between devices, send_to_z(): lax.all_to_all(parts, 'col', split_axis=0, concat_axis=0, axis_index_grou...  8.59 us
    pallas_call x1, Pallas kernels, first_sums(): pl.pallas_call(first_sums_kernel, grid=(n // tile,), in_specs=[SCALARS, c...  7.68 us
  transfers between devices with their start and end apart: 13, of which 7 were waited for; matrix products, arithmetic and copies ran while one was open for 2% of the time, Pallas kernels for 14%

profile of v6, /device:TPU:6, one launch (start us, length us, event | category | flops | bytes accessed | tf_op | source)
XLA Modules:
  0.0 150.7 jit_solution(10180138296386661563)
XLA Ops:
  0.0 0.0 copy-start.9
  0.0 1.6 %copy-done.3 = bf16[512,2048]{1,0:T(8,128)(2,1)S(1)} copy-done((bf16[512,2048]{1,0:T(8,128)(2,1)S(1)}, bf16[512,2048]{1,0:T(8,128)(2,1)}, u32[]{:S(2)}) %copy-start.3) | copy-done | bytes 2097176
  1.6 3.1 %shard_map.65 = (bf16[256,2048]{1,0:T(8,128)(2,1)}, bf16[256,2048]{1,0:T(8,128)(2,1)}, bf16[192,2048]{1,0:T(8,128)(2,1)S(1)}) custom-call(s32[1]{0:T(128)} %bitcast.5.r_ref, bf16[512,2048]{1,0:T(8,128)(2,1)S(1)} %copy-done.3), custom_call_target="tpu_custom_call" | custom-call | tf_op jit(solution)/shard_map/pallas_call | solution.py:102
  4.8 1.6 %collective-permute-start = (bf16[256,2048]{1,0:T(8,128)(2,1)}, bf16[256,2048]{1,0:T(8,128)(2,1)}, u32[]{:S(2)}, u32[]{:S(2)}) collective-permute-start(bf16[256,2048]{1,0:T(8,128)(2,1)} %get-tuple-element.30.own_ref), channel_id=1, source_target_pairs={{0,32},{32,0},{64,96},{96,64},{128,160},{160,128},{192,224},{224,1... | collective-permute-start | bytes 3145736 | tf_op jit(solution)/shard_map/ppermute | solution.py:328
  6.3 0.8 collective-permute-start.2
  7.2 2.4 %collective-permute-start.1 = (bf16[256,2048]{1,0:T(8,128)(2,1)}, bf16[256,2048]{1,0:T(8,128)(2,1)}, u32[]{:S(2)}, u32[]{:S(2)}) collective-permute-start(bf16[256,2048]{1,0:T(8,128)(2,1)} %get-tuple-element.31), channel_id=1, source_target_pairs={{0,64},{32,96},{64,128},{96,160},{128,192},{160,224},{192,0},{224,... | collective-permute-start | bytes 3145736 | tf_op jit(solution)/shard_map/ppermute | solution.py:330
  9.6 0.0 copy-done.9
  9.6 0.0 copy-done.10
  9.6 1.9 %copy-done = bf16[2048,768]{1,0:T(8,128)(2,1)S(1)} copy-done((bf16[2048,768]{1,0:T(8,128)(2,1)S(1)}, bf16[2048,768]{1,0:T(8,128)(2,1)}, u32[]{:S(2)}) %copy-start) | copy-done | bytes 3145752
  11.5 1.6 %shard_map.66.panel_ref = bf16[2048,768]{1,0:T(8,128)(2,1)S(1)} custom-call(s32[16]{0:T(128)S(1)} %copy-done.9, s32[6]{0:T(128)S(1)} %copy-done.10, bf16[2048,768]{1,0:T(8,128)(2,1)S(1)} %copy-done), custom_call_target="tpu_custom_call" | custom-call | bytes 6291456 | tf_op jit(solution)/shard_map/pallas_call | solution.py:64
  13.1 0.0 copy-done.5
  13.1 0.0 copy-start.1
  13.1 0.1 collective-permute-start.7
  13.3 16.7 %collective-permute-done.partner_ref = bf16[256,2048]{1,0:T(8,128)(2,1)} collective-permute-done((bf16[256,2048]{1,0:T(8,128)(2,1)}, bf16[256,2048]{1,0:T(8,128)(2,1)}, u32[]{:S(2)}, u32[]{:S(2)}) %collective-permute-start) | collective-permute-done | bytes 1048608 | tf_op jit(solution)/shard_map/ppermute | solution.py:328
  30.0 2.5 %collective-permute-done.2.right_ref = bf16[256,2048]{1,0:T(8,128)(2,1)} collective-permute-done((bf16[256,2048]{1,0:T(8,128)(2,1)}, bf16[256,2048]{1,0:T(8,128)(2,1)}, u32[]{:S(2)}, u32[]{:S(2)}) %collective-permute-start.2) | collective-permute-done | bytes 1048608 | tf_op jit(solution)/shard_map/ppermute | solution.py:329
  32.5 0.0 collective-permute-done.1.left_ref
  32.5 1.1 copy-done.6
  33.6 4.4 %shard_map.67 = (bf16[192,2048]{1,0:T(8,128)(2,1)S(1)}, bf16[320,2048]{1,0:T(8,128)(2,1)S(1)}, bf16[64,2048]{1,0:T(8,128)(2,1)S(1)}, bf16[512,2048]{1,0:T(8,128)(2,1)}) custom-call(s32[1]{0:T(128)} %bitcast.4.k_ref, bf16[256,2048]{1,0:T(8,128)(2,1)} %get-tuple-element.30.own_ref, bf16[256,2048]{1,0:T(8,128)(2,1)} %collective-permute-done.partner_ref, ...), custom_call_target="tpu_custom_call" | custom-call | tf_op jit(solution)/shard_map/pallas_call | solution.py:102
  38.0 0.0 copy-done.1
  38.0 1.1 copy-done.12
  39.1 0.9 copy-done.13
  40.0 0.0 collective-permute-start.8
  40.0 0.1 pad_add_fusion._.at_ref
  40.1 0.8 shard_map.70.weights_ref
  40.9 0.5 collective-permute-start.5
  41.4 0.0 collective-permute-start.3
  41.4 3.2 %collective-permute-start.4 = (bf16[192,2048]{1,0:T(8,128)(2,1)}, bf16[192,2048]{1,0:T(8,128)(2,1)}, u32[]{:S(2)}, u32[]{:S(2)}) collective-permute-start(bf16[192,2048]{1,0:T(8,128)(2,1)} %copy-done.13), channel_id=1, source_target_pairs={{0,64},{32,96},{64,128},{96,160},{128,192},{160,224},{192,0},{224,... | collective-permute-start | bytes 2359304 | tf_op jit(solution)/shard_map/ppermute | solution.py:348
  44.6 0.0 collective-permute-done.8.got_ref
  44.6 1.3 collective-permute-start.6
  46.0 0.0 collective-permute-done.7.other_panel_ref
  46.0 7.7 %shard_map.69 = f32[8,64,768]{2,1,0:T(8,128)S(1)} custom-call(s32[1]{0:T(128)} %bitcast.4.k_ref, bf16[2048,768]{1,0:T(8,128)(2,1)} %copy-done.1, bf16[2048,768]{1,0:T(8,128)(2,1)} %collective-permute-done.7.other_panel_ref, bf16[256,2048]{1,0:T(8,128)(2,1)} %get-tuple-element.30.own_ref, bf16[256,2048]{1,0:T(8,128)(2,1)} %collective-permute-done.partner_ref, ...), custom_call_target="tpu_custom_call" | custom-call | flops 40000000000 | tf_op jit(solution)/shard_map/pallas_call | solution.py:150
  53.7 0.0 copy-start.2
  53.7 1.0 multiply_convert_fusion.1
  54.7 8.6 %all-to-all-start = ((f16[8,64,768]{2,1,0:T(8,128)(2,1)}), f16[8,64,768]{2,1,0:T(8,128)(2,1)}, u32[]{:S(2)}, u32[]{:S(2)}) async-start(f16[8,64,768]{2,1,0:T(8,128)(2,1)} %multiply_convert_fusion.1), calls=%async_computation | async-start | bytes 1572864 | tf_op jit(solution)/shard_map/all_to_all | solution.py:222
  63.3 11.7 %collective-permute-done.6.refs_4_ = bf16[64,2048]{1,0:T(8,128)(2,1)} collective-permute-done((bf16[64,2048]{1,0:T(8,128)(2,1)S(1)}, bf16[64,2048]{1,0:T(8,128)(2,1)}, u32[]{:S(2)}, u32[]{:S(2)}) %collective-permute-start.6) | collective-permute-done | bytes 262176 | tf_op jit(solution)/shard_map/ppermute | solution.py:350
  75.0 0.0 collective-permute-done.4.refs_2_
  75.0 0.0 collective-permute-done.3.refs_0_
  75.0 0.0 collective-permute-done.5.refs_3_
  75.0 0.0 copy-done.2
  75.0 0.0 copy-start.7
  75.0 1.1 copy-done.7
  76.2 6.1 %shard_map.68 = (f32[16,32,768]{2,1,0:T(8,128)S(1)}, f32[16,32,768]{2,1,0:T(8,128)S(1)}) custom-call(s32[1]{0:T(128)} %bitcast.4.k_ref, bf16[2048,768]{1,0:T(8,128)(2,1)S(1)} %copy-done.2, bf16[256,2048]{1,0:T(8,128)(2,1)} %collective-permute-done.3.refs_0_, bf16[192,2048]{1,0:T(8,128)(2,1)S(1)} %copy-done.7, ...), custom_call_target="tpu_custom_call" | custom-call | flops 40000000000 | tf_op jit(solution)/shard_map/pallas_call | solution.py:198
  82.3 0.0 copy-start.4
  82.3 1.2 copy-done.4
  83.5 1.1 copy-done.11
  84.6 2.0 %all-to-all-done = f16[8,64,768]{2,1,0:T(8,128)(2,1)} async-done(((f16[8,64,768]{2,1,0:T(8,128)(2,1)}), f16[8,64,768]{2,1,0:T(8,128)(2,1)}, u32[]{:S(2)}, u32[]{:S(2)}) %all-to-all-start) | async-done | bytes 786464 | tf_op jit(solution)/shard_map/all_to_all | solution.py:222
  86.6 0.0 collective-permute-start.10
  86.6 3.6 %collective-permute-done.10 = f32[16,32,768]{2,1,0:T(8,128)S(1)} collective-permute-done((f32[16,32,768]{2,1,0:T(8,128)}, f32[16,32,768]{2,1,0:T(8,128)S(1)}, u32[]{:S(2)}, u32[]{:S(2)}) %collective-permute-start.10) | collective-permute-done | bytes 1572896 | tf_op jit(solution)/shard_map/ppermute | solution.py:211
  90.2 2.6 %multiply_convert_fusion = f16[16,32,768]{2,1,0:T(8,128)(2,1)} fusion(f32[16,32,768]{2,1,0:T(8,128)} %copy-done.4, f32[16,32,768]{2,1,0:T(8,128)S(1)} %collective-permute-done.10), kind=kLoop, calls=%fused_computation.1 | loop fusion | flops 1179648 | bytes 3932160 | tf_op jit(solution)/shard_map/convert_element_type | solution.py:211
  92.7 9.4 %all-to-all-start.1 = ((f16[16,32,768]{2,1,0:T(8,128)(2,1)}), f16[16,32,768]{2,1,0:T(8,128)(2,1)S(1)}, u32[]{:S(2)}, u32[]{:S(2)}) async-start(f16[16,32,768]{2,1,0:T(8,128)(2,1)} %multiply_convert_fusion), calls=%async_computation.1 | async-start | bytes 1572864 | tf_op jit(solution)/shard_map/all_to_all | solution.py:215
  102.2 1.3 convert_reduce_fusion.1
  103.4 3.7 %collective-permute-start.9 = (f32[32,768]{1,0:T(8,128)S(1)}, f32[32,768]{1,0:T(8,128)S(1)}, u32[]{:S(2)}, u32[]{:S(2)}) collective-permute-start(f32[32,768]{1,0:T(8,128)S(1)} %dynamic-slice_bitcast_fusion), channel_id=1, source_target_pairs={{0,16},{1,17},{2,18},{3,19},{4,20},{5,21},{6,22},{7,23},{8,24},{9,... | collective-permute-start | bytes 294920 | tf_op jit(solution)/shard_map/ppermute | solution.py:363
  107.1 0.0 copy-done.14
  107.1 0.1 copy.7
  107.2 0.1 tile.10.fock_ref
  107.4 0.0 copy-done.8
  107.4 1.0 shard_map.64.fock_ref
  108.4 2.6 %collective-permute-done.9 = f32[32,768]{1,0:T(8,128)S(1)} collective-permute-done((f32[32,768]{1,0:T(8,128)S(1)}, f32[32,768]{1,0:T(8,128)S(1)}, u32[]{:S(2)}, u32[]{:S(2)}) %collective-permute-start.9) | collective-permute-done | bytes 98336 | tf_op jit(solution)/shard_map/ppermute | solution.py:363
  111.0 14.4 %all-to-all-done.1 = f16[16,32,768]{2,1,0:T(8,128)(2,1)S(1)} async-done(((f16[16,32,768]{2,1,0:T(8,128)(2,1)}), f16[16,32,768]{2,1,0:T(8,128)(2,1)S(1)}, u32[]{:S(2)}, u32[]{:S(2)}) %all-to-all-start.1) | async-done | bytes 786464 | tf_op jit(solution)/shard_map/all_to_all | solution.py:215
  125.4 0.1 convert_reduce_fusion.second_ref
  125.5 1.4 shard_map.71
  127.0 21.9 %all_to_all.19 = f16[32,8,768]{2,1,0:T(8,128)(2,1)S(1)} all-to-all(f16[32,8,768]{2,1,0:T(8,128)(2,1)S(1)} %convert_bitcast_fusion), channel_id=1, replica_groups=mesh['row'=8,'col'=32] {'col'}, dimensions={0} | all-to-all | bytes 786432 | tf_op jit(solution)/shard_map/all_to_all | solution.py:311
  148.9 0.1 bitcast_convert_fusion.got_ref
  148.9 1.8 %shard_map.72 = f32[128,768]{1,0:T(8,128)} custom-call(s32[3]{0:T(128)S(1)} %pad_add_fusion._.at_ref, f32[128,768]{1,0:T(8,128)S(1)} %shard_map.64.fock_ref, f32[128,256]{1,0:T(8,128)S(1)} %shard_map.70.weights_ref, f32[256,768]{1,0:T(8,128)S(1)} %bitcast_convert_fusion.got_ref), custom_call_target="tpu_custom_call" | custom-call | bytes 1310720 | tf_op jit(solution)/shard_map/pallas_call | solution.py:241
  (14 shorter events, 0.1 us)
Async XLA Ops:
  0.0 9.6 %copy-start.9 = (s32[16]{0:T(128)S(1)}, s32[16]{0:T(128)}, u32[]{:S(2)}) copy-start(s32[16]{0:T(128)} %cd_ref.1) | copy-start | bytes 196
  0.0 9.6 %copy-start.10 = (s32[6]{0:T(128)S(1)}, s32[6]{0:T(128)}, u32[]{:S(2)}) copy-start(s32[6]{0:T(128)} %ab_ref.1) | copy-start | bytes 76
  0.0 1.6 %copy-start.3 = (bf16[512,2048]{1,0:T(8,128)(2,1)S(1)}, bf16[512,2048]{1,0:T(8,128)(2,1)}, u32[]{:S(2)}) copy-start(bf16[512,2048]{1,0:T(8,128)(2,1)} %amplitudes_ref.1) | copy-start | bytes 6291460
  4.8 8.4 %copy-start.5 = (bf16[192,2048]{1,0:T(8,128)(2,1)}, bf16[192,2048]{1,0:T(8,128)(2,1)S(1)}, u32[]{:S(2)}) copy-start(bf16[192,2048]{1,0:T(8,128)(2,1)S(1)} %get-tuple-element.36.mirrored_ref.refs_1_) | copy-start | bytes 2359300
  4.8 25.2 %collective-permute-start = (bf16[256,2048]{1,0:T(8,128)(2,1)}, bf16[256,2048]{1,0:T(8,128)(2,1)}, u32[]{:S(2)}, u32[]{:S(2)}) collective-permute-start(bf16[256,2048]{1,0:T(8,128)(2,1)} %get-tuple-element.30.own_ref), channel_id=1, source_target_pairs={{0,32},{32,0},{64,96},{96,64},{128,160},{160,128},{192,224},{224,1... | collective-permute-start | bytes 3145736 | tf_op jit(solution)/shard_map/ppermute | solution.py:328
  6.3 26.1 %collective-permute-start.2 = (bf16[256,2048]{1,0:T(8,128)(2,1)}, bf16[256,2048]{1,0:T(8,128)(2,1)}, u32[]{:S(2)}, u32[]{:S(2)}) collective-permute-start(bf16[256,2048]{1,0:T(8,128)(2,1)} %get-tuple-element.30.own_ref), channel_id=1, source_target_pairs={{0,192},{32,224},{64,0},{96,32},{128,64},{160,96},{192,128},{224,1... | collective-permute-start | bytes 3145736 | tf_op jit(solution)/shard_map/ppermute | solution.py:329
  7.2 25.3 %collective-permute-start.1 = (bf16[256,2048]{1,0:T(8,128)(2,1)}, bf16[256,2048]{1,0:T(8,128)(2,1)}, u32[]{:S(2)}, u32[]{:S(2)}) collective-permute-start(bf16[256,2048]{1,0:T(8,128)(2,1)} %get-tuple-element.31), channel_id=1, source_target_pairs={{0,64},{32,96},{64,128},{96,160},{128,192},{160,224},{192,0},{224,... | collective-permute-start | bytes 3145736 | tf_op jit(solution)/shard_map/ppermute | solution.py:330
  9.6 1.9 %copy-start = (bf16[2048,768]{1,0:T(8,128)(2,1)S(1)}, bf16[2048,768]{1,0:T(8,128)(2,1)}, u32[]{:S(2)}) copy-start(bf16[2048,768]{1,0:T(8,128)(2,1)} %integrals_ref) | copy-start | bytes 9437188
  13.1 24.9 %copy-start.1 = (bf16[2048,768]{1,0:T(8,128)(2,1)}, bf16[2048,768]{1,0:T(8,128)(2,1)S(1)}, u32[]{:S(2)}) copy-start(bf16[2048,768]{1,0:T(8,128)(2,1)S(1)} %shard_map.66.panel_ref) | copy-start | bytes 9437188
  13.1 32.8 %collective-permute-start.7 = (bf16[2048,768]{1,0:T(8,128)(2,1)S(1)}, bf16[2048,768]{1,0:T(8,128)(2,1)}, u32[]{:S(2)}, u32[]{:S(2)}) collective-permute-start(bf16[2048,768]{1,0:T(8,128)(2,1)S(1)} %shard_map.66.panel_ref), channel_id=1, source_target_pairs={{0,1},{1,0},{2,3},{3,2},{4,5},{5,4},{6,7},{7,6},{8,9},{9,8},{10,11... | collective-permute-start | bytes 9437192 | tf_op jit(solution)/shard_map/ppermute | solution.py:334
  32.5 1.1 copy-start.6
  38.0 1.1 copy-start.12
  39.1 0.9 copy-start.13
  40.0 4.6 %collective-permute-start.8 = (bf16[512,2048]{1,0:T(8,128)(2,1)}, bf16[512,2048]{1,0:T(8,128)(2,1)}, u32[]{:S(2)}, u32[]{:S(2)}) collective-permute-start(bf16[512,2048]{1,0:T(8,128)(2,1)} %get-tuple-element.50), channel_id=1, source_target_pairs={{0,1},{1,0},{2,3},{3,2},{4,5},{5,4},{6,7},{7,6},{8,9},{9,8},{10,11... | collective-permute-start | bytes 6291464 | tf_op jit(solution)/shard_map/ppermute | solution.py:346
  40.9 34.2 %collective-permute-start.5 = (bf16[320,2048]{1,0:T(8,128)(2,1)}, bf16[320,2048]{1,0:T(8,128)(2,1)}, u32[]{:S(2)}, u32[]{:S(2)}) collective-permute-start(bf16[320,2048]{1,0:T(8,128)(2,1)} %copy-done.12), channel_id=1, source_target_pairs={{0,32},{32,0},{64,96},{96,64},{128,160},{160,128},{192,224},{224,1... | collective-permute-start | bytes 3932168 | tf_op jit(solution)/shard_map/ppermute | solution.py:349
  41.4 33.6 %collective-permute-start.3 = (bf16[256,2048]{1,0:T(8,128)(2,1)}, bf16[256,2048]{1,0:T(8,128)(2,1)}, u32[]{:S(2)}, u32[]{:S(2)}) collective-permute-start(bf16[256,2048]{1,0:T(8,128)(2,1)} %collective-permute-done.partner_ref), channel_id=1, source_target_pairs={{0,192},{32,224},{64,0},{96,32},{128,64},{160,96},{192,128},{224,1... | collective-permute-start | bytes 3145736 | tf_op jit(solution)/shard_map/ppermute | solution.py:347
  41.4 33.6 %collective-permute-start.4 = (bf16[192,2048]{1,0:T(8,128)(2,1)}, bf16[192,2048]{1,0:T(8,128)(2,1)}, u32[]{:S(2)}, u32[]{:S(2)}) collective-permute-start(bf16[192,2048]{1,0:T(8,128)(2,1)} %copy-done.13), channel_id=1, source_target_pairs={{0,64},{32,96},{64,128},{96,160},{128,192},{160,224},{192,0},{224,... | collective-permute-start | bytes 2359304 | tf_op jit(solution)/shard_map/ppermute | solution.py:348
  44.6 30.4 %collective-permute-start.6 = (bf16[64,2048]{1,0:T(8,128)(2,1)S(1)}, bf16[64,2048]{1,0:T(8,128)(2,1)}, u32[]{:S(2)}, u32[]{:S(2)}) collective-permute-start(bf16[64,2048]{1,0:T(8,128)(2,1)S(1)} %get-tuple-element.46), channel_id=1, source_target_pairs={{0,128},{32,160},{64,192},{96,224},{128,0},{160,32},{192,64},{224,... | collective-permute-start | bytes 786440 | tf_op jit(solution)/shard_map/ppermute | solution.py:350
  53.7 21.4 %copy-start.2 = (bf16[2048,768]{1,0:T(8,128)(2,1)S(1)}, bf16[2048,768]{1,0:T(8,128)(2,1)}, u32[]{:S(2)}) copy-start(bf16[2048,768]{1,0:T(8,128)(2,1)} %copy-done.1) | copy-start | bytes 9437188
  54.7 31.8 %all-to-all-start = ((f16[8,64,768]{2,1,0:T(8,128)(2,1)}), f16[8,64,768]{2,1,0:T(8,128)(2,1)}, u32[]{:S(2)}, u32[]{:S(2)}) async-start(f16[8,64,768]{2,1,0:T(8,128)(2,1)} %multiply_convert_fusion.1), calls=%async_computation | async-start | bytes 1572864 | tf_op jit(solution)/shard_map/all_to_all | solution.py:222
  75.0 1.1 copy-start.7
  82.3 1.2 copy-start.4
  83.5 1.2 copy-start.11
  86.6 3.6 %collective-permute-start.10 = (f32[16,32,768]{2,1,0:T(8,128)}, f32[16,32,768]{2,1,0:T(8,128)S(1)}, u32[]{:S(2)}, u32[]{:S(2)}) collective-permute-start(f32[16,32,768]{2,1,0:T(8,128)} %copy-done.11), channel_id=1, source_target_pairs={{0,1},{1,0},{2,3},{3,2},{4,5},{5,4},{6,7},{7,6},{8,9},{9,8},{10,11... | collective-permute-start | bytes 4718600 | tf_op jit(solution)/shard_map/ppermute | solution.py:211
  92.7 14.4 %copy-start.14 = (f32[64,64]{1,0:T(8,128)S(1)}, f32[64,64]{1,0:T(8,128)}, u32[]{:S(2)}) copy-start(f32[64,64]{1,0:T(8,128)} %param.11) | copy-start | bytes 49156
  92.7 14.6 %copy-start.8 = (bf16[128,768]{1,0:T(8,128)(2,1)S(1)}, bf16[128,768]{1,0:T(8,128)(2,1)}, u32[]{:S(2)}) copy-start(bf16[128,768]{1,0:T(8,128)(2,1)} %slab_ref.1) | copy-start | bytes 589828
  92.7 32.7 %all-to-all-start.1 = ((f16[16,32,768]{2,1,0:T(8,128)(2,1)}), f16[16,32,768]{2,1,0:T(8,128)(2,1)S(1)}, u32[]{:S(2)}, u32[]{:S(2)}) async-start(f16[16,32,768]{2,1,0:T(8,128)(2,1)} %multiply_convert_fusion), calls=%async_computation.1 | async-start | bytes 1572864 | tf_op jit(solution)/shard_map/all_to_all | solution.py:215
  103.4 7.6 %collective-permute-start.9 = (f32[32,768]{1,0:T(8,128)S(1)}, f32[32,768]{1,0:T(8,128)S(1)}, u32[]{:S(2)}, u32[]{:S(2)}) collective-permute-start(f32[32,768]{1,0:T(8,128)S(1)} %dynamic-slice_bitcast_fusion), channel_id=1, source_target_pairs={{0,16},{1,17},{2,18},{3,19},{4,20},{5,21},{6,22},{7,23},{8,24},{9,... | collective-permute-start | bytes 294920 | tf_op jit(solution)/shard_map/ppermute | solution.py:363
